TPU v7x, 32 devices: a whole 2x2x4 slice. The times are simulated.
32 devices in a mesh: col: 4 (over y, x), row: 8 (over z, core).
Axes of the slice: x: 2, y: 2, z: 4, core: 2. Of those that a mesh axis runs over, the one named last changes fastest.
Arguments:
- true_ids: int32 [65536], P(('col', 'row')), may hold values from 4 to 28
- picked: int32 [65536], P(('col', 'row')), may hold values from 0 to 1, as said below
- replace_kinds: int32 [65536], P(('col', 'row')), may hold values from 0 to 9
- random_ids: int32 [65536], P(('col', 'row')), may hold values from 4 to 28
- splits: int32 [64], P(('col', 'row')), may hold values from 0 to 1, as said below
- embedding: float32 [33, 640], replicated, may hold values from -0.6 to 0.6
- projection: float32 [640, 1920], replicated, may hold values from -0.25 to 0.25
- outward: float32 [640, 640], replicated, may hold values from -1 to 1
- feedforward: float32 [2, 640, 2560], P(None, 'row', 'col'), may hold values from -0.25 to 0.25
- vectors: float32 [15, 640], replicated
- embedding_drift: float32 [33, 640], replicated, may hold values from -1.335144e-05 to 1.335144e-05
- embedding_spread: float32 [33, 640], replicated, may hold values from 8.0874744e-13 to 3.2349898e-12
- projection_drift: float32 [640, 1920], replicated, may hold values from -1.335144e-05 to 1.335144e-05
- projection_spread: float32 [640, 1920], replicated, may hold values from 8.0874744e-13 to 3.2349898e-12
- outward_drift: float32 [640, 640], replicated, may hold values from -1.335144e-05 to 1.335144e-05
- outward_spread: float32 [640, 640], replicated, may hold values from 8.0874744e-13 to 3.2349898e-12
- feedforward_drift: float32 [2, 640, 2560], P(None, 'row', 'col'), may hold values from -1.335144e-05 to 1.335144e-05
- feedforward_spread: float32 [2, 640, 2560], P(None, 'row', 'col'), may hold values from 8.0874744e-13 to 3.2349898e-12
- vectors_drift: float32 [15, 640], replicated, may hold values from -5.340576e-05 to 5.340576e-05
- vectors_spread: float32 [15, 640], replicated, may hold values from 1.2939959e-11 to 5.1759836e-11
Outputs:
- loss_pair: float32 [2], replicated
- grad_norm: float32 [], replicated
- embedding_next: float32 [33, 640], replicated
- embedding_moved: float32 [33, 640], replicated
- embedding_varied: float32 [33, 640], replicated
- embedding_copy: bfloat16 [33, 640], replicated
- projection_next: float32 [640, 1920], replicated
- projection_moved: float32 [640, 1920], replicated
- projection_varied: float32 [640, 1920], replicated
- projection_copy: bfloat16 [640, 1920], replicated
- outward_next: float32 [640, 640], replicated
- outward_moved: float32 [640, 640], replicated
- outward_varied: float32 [640, 640], replicated
- outward_copy: bfloat16 [640, 640], replicated
- feedforward_next: float32 [2, 640, 2560], P(None, 'row', 'col')
- feedforward_moved: float32 [2, 640, 2560], P(None, 'row', 'col')
- feedforward_varied: float32 [2, 640, 2560], P(None, 'row', 'col')
- feedforward_copy: bfloat16 [2, 640, 2560], P(None, 'row', 'col')
- vectors_next: float32 [15, 640], replicated
- vectors_moved: float32 [15, 640], replicated
- vectors_varied: float32 [15, 640], replicated
- vectors_copy: bfloat16 [15, 640], replicated
Inputs may be any that keep to these rules, and one draw needn't show every extreme that they name: Each half of every slot of 1024 positions holds at least one picked position. `replace_kinds`: 0 to 7 mask a picked position, 8 replaces it by random_ids, 9 keeps it; unpicked positions keep true_ids. `splits`: the last slot is always split.
All inputs are finite; a program needn't handle non-finite values.
Results may differ from a plain program's by a relative error of at most 0.0088.
Values may be sent and summed in bfloat16 or wider, within the bound.
No kernel may reach another device: no remote copies, remote signals or barrier semaphores. Data moves between devices by JAX's collectives and lax.ppermute only.
A program may use at most 512 MiB of HBM per device.

v0:
```python
import jax
import jax.numpy as jnp
from jax import lax
from jax.sharding import PartitionSpec as P

HEAD_DIM = 32
FF = 2560
STEP = 10


PRECISE = lax.Precision.HIGHEST
EPS_NORM = 1e-05
CLIP_NORM = 0.002
FIRST_DECAY = 0.5
SECOND_DECAY = 0.5
ADAM_EPS = 1e-08
WEIGHT_DECAY = 0.01
MASK_ID = 32


def layer_norm(values, gain_row, shift_row):
    center = values - jnp.mean(values, axis=-1, keepdims=True)
    spread = jnp.mean(center * center, axis=-1, keepdims=True)
    return center * lax.rsqrt(spread + EPS_NORM) * gain_row + shift_row


def rotary(values, cos_table, sin_table):
    half_dim = values.shape[-1] // 2
    turned = jnp.concatenate([-values[..., half_dim:], values[..., :half_dim]], axis=-1)
    return values * cos_table[:, None, :] + turned * sin_table[:, None, :]


def rotary_tables(positions):
    freq = 10000.0 ** (-jnp.arange(0, HEAD_DIM, 2, dtype=jnp.float32) / HEAD_DIM)
    angle = positions.astype(jnp.float32)[:, None] * freq[None, :]
    angle = jnp.concatenate([angle, angle], axis=1)
    return (jnp.cos(angle), jnp.sin(angle))


def inputs_of(true_ids, picked, replace_kinds, random_ids):
    masked = (picked == 1) & (replace_kinds < 8)
    swapped = (picked == 1) & (replace_kinds == 8)
    return jnp.where(masked, MASK_ID, jnp.where(swapped, random_ids, true_ids))


def adam_step(weight, grad, drift, spread, rate):
    drift = FIRST_DECAY * drift + (1.0 - FIRST_DECAY) * grad
    spread = SECOND_DECAY * spread + (1.0 - SECOND_DECAY) * grad * grad
    adjusted = (
        drift
        / (1.0 - FIRST_DECAY**STEP)
        / (jnp.sqrt(spread / (1.0 - SECOND_DECAY**STEP)) + ADAM_EPS)
    )
    return (weight - rate * (adjusted + WEIGHT_DECAY * weight), drift, spread)


def exact_gelu(values):
    return jax.nn.gelu(values, approximate=False)


def contract_rows(left, right):
    return lax.dot_general(
        left, right, (((0,), (0,)), ((), ())), preferred_element_type=jnp.float32
    )


def contract_cols(left, right):
    return lax.dot_general(
        left, right, (((1,), (1,)), ((), ())), preferred_element_type=jnp.float32
    )


def slot_scores(queries, key_rows, second):
    scores = jnp.einsum(
        "qhe,khe->hqk", queries, key_rows, preferred_element_type=jnp.float32
    ) * HEAD_DIM ** (-0.5)
    same = second[:, None] == second[None, :]
    return jnp.where(same[None], scores, -1e30)


def slot_forward(pieces):
    queries, key_rows, value_rows, second = pieces
    scores = slot_scores(queries, key_rows, second)
    top_score = jnp.max(scores, axis=-1, keepdims=True)
    log_total = jnp.log(jnp.sum(jnp.exp(scores - top_score), axis=-1, keepdims=True)) + top_score
    probability = jnp.exp(scores - log_total).astype(jnp.bfloat16)
    attended = jnp.einsum(
        "hqk,khe->qhe", probability, value_rows, preferred_element_type=jnp.float32
    )
    return (attended.astype(jnp.bfloat16), log_total)


def slot_backward(pieces):
    queries, key_rows, value_rows, attended_grad, log_total, second = pieces
    probability = jnp.exp(slot_scores(queries, key_rows, second) - log_total)
    prob_low = probability.astype(jnp.bfloat16)
    prob_grad = jnp.einsum(
        "qhe,khe->hqk", attended_grad, value_rows, preferred_element_type=jnp.float32
    )
    row_inner = jnp.sum(probability * prob_grad, axis=-1, keepdims=True)
    score_grad = (probability * (prob_grad - row_inner)).astype(jnp.bfloat16)
    score_scale = HEAD_DIM ** (-0.5)
    query_grad = (
        jnp.einsum("hqk,khe->qhe", score_grad, key_rows, preferred_element_type=jnp.float32)
        * score_scale
    )
    key_grad = (
        jnp.einsum("hqk,qhe->khe", score_grad, queries, preferred_element_type=jnp.float32)
        * score_scale
    )
    value_grad = jnp.einsum(
        "hqk,qhe->khe", prob_low, attended_grad, preferred_element_type=jnp.float32
    )
    return (query_grad, key_grad, value_grad)


def body(
    true_ids,
    picked,
    replace_kinds,
    random_ids,
    splits,
    embedding,
    projection,
    outward,
    feedforward,
    vectors,
    embedding_drift,
    embedding_spread,
    projection_drift,
    projection_spread,
    outward_drift,
    outward_spread,
    feedforward_drift,
    feedforward_spread,
    vectors_drift,
    vectors_spread,
):
    tokens = true_ids.shape[0]
    slot_count = splits.shape[0]
    slot_rows = tokens // slot_count
    model_width = embedding.shape[1]
    vocab_size = embedding.shape[0]
    head_count = model_width // HEAD_DIM
    bias_rows = FF // model_width
    bf16 = jnp.bfloat16
    f32 = jnp.float32
    input_ids = inputs_of(true_ids, picked, replace_kinds, random_ids)
    within = jnp.arange(slot_rows, dtype=jnp.int32)
    second = (within[None, :] >= slot_rows // 2).astype(jnp.int32) * splits[:, None]
    cos_table, sin_table = rotary_tables((within[None, :] - second * (slot_rows // 2)).reshape(-1))
    crop_local = jnp.sum(1 + splits).astype(f32)
    crops = lax.psum(crop_local, ("col", "row"))
    vocab_iota = jnp.arange(vocab_size, dtype=jnp.int32)[None, :]
    onehot_ids = (input_ids[:, None] == vocab_iota).astype(f32)
    onehot_targets = (true_ids[:, None] == vocab_iota).astype(f32)
    embedded = jnp.dot(onehot_ids, embedding, precision=PRECISE)
    normed_one, ln_one_back = jax.vjp(layer_norm, embedded, vectors[0], vectors[1])
    normed_low = normed_one.astype(bf16)
    qkv_weight = projection.astype(bf16)
    mixed = jnp.dot(normed_low, qkv_weight, preferred_element_type=f32) + vectors[2:5].reshape(-1)
    shaped = mixed.reshape(tokens, 3, head_count, HEAD_DIM)
    queries = rotary(shaped[:, 0], cos_table, sin_table).astype(bf16)
    key_rows = rotary(shaped[:, 1], cos_table, sin_table).astype(bf16)
    value_rows = shaped[:, 2].astype(bf16)

    def by_slot(array):
        return array.reshape(slot_count, slot_rows, head_count, HEAD_DIM)

    attended, log_totals = lax.map(
        slot_forward, (by_slot(queries), by_slot(key_rows), by_slot(value_rows), second)
    )
    attended = attended.reshape(tokens, model_width)
    out_weight = outward.astype(bf16)
    residual_one = embedded + jnp.dot(attended, out_weight, preferred_element_type=f32) + vectors[5]
    normed_two, ln_two_back = jax.vjp(layer_norm, residual_one, vectors[6], vectors[7])
    normed_two_low = normed_two.astype(bf16)
    ffn_tile = lax.all_gather(feedforward.astype(bf16), "row", axis=1, tiled=True)
    bias_hidden = vectors[8 : 8 + bias_rows].reshape(-1)
    col_index = lax.axis_index("col")
    col_width = ffn_tile.shape[2]
    bias_part = lax.dynamic_slice_in_dim(bias_hidden, col_index * col_width, col_width)
    ffn_in = lax.all_gather(normed_two_low, "col", axis=0, tiled=True)
    hidden = jnp.dot(ffn_in, ffn_tile[0], preferred_element_type=f32) + bias_part
    active, gelu_back = jax.vjp(exact_gelu, hidden)
    active_low = active.astype(bf16)
    part = active_low
    branch = lax.psum_scatter(
        contract_cols(part, ffn_tile[1]).astype(jnp.bfloat16),
        "col",
        scatter_dimension=0,
        tiled=True,
    ).astype(jnp.float32)
    residual_two = residual_one + branch + vectors[8 + bias_rows]
    final_out, ln_final_back = jax.vjp(
        layer_norm, residual_two, vectors[9 + bias_rows], vectors[10 + bias_rows]
    )
    final_low = final_out.astype(bf16)
    table_low = embedding.astype(bf16)
    logits = contract_cols(final_low, table_low)
    pick_float = picked.astype(f32).reshape(slot_count, slot_rows)
    second_float = second.astype(f32)
    first_count = jnp.sum(pick_float * (1.0 - second_float), axis=1, keepdims=True)
    second_count = jnp.sum(pick_float * second_float, axis=1, keepdims=True)
    crop_count = jnp.where(second == 1, second_count, first_count)
    token_weight = (pick_float / crop_count).reshape(-1)

    def token_loss(values):
        log_total = jax.nn.logsumexp(values, axis=-1)
        chosen = jnp.sum(values * onehot_targets, axis=-1)
        return jnp.sum(token_weight * (log_total - chosen))

    loss_local, loss_back = jax.vjp(token_loss, logits)
    logit_grad = loss_back(1.0 / crops)[0].astype(bf16)
    final_grad = jnp.dot(logit_grad, table_low, preferred_element_type=f32)
    table_grad = contract_rows(logit_grad, final_low)
    res_two_grad, gain_final, shift_final = ln_final_back(final_grad)
    branch_low = res_two_grad.astype(bf16)
    bias_out_grad = jnp.sum(branch_low, axis=0, dtype=f32)
    grad_in = lax.all_gather(branch_low, "col", axis=0, tiled=True)
    active_grad = jnp.dot(grad_in, ffn_tile[1], preferred_element_type=f32)
    hidden_grad = gelu_back(active_grad)[0].astype(bf16)
    pair_grad = jnp.stack([contract_rows(ffn_in, hidden_grad), contract_rows(grad_in, active_low)])
    bias_hidden_grad = jnp.sum(hidden_grad, axis=0, dtype=f32)
    part = hidden_grad
    normed_two_grad = lax.psum_scatter(
        contract_cols(part, ffn_tile[0]).astype(jnp.bfloat16),
        "col",
        scatter_dimension=0,
        tiled=True,
    ).astype(jnp.float32)
    bias_hidden_full = lax.dynamic_update_slice_in_dim(
        jnp.zeros_like(bias_hidden), bias_hidden_grad, col_index * col_width, 0
    )
    pair_grad = lax.psum_scatter(pair_grad, "row", scatter_dimension=1, tiled=True)
    back_two, gain_two, shift_two = ln_two_back(normed_two_grad)
    res_one_grad = res_two_grad + back_two
    attn_low = res_one_grad.astype(bf16)
    bias_attn_grad = jnp.sum(attn_low, axis=0, dtype=f32)
    out_grad = contract_rows(attended, attn_low)
    attended_grad = contract_cols(attn_low, out_weight).astype(bf16)
    query_grad, key_grad, value_grad = lax.map(
        slot_backward,
        (
            by_slot(queries),
            by_slot(key_rows),
            by_slot(value_rows),
            by_slot(attended_grad),
            log_totals,
            second,
        ),
    )
    query_grad = rotary(query_grad.reshape(tokens, head_count, HEAD_DIM), cos_table, -sin_table)
    key_grad = rotary(key_grad.reshape(tokens, head_count, HEAD_DIM), cos_table, -sin_table)
    value_grad = value_grad.reshape(tokens, head_count, HEAD_DIM)
    qkv_grad = (
        jnp.stack([query_grad, key_grad, value_grad], axis=1)
        .reshape(tokens, 3 * model_width)
        .astype(bf16)
    )
    in_grad = contract_rows(normed_low, qkv_grad)
    bias_qkv_grad = jnp.sum(qkv_grad, axis=0, dtype=f32).reshape(3, model_width)
    normed_one_grad = contract_cols(qkv_grad, qkv_weight)
    back_one, gain_one, shift_one = ln_one_back(normed_one_grad)
    embedded_grad = res_one_grad + back_one
    table_grad = table_grad + lax.dot_general(
        onehot_ids, embedded_grad, (((0,), (0,)), ((), ())), precision=PRECISE
    )
    vector_grad = jnp.concatenate(
        [
            gain_one[None],
            shift_one[None],
            bias_qkv_grad,
            bias_attn_grad[None],
            gain_two[None],
            shift_two[None],
            bias_hidden_full.reshape(bias_rows, model_width),
            bias_out_grad[None],
            gain_final[None],
            shift_final[None],
        ],
        axis=0,
    )
    ffn_square = jnp.sum(pair_grad * pair_grad)
    replicated = (embedding, projection, outward, vectors)
    drifts = (embedding_drift, projection_drift, outward_drift, vectors_drift)
    spreads = (embedding_spread, projection_spread, outward_spread, vectors_spread)
    step_rates = (0.05, 0.05, 0.1, 0.2)
    summed = lax.psum(
        (table_grad, in_grad, out_grad, vector_grad, ffn_square, loss_local), ("col", "row")
    )
    rep_grads = summed[:4]
    ffn_total = summed[4]
    loss_total = summed[5]
    squares = ffn_total
    for grad in rep_grads:
        squares = squares + jnp.sum(grad * grad)
    grad_norm = jnp.sqrt(squares)
    factor = jnp.minimum(1.0, CLIP_NORM / (grad_norm + 1e-06))
    rep_out = []
    for weight, grad, drift, spread, rate in zip(
        replicated, rep_grads, drifts, spreads, step_rates
    ):
        rep_out.append(adam_step(weight, grad * factor, drift, spread, rate))
    ffn_out = adam_step(
        feedforward, pair_grad * factor, feedforward_drift, feedforward_spread, 0.05
    )
    ordered = [rep_out[0], rep_out[1], rep_out[2], ffn_out, rep_out[3]]
    results = [jnp.stack([loss_total, crops]), grad_norm]
    for fresh_w, moved_w, varied_w in ordered:
        results.extend([fresh_w, moved_w, varied_w, fresh_w.astype(bf16)])
    return tuple(results)


def solution(mesh):
    return jax.shard_map(
        body,
        mesh=mesh,
        in_specs=(
            P(("col", "row")),
            P(("col", "row")),
            P(("col", "row")),
            P(("col", "row")),
            P(("col", "row")),
            P(),
            P(),
            P(),
            P(None, "row", "col"),
            P(),
            P(),
            P(),
            P(),
            P(),
            P(),
            P(),
            P(None, "row", "col"),
            P(None, "row", "col"),
            P(),
            P(),
        ),
        out_specs=(
            P(),
            P(),
            P(),
            P(),
            P(),
            P(),
            P(),
            P(),
            P(),
            P(),
            P(),
            P(),
            P(),
            P(),
            P(None, "row", "col"),
            P(None, "row", "col"),
            P(None, "row", "col"),
            P(None, "row", "col"),
            P(),
            P(),
            P(),
            P(),
        ),
        check_vma=False,
    )
```

profile of v0, /device:TPU:0, one launch (start us, length us, event | category | flops | bytes accessed | tf_op | source)
XLA Modules:
  0.0 1990.2 jit_solution(13657180137653621041)
XLA Ops:
  17.0 10.6 broadcast_add_fusion
  35.0 13.0 fusion.120
  76.6 9.0 slice_negate_fusion.2
  103.7 11.0 fusion.60
  119.3 178.7 %while.26 = (s32[]{:T(128)}, bf16[2,1024,20,32]{1,3,2,0:T(8,128)(2,1)}, f32[2,20,1024,1]{2,1,3,0:T(8,128)S(1)}, bf16[2,1024,20,32]{1,3,2,0:T(8,128)(2,1)}, s32[2...) while((s32[]{:T(128)}, ...), condition=%wide.region_7.8_spmd, body=%wide.region_4.7_spmd.sunk | while | flops 2916724736 | bytes 261830768 | solution.py:170
  120.0 31.0 %fusion.162 = (f32[20,1024]{1,0:T(8,128)S(1)}, f32[20,1024,1024]{1,2,0:T(8,128)}) fusion(pred[1024,1024]{0,1:T(8,128)(4,1)S(1)} %broadcast_compare_fusion.4, bf16[2,1024,20,32]{1,3,2,0:T(8,128)(2,1)} %get-tuple-element.425, s32[]{:T(128)S(6)} %copy.149, bf16[2,1024,20,32]{1,3,2,0:T(8,128)(2,1)} %get-tuple-element.424), kind=kOutput, calls=%fused_computation.3.clone.1 | convolution fusion | flops 1405071360 | bytes 87639040 | tf_op jit(solution)/shard_map/while/body/eval_jaxpr/qhe,khe->hqk/dot_general | solution.py:74
  151.0 26.4 %exponential_reduce_fusion.2 = f32[20,1024]{1,0:T(8,128)S(1)} fusion(f32[20,1024,1024]{1,2,0:T(8,128)} %get-tuple-element.387, f32[20,1024]{1,0:T(8,128)S(1)} %get-tuple-element.388, pred[1024,1024]{0,1:T(8,128)(4,1)S(1)} %broadcast_compare_fusion.4), kind=kLoop, calls=%fused_computation.1.clone.1 | loop fusion | flops 83865600 | bytes 85098496 | tf_op jit(solution)/shard_map/while/body/eval_jaxpr/reduce_sum | solution.py:85
  177.5 31.1 %fusion.163 = bf16[2,1024,20,32]{1,3,2,0:T(8,128)(2,1)} fusion(bf16[2,1024,20,32]{1,3,2,0:T(8,128)(2,1)} %get-tuple-element.412, s32[]{:T(128)S(6)} %copy.149, f32[20,1024,1024]{1,2,0:T(8,128)} %get-tuple-element.387, f32[20,1024]{1,0:T(8,128)S(1)} %get-tuple-element.389, pred[1024,1024]{0,1:T(8,128)(4,1)S(1)} %broadcast_compare_fusion.4, ...), kind=kOutput, calls=%fused_computation.9.clone.1 | convolution fusion | flops 1426718720 | bytes 87639040 | tf_op jit(solution)/shard_map/while/body/eval_jaxpr/hqk,khe->qhe/dot_general | solution.py:87
  209.3 31.0 %fusion.162 = (f32[20,1024]{1,0:T(8,128)S(1)}, f32[20,1024,1024]{1,2,0:T(8,128)}) fusion(pred[1024,1024]{0,1:T(8,128)(4,1)S(1)} %broadcast_compare_fusion.4, bf16[2,1024,20,32]{1,3,2,0:T(8,128)(2,1)} %get-tuple-element.425, s32[]{:T(128)S(6)} %copy.149, bf16[2,1024,20,32]{1,3,2,0:T(8,128)(2,1)} %get-tuple-element.424), kind=kOutput, calls=%fused_computation.3.clone.1 | convolution fusion | flops 1405071360 | bytes 87639040 | tf_op jit(solution)/shard_map/while/body/eval_jaxpr/qhe,khe->hqk/dot_general | solution.py:74
  240.3 26.4 %exponential_reduce_fusion.2 = f32[20,1024]{1,0:T(8,128)S(1)} fusion(f32[20,1024,1024]{1,2,0:T(8,128)} %get-tuple-element.387, f32[20,1024]{1,0:T(8,128)S(1)} %get-tuple-element.388, pred[1024,1024]{0,1:T(8,128)(4,1)S(1)} %broadcast_compare_fusion.4), kind=kLoop, calls=%fused_computation.1.clone.1 | loop fusion | flops 83865600 | bytes 85098496 | tf_op jit(solution)/shard_map/while/body/eval_jaxpr/reduce_sum | solution.py:85
  266.7 31.1 %fusion.163 = bf16[2,1024,20,32]{1,3,2,0:T(8,128)(2,1)} fusion(bf16[2,1024,20,32]{1,3,2,0:T(8,128)(2,1)} %get-tuple-element.412, s32[]{:T(128)S(6)} %copy.149, f32[20,1024,1024]{1,2,0:T(8,128)} %get-tuple-element.387, f32[20,1024]{1,0:T(8,128)S(1)} %get-tuple-element.389, pred[1024,1024]{0,1:T(8,128)(4,1)S(1)} %broadcast_compare_fusion.4, ...), kind=kOutput, calls=%fused_computation.9.clone.1 | convolution fusion | flops 1426718720 | bytes 87639040 | tf_op jit(solution)/shard_map/while/body/eval_jaxpr/hqk,khe->qhe/dot_general | solution.py:87
  311.1 107.8 %all-gather.4.cloned.1.call-done = bf16[8192,640]{0,1:T(8,128)(2,1)} async-done(((bf16[2048,640]{0,1:T(8,128)(2,1)}), bf16[8192,640]{0,1:T(8,128)(2,1)}) %all-gather.4.cloned.1.call-update) | async-done | bytes 10485776 | tf_op jit(solution)/shard_map/all_gather | solution.py:183
  418.8 58.2 %multiply_convert_fusion.1 = (bf16[8192,640]{1,0:T(8,128)(2,1)S(1)}, f32[8192,640]{1,0:T(8,128)}, f32[8192,640]{1,0:T(8,128)}) fusion(f32[640]{0:T(1024)S(1)} %dynamic_slice.36, bf16[8192,640]{0,1:T(8,128)(2,1)} %all-gather.4.cloned.1.call-done, bf16[2,640,640]{2,1,0:T(8,128)(2,1)} %all-gather.6.cloned.1.call-done), kind=kOutput, calls=%fused_computation.63 | convolution fusion | flops 7056916480 | bytes 63736320 | tf_op jit(solution)/shard_map/dot_general | solution.py:184
  480.9 13.9 convolution_convert_fusion.1
  496.7 40.2 %psum.50 = f32[]{:T(128)} all-reduce(f32[]{:T(128)S(6)} %convert_element_type.161), channel_id=1, replica_groups=mesh['col'=4,'row'=8] {'col','row'}, use_global_device_ids=true, to_apply=%region_19.20 | all-reduce | flops 1 | bytes 8 | tf_op jit(solution)/shard_map/psum | solution.py:153
  537.9 61.8 %reduce-scatter.4.cloned.1.call-done = bf16[2048,640]{0,1:T(8,128)(2,1)} async-done(((bf16[8192,640]{0,1:T(8,128)(2,1)}), bf16[2048,640]{0,1:T(8,128)(2,1)}) %reduce-scatter.4.cloned.1.call-update) | async-done | bytes 2621456 | tf_op jit(solution)/shard_map/reduce_scatter | solution.py:188
  630.6 105.2 %all-gather.8.cloned.1.call-done = bf16[8192,640]{0,1:T(8,128)(2,1)} async-done(((bf16[2048,640]{0,1:T(8,128)(2,1)}), bf16[8192,640]{0,1:T(8,128)(2,1)}) %all-gather.8.cloned.1.call-update) | async-done | bytes 10485776 | tf_op jit(solution)/shard_map/all_gather | solution.py:220
  735.8 31.5 %convert_reduce_fusion = (f32[640]{0:T(1024)}, bf16[8192,640]{1,0:T(8,128)(2,1)}) fusion(f32[8192,640]{1,0:T(8,128)} %get-tuple-element.239, bf16[8192,640]{0,1:T(8,128)(2,1)} %all-gather.8.cloned.1.call-done, bf16[2,640,640]{2,1,0:T(8,128)(2,1)S(1)} %copy-done.95, f32[8192,640]{1,0:T(8,128)} %get-tuple-element.276, f32[640]{0:T(1024)S(1)} %dynamic_slice.36), kind=kOutput, calls=%fused_computation.61 | convolution fusion | flops 6800014848 | bytes 63740416 | tf_op jit(solution)/shard_map/dot_general | solution.py:221
  767.2 17.3 convolution_convert_fusion
  787.2 12.5 convolution_bitcast_fusion
  799.7 12.9 convolution_bitcast_fusion.1
  814.6 73.6 %reduce-scatter.8.cloned.1.call-done = bf16[2048,640]{0,1:T(8,128)(2,1)} async-done(((bf16[8192,640]{0,1:T(8,128)(2,1)}), bf16[2048,640]{0,1:T(8,128)(2,1)}) %reduce-scatter.8.cloned.1.call-update) | async-done | bytes 2621456 | tf_op jit(solution)/shard_map/reduce_scatter | solution.py:226
  920.9 759.1 %while.27 = (s32[]{:T(128)}, f32[2,1024,20,32]{1,0,3,2:T(2,128)}, f32[2,1024,20,32]{1,0,3,2:T(2,128)}, bf16[2,1024,20,32]{1,0,3,2:T(2,128)(2,1)}, bf16[2,1024,20...) while((s32[]{:T(128)}, f32[2,1024,20,32]{1,0,3,2:T(2,128)}, ...), condition=%wide.region_30.31_spmd, body=%wide.region_28.30_spmd.sunk | while | flops 7027798016 | bytes 686356608 | solution.py:242
  923.3 30.6 %fusion.172 = f32[20,1024,1024]{1,2,0:T(8,128)} fusion(bf16[2,1024,20,32]{1,3,2,0:T(8,128)(2,1)} %get-tuple-element.457, s32[]{:T(128)S(6)} %copy.159, bf16[2,1024,20,32]{1,3,2,0:T(8,128)(2,1)} %get-tuple-element.455), kind=kOutput, calls=%fused_computation.39.clone.1 | convolution fusion | flops 1342177280 | bytes 86508544 | tf_op jit(solution)/shard_map/while/body/eval_jaxpr/qhe,khe->hqk/dot_general | solution.py:74
  954.0 30.6 %fusion.173 = bf16[1,1024,20,32]{1,3,2,0:T(8,128)(2,1)S(1)} fusion(f32[20,1024,1024]{1,2,0:T(8,128)} %fusion.172, f32[20,1024]{1,0:T(8,128)S(1)} %dynamic-slice_bitcast_fusion.2, pred[1024,1024]{0,1:T(8,128)(4,1)S(1)} %broadcast_compare_fusion.5, bf16[2,1024,20,32]{1,3,2,0:T(8,128)(2,1)} %get-tuple-element.459, s32[]{:T(128)S(6)} %copy.159), kind=kOutput, calls=%fused_computation.33.clone.1 | convolution fusion | flops 1426063360 | bytes 87638016 | tf_op jit(solution)/shard_map/while/body/eval_jaxpr/hqk,qhe->khe/dot_general | solution.py:111
  988.6 43.0 %dynamic_update_slice.33 = bf16[2,1024,20,32]{1,0,3,2:T(2,128)(2,1)} dynamic-update-slice(bf16[2,1024,20,32]{1,0,3,2:T(2,128)(2,1)} %get-tuple-element.442, bf16[1,1024,20,32]{1,0,3,2:T(2,128)(2,1)} %copy.140, s32[]{:T(128)S(6)} %copy.159, s32[]{:T(128)} %constant.86.clone.1..sunk, s32[]{:T(128)} %constant.86.clone.1..sunk, s32[]{:T(128)} %constant.86.clone.1..sunk) | dynamic-update-slice | bytes 2621444 | tf_op jit(solution)/shard_map/while/body/jit(dynamic_update_index_in_dim)/dynamic_update_slice | solution.py:242
  1031.7 60.4 %multiply_reduce_fusion.17 = (f32[20,1024]{1,0:T(8,128)S(1)}, f32[20,1024,1024]{1,2,0:T(8,128)}) fusion(f32[20,1024,1024]{1,2,0:T(8,128)} %fusion.172, f32[20,1024]{1,0:T(8,128)S(1)} %dynamic-slice_bitcast_fusion.2, pred[1024,1024]{0,1:T(8,128)(4,1)S(1)} %broadcast_compare_fusion.5, bf16[2,1024,20,32]{1,3,2,0:T(8,128)(2,1)} %get-tuple-element.460, ...), kind=kOutput, calls=%fused_computation.25.clone.3 | convolution fusion | flops 1447014400 | bytes 171607040 | tf_op jit(solution)/shard_map/while/body/eval_jaxpr/qhe,khe->hqk/dot_general | solution.py:97
  1092.1 66.6 %multiply_convert_fusion.3 = bf16[20,1024,1024]{1,2,0:T(8,128)(2,1)} fusion(f32[20,1024,1024]{1,2,0:T(8,128)} %get-tuple-element.401, f32[20,1024,1024]{1,2,0:T(8,128)} %fusion.172, f32[20,1024]{1,0:T(8,128)S(1)} %get-tuple-element.402, f32[20,1024]{1,0:T(8,128)S(1)} %dynamic-slice_bitcast_fusion.2, pred[1024,1024]{0,1:T(8,128)(4,1)S(1)} %broadcast_compare_fusion.5), kind=kLoop, calls=%fused_computation.24.clone.1 | loop fusion | flops 125829120 | bytes 210927616 | tf_op jit(solution)/shard_map/while/body/eval_jaxpr/convert_element_type | solution.py:101
  1158.7 18.3 multiply_bitcast_fusion.5
  1177.0 18.3 multiply_bitcast_fusion.4
  1205.5 45.7 %dynamic_update_slice.32 = f32[2,1024,20,32]{1,0,3,2:T(2,128)} dynamic-update-slice(f32[2,1024,20,32]{1,0,3,2:T(2,128)} %get-tuple-element.441, f32[1,1024,20,32]{1,0,3,2:T(1,128)} %copy.139, s32[]{:T(128)S(6)} %copy.159, s32[]{:T(128)} %constant.86.clone.1..sunk, s32[]{:T(128)} %constant.86.clone.1..sunk, s32[]{:T(128)} %constant.86.clone.1..sunk) | dynamic-update-slice | bytes 5242884 | tf_op jit(solution)/shard_map/while/body/jit(dynamic_update_index_in_dim)/dynamic_update_slice | solution.py:242
  1251.2 45.3 %dynamic_update_slice.31 = f32[2,1024,20,32]{1,0,3,2:T(2,128)} dynamic-update-slice(f32[2,1024,20,32]{1,0,3,2:T(2,128)} %get-tuple-element.440, f32[1,1024,20,32]{1,0,3,2:T(1,128)S(1)} %copy-done, s32[]{:T(128)S(6)} %copy.159, s32[]{:T(128)} %constant.86.clone.1..sunk, s32[]{:T(128)} %constant.86.clone.1..sunk, s32[]{:T(128)} %constant.86.clone.1..sunk) | dynamic-update-slice | bytes 5242884 | tf_op jit(solution)/shard_map/while/body/jit(dynamic_update_index_in_dim)/dynamic_update_slice | solution.py:242
  1298.7 30.5 %fusion.172 = f32[20,1024,1024]{1,2,0:T(8,128)} fusion(bf16[2,1024,20,32]{1,3,2,0:T(8,128)(2,1)} %get-tuple-element.457, s32[]{:T(128)S(6)} %copy.159, bf16[2,1024,20,32]{1,3,2,0:T(8,128)(2,1)} %get-tuple-element.455), kind=kOutput, calls=%fused_computation.39.clone.1 | convolution fusion | flops 1342177280 | bytes 86508544 | tf_op jit(solution)/shard_map/while/body/eval_jaxpr/qhe,khe->hqk/dot_general | solution.py:74
  1329.2 30.6 %fusion.173 = bf16[1,1024,20,32]{1,3,2,0:T(8,128)(2,1)S(1)} fusion(f32[20,1024,1024]{1,2,0:T(8,128)} %fusion.172, f32[20,1024]{1,0:T(8,128)S(1)} %dynamic-slice_bitcast_fusion.2, pred[1024,1024]{0,1:T(8,128)(4,1)S(1)} %broadcast_compare_fusion.5, bf16[2,1024,20,32]{1,3,2,0:T(8,128)(2,1)} %get-tuple-element.459, s32[]{:T(128)S(6)} %copy.159), kind=kOutput, calls=%fused_computation.33.clone.1 | convolution fusion | flops 1426063360 | bytes 87638016 | tf_op jit(solution)/shard_map/while/body/eval_jaxpr/hqk,qhe->khe/dot_general | solution.py:111
  1363.8 43.0 %dynamic_update_slice.33 = bf16[2,1024,20,32]{1,0,3,2:T(2,128)(2,1)} dynamic-update-slice(bf16[2,1024,20,32]{1,0,3,2:T(2,128)(2,1)} %get-tuple-element.442, bf16[1,1024,20,32]{1,0,3,2:T(2,128)(2,1)} %copy.140, s32[]{:T(128)S(6)} %copy.159, s32[]{:T(128)} %constant.86.clone.1..sunk, s32[]{:T(128)} %constant.86.clone.1..sunk, s32[]{:T(128)} %constant.86.clone.1..sunk) | dynamic-update-slice | bytes 2621444 | tf_op jit(solution)/shard_map/while/body/jit(dynamic_update_index_in_dim)/dynamic_update_slice | solution.py:242
  1406.9 60.4 %multiply_reduce_fusion.17 = (f32[20,1024]{1,0:T(8,128)S(1)}, f32[20,1024,1024]{1,2,0:T(8,128)}) fusion(f32[20,1024,1024]{1,2,0:T(8,128)} %fusion.172, f32[20,1024]{1,0:T(8,128)S(1)} %dynamic-slice_bitcast_fusion.2, pred[1024,1024]{0,1:T(8,128)(4,1)S(1)} %broadcast_compare_fusion.5, bf16[2,1024,20,32]{1,3,2,0:T(8,128)(2,1)} %get-tuple-element.460, ...), kind=kOutput, calls=%fused_computation.25.clone.3 | convolution fusion | flops 1447014400 | bytes 171607040 | tf_op jit(solution)/shard_map/while/body/eval_jaxpr/qhe,khe->hqk/dot_general | solution.py:97
  1467.3 66.6 %multiply_convert_fusion.3 = bf16[20,1024,1024]{1,2,0:T(8,128)(2,1)} fusion(f32[20,1024,1024]{1,2,0:T(8,128)} %get-tuple-element.401, f32[20,1024,1024]{1,2,0:T(8,128)} %fusion.172, f32[20,1024]{1,0:T(8,128)S(1)} %get-tuple-element.402, f32[20,1024]{1,0:T(8,128)S(1)} %dynamic-slice_bitcast_fusion.2, pred[1024,1024]{0,1:T(8,128)(4,1)S(1)} %broadcast_compare_fusion.5), kind=kLoop, calls=%fused_computation.24.clone.1 | loop fusion | flops 125829120 | bytes 210927616 | tf_op jit(solution)/shard_map/while/body/eval_jaxpr/convert_element_type | solution.py:101
  1533.9 18.3 multiply_bitcast_fusion.5
  1552.2 18.3 multiply_bitcast_fusion.4
  1580.7 45.7 %dynamic_update_slice.32 = f32[2,1024,20,32]{1,0,3,2:T(2,128)} dynamic-update-slice(f32[2,1024,20,32]{1,0,3,2:T(2,128)} %get-tuple-element.441, f32[1,1024,20,32]{1,0,3,2:T(1,128)} %copy.139, s32[]{:T(128)S(6)} %copy.159, s32[]{:T(128)} %constant.86.clone.1..sunk, s32[]{:T(128)} %constant.86.clone.1..sunk, s32[]{:T(128)} %constant.86.clone.1..sunk) | dynamic-update-slice | bytes 5242884 | tf_op jit(solution)/shard_map/while/body/jit(dynamic_update_index_in_dim)/dynamic_update_slice | solution.py:242
  1626.4 45.3 %dynamic_update_slice.31 = f32[2,1024,20,32]{1,0,3,2:T(2,128)} dynamic-update-slice(f32[2,1024,20,32]{1,0,3,2:T(2,128)} %get-tuple-element.440, f32[1,1024,20,32]{1,0,3,2:T(1,128)S(1)} %copy-done, s32[]{:T(128)S(6)} %copy.159, s32[]{:T(128)} %constant.86.clone.1..sunk, s32[]{:T(128)} %constant.86.clone.1..sunk, s32[]{:T(128)} %constant.86.clone.1..sunk) | dynamic-update-slice | bytes 5242884 | tf_op jit(solution)/shard_map/while/body/jit(dynamic_update_index_in_dim)/dynamic_update_slice | solution.py:242
  1688.1 8.2 reshape.510
  1696.3 8.2 reshape.513
  1704.5 8.3 reshape.512
  1732.8 13.7 fusion.125
  1790.8 41.7 %all-reduce = (f32[1]{0:T(128)}, f32[]{:T(128)}, f32[15,640]{1,0:T(8,128)S(1)}) all-reduce(f32[1]{0:T(128)} %bitcast.24, f32[]{:T(128)} %multiply_reduce_fusion.10, f32[15,640]{1,0:T(8,128)S(1)} %concatenate.78), channel_id=1, replica_groups=mesh['col'=4,'row'=8] {'col','row'}, use_global_device_ids=true, to_apply=%region_17.18 | all-reduce | flops 9602 | bytes 76816 | tf_op jit(solution)/shard_map/psum | solution.py:289
  1835.0 114.7 %all-reduce.4.cloned.1.call-done = (f32[33,640]{1,0:T(8,128)}, f32[640,1920]{1,0:T(8,128)}, f32[640,640]{1,0:T(8,128)}) async-done(((f32[33,640]{1,0:T(8,128)}, f32[640,1920]{1,0:T(8,128)}, f32[640,640]{1,0:T(8,128)}), (f32[33,640]{1,0:T(8,128)}, f32[640,1920]{1,0:T(8,128)}, f32[640,640]{1,0:T(8,128)})) %all-reduce.4.cloned.1.call-update) | async-done | bytes 6638096 | tf_op jit(solution)/shard_map/psum | solution.py:289
  1969.4 11.0 fusion.112
  (387 shorter events, 280.9 us)
Async XLA Ops:
  7.2 303.9 %all-gather.6.cloned.1.call-start = ((), (), s32[]{:S(2)}) async-start(), calls=%async_computation.4 | async-start | bytes 1843200 | tf_op jit(solution)/shard_map/all_gather | solution.py:178
  9.0 409.9 %all-gather.4.cloned.1.call-start = ((), (), s32[]{:S(2)}) async-start(), calls=%async_computation.3 | async-start | bytes 13107200 | tf_op jit(solution)/shard_map/all_gather | solution.py:183
  9.0 39.6 %copy-start.93 = (f32[16]{0:T(128)}, f32[16]{0:T(128)S(1)}, u32[]{:S(2)}) copy-start(f32[16]{0:T(128)S(1)} %multiply_power_fusion) | copy-start | bytes 196
  9.1 38.9 %copy-start.65 = (s32[1024]{0:T(1024)}, s32[1024]{0:T(1024)S(1)}, u32[]{:S(2)}) copy-start(s32[1024]{0:T(1024)S(1)} %fusion.101) | copy-start | bytes 12292
  16.2 11.5 copy-start.3
  16.2 11.5 copy-start.47
  17.0 10.7 copy-start.58
  17.0 10.7 copy-start.76
  35.0 13.0 copy-start.87
  35.0 17.7 copy-start.13
  310.9 288.7 %reduce-scatter.4.cloned.1.call-start = ((), (), s32[]{:S(2)}) async-start(), calls=%async_computation.5 | async-start | bytes 13107200 | tf_op jit(solution)/shard_map/reduce_scatter | solution.py:188
  418.8 62.1 %copy-start.95 = (bf16[2,640,640]{2,1,0:T(8,128)(2,1)S(1)}, bf16[2,640,640]{2,1,0:T(8,128)(2,1)}, u32[]{:S(2)}) copy-start(bf16[2,640,640]{2,1,0:T(8,128)(2,1)} %all-gather.6.cloned.1.call-done) | copy-start | bytes 4915204
  494.8 42.1 %copy-start.75 = (f32[2048]{0:T(1024)S(1)}, f32[2048]{0:T(1024)}, u32[]{:S(2)}) copy-start(f32[2048]{0:T(1024)} %get-tuple-element.267) | copy-start | bytes 24580
  494.8 42.8 %copy-start.66 = (s32[1024]{0:T(1024)S(1)}, s32[1024]{0:T(1024)}, u32[]{:S(2)}) copy-start(s32[1024]{0:T(1024)} %copy-done.65) | copy-start | bytes 12292
  494.8 104.9 %copy-start.84 = (f32[640]{0:T(1024)S(1)}, f32[640]{0:T(1024)}, u32[]{:S(2)}) copy-start(f32[640]{0:T(1024)} %get-tuple-element.157) | copy-start | bytes 7684
  494.8 241.0 %all-gather.8.cloned.1.call-start = ((), (), s32[]{:S(2)}) async-start(), calls=%async_computation.6 | async-start | bytes 13107200 | tf_op jit(solution)/shard_map/all_gather | solution.py:220
  611.3 12.4 slice-start.4
  625.7 273.7 %copy-start.62 = (f32[2048]{0:T(1024)}, f32[2048]{0:T(1024)S(1)}, u32[]{:S(2)}) copy-start(f32[2048]{0:T(1024)S(1)} %negate_multiply_fusion.3) | copy-start | bytes 24580
  630.5 257.7 %reduce-scatter.8.cloned.1.call-start = ((), (), s32[]{:S(2)}) async-start(), calls=%async_computation.8 | async-start | bytes 13107200 | tf_op jit(solution)/shard_map/reduce_scatter | solution.py:226
  784.6 1004.3 %reduce-scatter.6.cloned.1.call-start = ((), (), s32[]{:S(2)}) async-start(), calls=%async_computation.7 | async-start | bytes 3686400 | tf_op jit(solution)/shard_map/reduce_scatter | solution.py:235
  812.6 75.7 %copy-start.35 = (f32[2048]{0:T(1024)S(1)}, f32[2048]{0:T(1024)}, u32[]{:S(2)}) copy-start(f32[2048]{0:T(1024)} %copy-done.34) | copy-start | bytes 24580
  812.6 75.7 %copy-start.50 = (f32[640]{0:T(1024)S(1)}, f32[640]{0:T(1024)}, u32[]{:S(2)}) copy-start(f32[640]{0:T(1024)} %get-tuple-element.159) | copy-start | bytes 7684
  814.5 79.2 %copy-start.61 = (f32[2048]{0:T(1024)S(1)}, f32[2048]{0:T(1024)}, u32[]{:S(2)}) copy-start(f32[2048]{0:T(1024)} %copy-done.60) | copy-start | bytes 24580
  814.5 79.2 %copy-start.41 = (f32[2048]{0:T(1024)S(1)}, f32[2048]{0:T(1024)}, u32[]{:S(2)}) copy-start(f32[2048]{0:T(1024)} %copy-done.40) | copy-start | bytes 24580
  814.6 1135.2 %all-reduce.4.cloned.1.call-start = ((), (), s32[]{:S(2)}) async-start(), calls=%async_computation.9 | async-start | bytes 13312000 | tf_op jit(solution)/shard_map/psum | solution.py:289
  888.3 11.2 slice-start
  893.8 11.1 copy-start.56
  1205.5 45.7 %copy-start = (f32[1,1024,20,32]{1,0,3,2:T(1,128)S(1)}, f32[1,1024,20,32]{1,0,3,2:T(1,128)}, u32[]{:S(2)}) copy-start(f32[1,1024,20,32]{1,0,3,2:T(1,128)} %copy.138) | copy-start | bytes 7864324 | tf_op jit(solution)/shard_map/while
  1580.7 45.7 %copy-start = (f32[1,1024,20,32]{1,0,3,2:T(1,128)S(1)}, f32[1,1024,20,32]{1,0,3,2:T(1,128)}, u32[]{:S(2)}) copy-start(f32[1,1024,20,32]{1,0,3,2:T(1,128)} %copy.138) | copy-start | bytes 7864324 | tf_op jit(solution)/shard_map/while
  1704.5 8.3 copy-start.19
  1732.7 13.7 copy-start.14
  1746.4 11.1 copy-start.59
  1746.4 11.1 copy-start.77
  1746.5 17.3 copy-start.11
  1752.5 11.3 slice-start.2
  1752.6 11.3 slice-start.6
  1752.6 11.3 slice-start.8
  1757.6 8.3 copy-start.6
  1757.6 8.3 copy-start.36
  1757.6 8.3 copy-start.42
  1787.6 172.9 %copy-start.38 = (f32[15,640]{1,0:T(8,128)S(1)}, f32[15,640]{1,0:T(8,128)}, u32[]{:S(2)}) copy-start(f32[15,640]{1,0:T(8,128)} %param.33) | copy-start | bytes 115204
  1787.6 174.4 %copy-start.27 = (f32[33,640]{1,0:T(8,128)S(1)}, f32[33,640]{1,0:T(8,128)}, u32[]{:S(2)}) copy-start(f32[33,640]{1,0:T(8,128)} %param.29) | copy-start | bytes 253444
  1787.7 176.3 %copy-start.23 = (f32[640,640]{1,0:T(8,128)S(1)}, f32[640,640]{1,0:T(8,128)}, u32[]{:S(2)}) copy-start(f32[640,640]{1,0:T(8,128)} %param.31) | copy-start | bytes 4915204
  1949.7 14.2 copy-start.17
  1969.4 11.1 copy-start.24
  1969.4 11.1 copy-start.25
  1969.4 11.1 copy-start.31
  1969.4 11.1 copy-start.32
  (76 other events, 337.5 us)
Sparse Core Ops, SparseCore 0:
  10.2 28.2 all-gather.5
  311.0 107.7 all-gather.3
  494.9 104.6 reduce-scatter.3
  630.7 105.0 all-gather.7
  784.7 103.5 reduce-scatter.7
  891.0 41.3 reduce-scatter.5
  1787.7 161.9 all-reduce.3
where the time goes:
time: 2020 us; the launch traced here: 1990 us
  matrix products  647 us (32%)
  waiting for transfers between devices  463 us (23%)
  local copies, waits for them, and re-layouts  450 us (22%)
  other arithmetic  318 us (16%)
  blocking collectives  81.9 us (4%)
  between operations  21.9 us (1%)
    dynamic_update_slice x12, local copies, waits for them, and re-layouts, body(): lax.map(slot_backward, (by_slot(queries), by_slot(key_rows), by_slot(valu...  297 us
    convert_element_type x2, other arithmetic, slot_backward(): score_grad = (probability * (prob_grad - row_inner)).astype(jnp.bfloat16)  133 us
    dot_general x4, matrix products, slot_scores(): jnp.einsum('qhe,khe->hqk', queries, key_rows, preferred_element_type=jnp....  123 us
    dot_general x2, matrix products, slot_backward(): jnp.einsum('qhe,khe->hqk', attended_grad, value_rows, preferred_element_t...  121 us
    psum x1, waiting for transfers between devices, body(): lax.psum((table_grad, in_grad, out_grad, vector_grad, ffn_square, loss_lo...  115 us
    all_gather x1, waiting for transfers between devices, body(): ffn_in = lax.all_gather(normed_two_low, 'col', axis=0, tiled=True)  108 us
    all_gather x1, waiting for transfers between devices, body(): grad_in = lax.all_gather(branch_low, 'col', axis=0, tiled=True)  105 us
    reduce_scatter x1, waiting for transfers between devices, body(): lax.psum_scatter(contract_cols(part, ffn_tile[0]).astype(jnp.bfloat16), '...  73.6 us
  transfers between devices with their start and end apart: 7, of which 5 were waited for; matrix products, arithmetic and copies ran while one was open for 61% of the time, Pallas kernels for 0%

commit v1 on v0

v1 whole, which is shorter than its diff:
```python
import functools
import math

import jax
import jax.numpy as jnp
import numpy as np
from jax import lax
from jax.experimental import pallas as pl
from jax.experimental.pallas import tpu as pltpu
from jax.sharding import PartitionSpec as P

HEAD_DIM = 32
HALF = HEAD_DIM // 2
EXT = HEAD_DIM + 16
FF = 2560
STEP = 10
VPAD = 48
THIRD = 40
REST_TABLE = 32

EPS_NORM = 1e-05
CLIP_NORM = 0.002
FIRST_DECAY = 0.5
SECOND_DECAY = 0.5
ADAM_EPS = 1e-08
WEIGHT_DECAY = 0.01
MASK_ID = 32
MASKED = 1e30

LOG2E = math.log2(math.e)
SCALE = HEAD_DIM ** (-0.5)
MIB = 2**20

bf16 = jnp.bfloat16
f32 = jnp.float32

NN = ((1,), (0,))
NT = ((1,), (1,))
TN = ((0,), (0,))


def dot(left, right, dims=NN):
    return lax.dot_general(left, right, (dims, ((), ())), preferred_element_type=f32)


def split3(values):
    high = values.astype(bf16).astype(f32)
    rest = values - high
    middle = rest.astype(bf16).astype(f32)
    return high, middle, rest - middle


def norm_stats(values):
    center = values - jnp.mean(values, axis=0, keepdims=True)
    inverse = lax.rsqrt(jnp.mean(center * center, axis=0, keepdims=True) + EPS_NORM)
    return center * inverse, inverse


def norm_back(grad, hat, inverse, gain):
    scaled = grad * gain
    return inverse * (
        scaled
        - jnp.mean(scaled, axis=0, keepdims=True)
        - hat * jnp.mean(scaled * hat, axis=0, keepdims=True)
    )


def rows_of(count, width):
    return lax.broadcasted_iota(jnp.int32, (count, width), 0)


def lane_sum(values):
    return jnp.sum(values, axis=1, keepdims=True)


def columns_of(vectors, wide):
    wide[...] = jnp.zeros_like(wide)
    wide[0 : vectors.shape[0], :] = vectors[...]
    return wide[...].T


def qkv_kernel(
    meta, embedding, projection, vectors, cos_a, cos_b, sin_a, sin_b,
    x0, low, q_ext, k_ext, v_ext,
    table, weight, vec, wide,
):
    width = meta.shape[1]
    heads = q_ext.shape[0]
    model = x0.shape[0]
    vocab = embedding.shape[0]

    @pl.when(pl.program_id(0) == 0)
    def _():
        vec[...] = columns_of(vectors, wide)
        wide[...] = jnp.zeros_like(wide)
        for part, piece in enumerate(split3(embedding[...])):
            wide[part * THIRD : part * THIRD + vocab, :] = piece
        table[...] = wide[...].T.astype(bf16)
        for part in range(3):
            span = slice(part * model, (part + 1) * model)
            weight[span, :] = projection[:, span].astype(bf16).T

    ids = meta[0:1, :].astype(jnp.int32)
    vocab3 = rows_of(128, width)
    onehot = ((vocab3 == ids) | (vocab3 == ids + THIRD) | (vocab3 == ids + 2 * THIRD)).astype(f32).astype(bf16)
    embedded = dot(table[...], onehot)
    x0[...] = embedded
    hat, _ = norm_stats(embedded)
    normed = (hat * vec[:, 0:1] + vec[:, 1:2]).astype(bf16)
    row = rows_of(EXT - HEAD_DIM, width)
    low[0:model, :] = normed
    low[model : model + 16, :] = jnp.where(row == 0, 1.0, 0.0).astype(bf16)
    second = meta[2:3, :]
    in_second = second > 0.5
    cos = jnp.where(in_second, cos_a[...], cos_b[...])
    sin = jnp.where(in_second, sin_a[...], sin_b[...])
    q_rows = jnp.where(row == 0, second, jnp.where(row == 1, 1.0 - second, 0.0)).astype(bf16)
    k_rows = jnp.where(
        row == 0,
        -MASKED * (1.0 - second),
        jnp.where(row == 1, -MASKED * second, jnp.where(row < 5, 1.0, 0.0)),
    ).astype(bf16)
    v_rows = jnp.where(row < 3, 1.0, 0.0).astype(bf16)
    for part, out, extra in ((0, q_ext, q_rows), (1, k_ext, k_rows), (2, v_ext, v_rows)):
        base = part * model
        mixed = dot(weight[base : base + model, :], normed) + vec[:, 2 + part : 3 + part]
        for head in range(heads):
            one = mixed[head * HEAD_DIM : head * HEAD_DIM + HALF, :]
            two = mixed[head * HEAD_DIM + HALF : (head + 1) * HEAD_DIM, :]
            if part < 2:
                one, two = one * cos - two * sin, two * cos + one * sin
            out[head, 0:HALF, :] = one.astype(bf16)
            out[head, HALF:HEAD_DIM, :] = two.astype(bf16)
            out[head, HEAD_DIM:EXT, :] = extra


def attention_kernel(q_ext, k_ext, v_ext, out, q_next):
    heads, _, width = q_ext.shape
    factor = LOG2E * SCALE
    for head in range(heads):
        queries = q_ext[head]
        scores = dot(k_ext[head], queries, TN)
        top = jnp.max(scores, axis=0, keepdims=True)
        weights = jnp.exp2((scores - top) * factor).astype(bf16)
        mixed = dot(v_ext[head], weights)
        total = mixed[HEAD_DIM : HEAD_DIM + 1, :]
        out[head] = (mixed[0:HEAD_DIM, :] / total).astype(bf16)
        high, middle, rest = split3(-(top + jnp.log2(total) * (1.0 / factor)))
        q_next[head, 0:HEAD_DIM, :] = queries[0:HEAD_DIM, :]
        row = rows_of(EXT - HEAD_DIM, width)
        tail = queries[HEAD_DIM:EXT, :].astype(f32)
        tail = jnp.where(row == 2, high, jnp.where(row == 3, middle, jnp.where(row == 4, rest, tail)))
        q_next[head, HEAD_DIM:EXT, :] = tail.astype(bf16)


def attention_back_kernel(
    q_ext, k_ext, v_ext, do_ext, low, meta, cos_a, cos_b, sin_a, sin_b, *rest, chunk, chained
):
    dq, dk, dv, dweight, grads, total = rest[3:] if chained else rest
    slot = pl.program_id(0)
    heads, _, width = q_ext.shape
    in_second = meta[2:3, :] > 0.5
    cos = jnp.where(in_second, cos_a[...], cos_b[...])
    sin = jnp.where(in_second, sin_a[...], sin_b[...])
    for head in range(heads):
        keys = k_ext[head]
        q_parts = []
        k_total = v_total = None
        for at in range(0, width, chunk):
            piece = slice(at, at + chunk)
            queries, outs = q_ext[head, :, piece], do_ext[head, :, piece]
            prob = jnp.exp2(dot(queries, keys, TN) * (LOG2E * SCALE))
            inner = dot(outs, v_ext[head], TN)
            score_grad = (prob * inner).astype(bf16)
            q_parts.append(dot(keys[0:HEAD_DIM, :], score_grad, NT))
            k_part = dot(queries[0:HEAD_DIM, :], score_grad)
            v_part = dot(outs[0:HEAD_DIM, :], prob.astype(bf16))
            k_total = k_part if k_total is None else k_total + k_part
            v_total = v_part if v_total is None else v_total + v_part
        for part, (out, grad) in enumerate(((dq, jnp.concatenate(q_parts, axis=1)), (dk, k_total), (dv, v_total))):
            one, two = grad[0:HALF, :], grad[HALF:HEAD_DIM, :]
            if part < 2:
                one, two = one * SCALE, two * SCALE
                one, two = one * cos + two * sin, two * cos - one * sin
            out[head, 0:HALF, :] = one.astype(bf16)
            out[head, HALF:HEAD_DIM, :] = two.astype(bf16)
            base = (part * heads + head) * HEAD_DIM
            grads[base : base + HEAD_DIM, :] = out[head]
    share = dot(low[...], grads[...], NT)
    rows = share.shape[0]

    @pl.when(slot == 0)
    def _():
        total[...] = share

    @pl.when(slot > 0)
    def _():
        total[...] += share

    @pl.when(slot == pl.num_programs(0) - 1)
    def _():
        dweight[...] = jnp.zeros_like(dweight)
        dweight[0:rows, :] = total[...].astype(bf16)


def middle_kernel(
    meta, x0, attended, outward, w_up, w_down, embedding, vectors,
    dx1, do_ext, dw_pair, dw_rest, loss,
    up_t, down_t, act, slope, dw_up, dw_down, dw_out, dtable, dvec, vec, wide, table, table_t, w_out, w_out_t, sems,
):
    step = pl.program_id(0)
    chunks = w_up.shape[0]
    model, width = x0.shape
    heads = do_ext.shape[0]
    vocab = embedding.shape[0]

    @pl.when(step == 0)
    def _():
        for part in range(chunks):
            up_t[part] = w_up[part].T
            down_t[part] = w_down[part].T
        vec[...] = columns_of(vectors, wide)
        wide[...] = jnp.zeros_like(wide)
        wide[0:vocab, :] = embedding[...]
        table[...] = wide[0:VPAD, :].astype(bf16)
        table_t[...] = wide[...].T.astype(bf16)
        w_out[...] = outward[...].astype(bf16)
        w_out_t[...] = w_out[...].T
        dw_up[...] = jnp.zeros_like(dw_up)
        dw_down[...] = jnp.zeros_like(dw_down)
        dw_out[...] = jnp.zeros_like(dw_out)
        dtable[...] = jnp.zeros_like(dtable)
        dvec[...] = jnp.zeros_like(dvec)
        loss[...] = jnp.zeros_like(loss)

    def col(index):
        return vec[:, index : index + 1]

    after = 8 + chunks_of_bias(model)
    x1 = x0[...] + dot(w_out_t[...], attended[...]) + col(5)
    hat_two, inverse_two = norm_stats(x1)
    c_low = (hat_two * col(6) + col(7)).astype(bf16)
    branch = None
    for part in range(chunks):
        hidden = dot(up_t[part], c_low) + col(8 + part)
        cdf = 0.5 + 0.5 * lax.erf(hidden * (0.5**0.5))
        density = jnp.exp(hidden * hidden * -0.5) * (1.0 / math.sqrt(2.0 * math.pi))
        act[part] = (hidden * cdf).astype(bf16)
        slope[part] = (cdf + hidden * density).astype(bf16)
        share = dot(w_down[part], act[part])
        branch = share if branch is None else branch + share
    x2 = x1 + branch + col(after)
    hat_end, inverse_end = norm_stats(x2)
    f_low = (hat_end * col(after + 1) + col(after + 2)).astype(bf16)
    vocab_rows = rows_of(VPAD, width)
    logits = jnp.where(vocab_rows < vocab, dot(table[...], f_low), -MASKED)
    top = jnp.max(logits, axis=0, keepdims=True)
    raised = jnp.exp(logits - top)
    total = jnp.sum(raised, axis=0, keepdims=True)
    target = (vocab_rows == meta[1:2, :].astype(jnp.int32)).astype(f32)
    chosen = jnp.sum(logits * target, axis=0, keepdims=True)
    weight = meta[3:4, :]
    loss[0:1, :] += jnp.broadcast_to(lane_sum(weight * (jnp.log(total) + top - chosen)), (1, loss.shape[1]))
    logit_grad = (weight * (raised / total - target)).astype(bf16)
    dtable[...] += dot(logit_grad, f_low, NT)
    f_grad = dot(table_t[:, 0:VPAD], logit_grad)
    dvec[:, 4 + chunks : 5 + chunks] += lane_sum(f_grad * hat_end)
    dvec[:, 5 + chunks : 6 + chunks] += lane_sum(f_grad)
    x2_grad = norm_back(f_grad, hat_end, inverse_end, col(after + 1))
    g_low = x2_grad.astype(bf16)
    dvec[:, 3 + chunks : 4 + chunks] += lane_sum(g_low.astype(f32))
    c_grad = None
    for part in range(chunks):
        hidden_grad = (dot(down_t[part], g_low) * slope[part]).astype(bf16)
        dw_up[part] += dot(c_low, hidden_grad, NT)
        dw_down[part] += dot(g_low, act[part], NT)
        dvec[:, 3 + part : 4 + part] += lane_sum(hidden_grad.astype(f32))
        share = dot(w_up[part], hidden_grad)
        c_grad = share if c_grad is None else c_grad + share
    dvec[:, 1:2] += lane_sum(c_grad * hat_two)
    dvec[:, 2:3] += lane_sum(c_grad)
    x1_grad = x2_grad + norm_back(c_grad, hat_two, inverse_two, col(6))
    dx1[...] = x1_grad
    x1_low = x1_grad.astype(bf16)
    dvec[:, 0:1] += lane_sum(x1_low.astype(f32))
    dw_out[...] += dot(attended[...], x1_low, NT)
    o_grad = dot(w_out[...], x1_low).astype(bf16)
    inner = o_grad.astype(f32) * attended[...].astype(f32)
    row = rows_of(EXT - HEAD_DIM, width)
    for head in range(heads):
        span = slice(head * HEAD_DIM, (head + 1) * HEAD_DIM)
        high, middle, rest = split3(-jnp.sum(inner[span, :], axis=0, keepdims=True))
        do_ext[head, 0:HEAD_DIM, :] = o_grad[span, :]
        tail = jnp.where(row == 0, high, jnp.where(row == 1, middle, jnp.where(row == 2, rest, 0.0)))
        do_ext[head, HEAD_DIM:EXT, :] = tail.astype(bf16)

    @pl.when(step == pl.num_programs(0) - 1)
    def _():
        copies = []
        for side, (low, grad) in enumerate(((up_t, dw_up), (down_t, dw_down))):
            low[...] = grad[...].astype(bf16)
            copies.append(pltpu.make_async_copy(low, dw_pair.at[side], sems.at[side]))
            copies[side].start()
        dw_rest[...] = jnp.zeros_like(dw_rest)
        dw_rest[0:model, :] = dw_out[...].astype(bf16)
        wide[...] = dvec[...].T
        wide[REST_TABLE : REST_TABLE + VPAD, :] = dtable[...]
        dw_rest[model : model + 128, :] = wide[...].astype(bf16)
        for copy in copies:
            copy.wait()


def chunks_of_bias(model):
    return FF // model


def input_back_kernel(meta, x0, dq, dk, dv, dx1, projection, vectors, rest, weight, vec, wide, dvec, dtable):
    step = pl.program_id(0)
    model, width = x0.shape

    @pl.when(step == 0)
    def _():
        vec[...] = columns_of(vectors, wide)
        weight[...] = projection[...].astype(bf16)
        dtable[...] = jnp.zeros_like(dtable)
        dvec[...] = jnp.zeros_like(dvec)

    back = None
    for part, grad in enumerate((dq, dk, dv)):
        share = dot(weight[:, part * model : (part + 1) * model], grad[...])
        back = share if back is None else back + share
    hat, inverse = norm_stats(x0[...])
    dvec[:, VPAD : VPAD + 1] += lane_sum(back * hat)
    dvec[:, VPAD + 1 : VPAD + 2] += lane_sum(back)
    x0_grad = dx1[...] + norm_back(back, hat, inverse, vec[:, 0:1])
    onehot = (rows_of(VPAD, width) == meta[0:1, :].astype(jnp.int32)).astype(f32).astype(bf16)
    for piece in split3(x0_grad):
        dtable[...] += dot(onehot, piece.astype(bf16), NT)

    @pl.when(step == pl.num_programs(0) - 1)
    def _():
        wide[...] = dvec[...].T
        rest[0:VPAD, :] = dtable[...]
        rest[VPAD:, :] = wide[VPAD : VPAD + 8, :]


def whole(shape):
    return pl.BlockSpec(shape, lambda *_: (0,) * len(shape), pipeline_mode=pl.Buffered(1))


def shaped(shape, dtype):
    return jax.ShapeDtypeStruct(shape, dtype)


def limits(mib):
    return pltpu.CompilerParams(vmem_limit_bytes=mib * MIB)


def cost(flops, moved, transcendentals=0):
    return pl.CostEstimate(flops=int(flops), bytes_accessed=int(moved), transcendentals=int(transcendentals))


def adam_step(weight, grad, drift, spread, rate):
    drift = FIRST_DECAY * drift + (1.0 - FIRST_DECAY) * grad
    spread = SECOND_DECAY * spread + (1.0 - SECOND_DECAY) * grad * grad
    adjusted = (
        drift
        / (1.0 - FIRST_DECAY**STEP)
        / (jnp.sqrt(spread / (1.0 - SECOND_DECAY**STEP)) + ADAM_EPS)
    )
    return (weight - rate * (adjusted + WEIGHT_DECAY * weight), drift, spread)


def rotary_constants(rows):
    freq = np.float32(10000.0) ** (-np.arange(0, HEAD_DIM, 2, dtype=np.float32) / np.float32(HEAD_DIM))
    angle = np.arange(rows, dtype=np.float32)[None, :] * freq[:, None].astype(np.float32)
    return np.cos(angle).astype(np.float32), np.sin(angle).astype(np.float32)


def body(
    columns,
    deep,
    true_ids,
    picked,
    replace_kinds,
    random_ids,
    splits,
    embedding,
    projection,
    outward,
    feedforward,
    vectors,
    embedding_drift,
    embedding_spread,
    projection_drift,
    projection_spread,
    outward_drift,
    outward_spread,
    feedforward_drift,
    feedforward_spread,
    vectors_drift,
    vectors_spread,
):
    tokens = true_ids.shape[0]
    slots = splits.shape[0]
    rows = tokens // slots
    half = rows // 2
    vocab, model = embedding.shape
    heads = model // HEAD_DIM
    bias_rows = chunks_of_bias(model)
    block = half
    blocks = tokens // block
    wide = FF // columns
    devices = columns * deep * 2
    chips = ("col", "deep")
    everywhere = ("col", "deep", "core")

    pair_all = lax.all_gather(feedforward.astype(bf16), everywhere, axis=1, tiled=True)
    pair_all = pair_all.reshape(2, columns, model, wide)

    masked = (picked == 1) & (replace_kinds < 8)
    swapped = (picked == 1) & (replace_kinds == 8)
    input_ids = jnp.where(masked, MASK_ID, jnp.where(swapped, random_ids, true_ids))
    within = jnp.arange(rows, dtype=jnp.int32)
    second = ((within[None, :] >= half).astype(jnp.int32) * splits[:, None]).astype(f32)
    pick = picked.astype(f32).reshape(slots, rows)
    half_counts = jnp.sum(pick.reshape(slots, 2, half), axis=2)
    split = splits[:, None].astype(f32)
    half_counts = jnp.where(split > 0.5, half_counts, jnp.sum(half_counts, axis=1, keepdims=True))
    token_weight = (pick.reshape(slots, 2, half) / half_counts[:, :, None]).reshape(tokens)
    zero = jnp.zeros((tokens,), f32)
    meta = jnp.stack(
        [input_ids.astype(f32), true_ids.astype(f32), second.reshape(-1), token_weight, zero, zero, zero, zero]
    )
    cos_np, sin_np = rotary_constants(rows)
    cos_table, sin_table = jnp.asarray(cos_np), jnp.asarray(sin_np)
    twice_cos, twice_sin = (jnp.asarray(np.tile(t[:, :half], (1, 2))) for t in (cos_np, sin_np))

    def by_block(count):
        return pl.BlockSpec((count, block), lambda i: (0, i))

    def heads_block(count):
        return pl.BlockSpec((heads, count, block), lambda i: (0, 0, i))

    first_half = pl.BlockSpec((HALF, block), lambda i: (0, 0))
    own_half = pl.BlockSpec((HALF, block), lambda i: (0, i % 2))
    x0, normed, q_ext, k_ext, v_ext = pl.pallas_call(
        qkv_kernel,
        grid=(blocks,),
        in_specs=[by_block(8), whole((vocab, model)), whole((model, 3 * model)), whole(vectors.shape),
                  first_half, own_half, first_half, own_half],
        out_specs=[by_block(model), by_block(model + 16), heads_block(EXT), heads_block(EXT), heads_block(EXT)],
        out_shape=[shaped((model, tokens), f32), shaped((model + 16, tokens), bf16)]
        + [shaped((heads, EXT, tokens), bf16)] * 3,
        scratch_shapes=[pltpu.VMEM((model, 128), bf16), pltpu.VMEM((3 * model, model), bf16), pltpu.VMEM((model, 128), f32),
                        pltpu.VMEM((128, model), f32)],
        compiler_params=limits(56),
        cost_estimate=cost(2 * 3 * model * model * tokens, 20 * model * tokens),
        name="embed_and_qkv",
    )(meta, embedding, projection, vectors, cos_table, cos_table, sin_table, sin_table)

    per = 4

    def head_group(count, size, first=0):
        return pl.BlockSpec((size, count, rows), lambda s, g: (first + g, 0, s))

    attended, q_next = pl.pallas_call(
        attention_kernel,
        grid=(slots, heads // per),
        in_specs=[head_group(EXT, per)] * 3,
        out_specs=[head_group(HEAD_DIM, per), head_group(EXT, per)],
        out_shape=[shaped((heads, HEAD_DIM, tokens), bf16), shaped((heads, EXT, tokens), bf16)],
        compiler_params=limits(56),
        cost_estimate=cost(2 * 16 * model * rows * tokens, 12 * model * tokens, heads * rows * tokens),
        name="attention",
    )(q_ext, k_ext, v_ext)
    attended = attended.reshape(model, tokens)

    shard = -(-(model + 128) // devices)
    shard = -(-shard // 8) * 8
    padded = shard * devices
    dx1, do_ext, dw_pair, dw_rest, loss = pl.pallas_call(
        middle_kernel,
        grid=(blocks,),
        in_specs=[by_block(8), by_block(model), by_block(model), whole((model, model)),
                  pl.BlockSpec((None, columns, model, wide), lambda i: (0, 0, 0, 0), pipeline_mode=pl.Buffered(1)),
                  pl.BlockSpec((None, columns, model, wide), lambda i: (1, 0, 0, 0), pipeline_mode=pl.Buffered(1)),
                  whole((vocab, model)), whole(vectors.shape)],
        out_specs=[by_block(model), heads_block(EXT), pl.BlockSpec(memory_space=pl.ANY), whole((model + 128, model)), whole((8, 128))],
        out_shape=[shaped((model, tokens), f32), shaped((heads, EXT, tokens), bf16), shaped((2, columns, model, wide), bf16),
                   shaped((model + 128, model), bf16), shaped((8, 128), f32)],
        scratch_shapes=[pltpu.VMEM((columns, wide, model), bf16), pltpu.VMEM((columns, wide, model), bf16),
                        pltpu.VMEM((columns, wide, block), bf16), pltpu.VMEM((columns, wide, block), bf16),
                        pltpu.VMEM((columns, model, wide), f32), pltpu.VMEM((columns, model, wide), f32),
                        pltpu.VMEM((model, model), f32), pltpu.VMEM((VPAD, model), f32), pltpu.VMEM((model, 128), f32),
                        pltpu.VMEM((model, 128), f32), pltpu.VMEM((128, model), f32),
                        pltpu.VMEM((VPAD, model), bf16), pltpu.VMEM((model, 128), bf16),
                        pltpu.VMEM((model, model), bf16), pltpu.VMEM((model, model), bf16), pltpu.SemaphoreType.DMA((2,))],
        compiler_params=limits(62),
        cost_estimate=cost(2 * tokens * model * (6 * FF + 3 * model), 14 * model * tokens + 16 * model * FF, FF * tokens),
        name="feedforward_and_head",
    )(meta, x0, attended, outward, pair_all, pair_all, embedding, vectors)

    def swap(values, axes):
        return lax.all_to_all(values, axes, 0, 0, tiled=True)

    def add_up(values, pieces):
        return jnp.sum(values.reshape((pieces, -1) + values.shape[1:]).astype(f32), axis=0)

    def pad_rows(values):
        return jnp.pad(values, ((0, padded - values.shape[0]), (0, 0))) if padded > values.shape[0] else values

    def reduce_core(values):
        return add_up(swap(values, "core"), 2).astype(bf16)

    def spread(values, axes, count):
        return swap(jnp.broadcast_to(values[None], (count,) + values.shape).reshape((-1,) + values.shape[1:]), axes)

    pair = dw_pair.reshape(2 * columns * model, wide)
    pair = reduce_core(pair)
    pair = add_up(swap(pair, "col"), columns).astype(bf16)
    pair = add_up(swap(pair, "deep"), deep)
    pair_grad = swap(pair, "core").reshape(feedforward.shape)

    def to_owner(values):
        return add_up(swap(values, chips), columns * deep).astype(bf16)

    def to_chips(values):
        return spread(values, chips, columns * deep)

    rest_mine = reduce_core(pad_rows(dw_rest))
    rest_mine = to_chips(to_owner(rest_mine))

    per_call = 4
    width = 3 * per_call * HEAD_DIM
    grads = None
    in_parts = []
    for first in range(0, heads // per_call):
        chained = grads is not None

        def group(count, first=first):
            return pl.BlockSpec((per_call, count, rows), lambda s: (first, 0, s))

        table_spec = pl.BlockSpec((HALF, rows), lambda s: (0, 0))
        outs = pl.pallas_call(
            functools.partial(attention_back_kernel, chunk=half, chained=chained),
            grid=(slots,),
            in_specs=[group(EXT)] * 4
            + [pl.BlockSpec((model + 16, rows), lambda s: (0, s)), pl.BlockSpec((8, rows), lambda s: (0, s))]
            + [table_spec] * 4
            + [pl.BlockSpec(memory_space=pl.ANY)] * (3 if chained else 0),
            out_specs=[group(HEAD_DIM)] * 3 + [pl.BlockSpec((model + 128, width), lambda s: (0, 0))],
            out_shape=[shaped((heads, HEAD_DIM, tokens), bf16)] * 3 + [shaped((model + 128, width), bf16)],
            scratch_shapes=[pltpu.VMEM((width, rows), bf16), pltpu.VMEM((model + 16, width), f32)],
            input_output_aliases={10: 0, 11: 1, 12: 2} if chained else {},
            compiler_params=limits(56),
            cost_estimate=cost(2 * 40 * width // 3 * rows * tokens, 20 * width * tokens, per_call * rows * tokens),
            name="attention_back",
        )(q_next, k_ext, v_ext, do_ext, normed, meta, twice_cos, cos_table, twice_sin, sin_table, *(grads or ()))
        grads = outs[:3]
        in_parts.append(pad_rows(outs[3]))
    dq, dk, dv = (grad.reshape(model, tokens) for grad in grads)
    early = len(in_parts) - 2
    in_mine = []
    for parts in (in_parts[:early], in_parts[early:]):
        merged = jnp.concatenate([reduce_core(part) for part in parts], axis=1)
        in_mine.append(to_chips(to_owner(merged)))
    in_mine = jnp.concatenate(in_mine, axis=1)

    rest_start = pl.pallas_call(
        input_back_kernel,
        grid=(blocks,),
        in_specs=[by_block(8)] + [by_block(model)] * 5 + [whole((model, 3 * model)), whole(vectors.shape)],
        out_specs=whole((VPAD + 8, model)),
        out_shape=shaped((VPAD + 8, model), f32),
        scratch_shapes=[pltpu.VMEM((model, 3 * model), bf16), pltpu.VMEM((model, 128), f32), pltpu.VMEM((128, model), f32),
                        pltpu.VMEM((model, 128), f32), pltpu.VMEM((VPAD, model), f32)],
        compiler_params=limits(56),
        cost_estimate=cost(2 * 3 * model * model * tokens, 20 * model * tokens),
        name="input_back",
    )(meta, x0, dq, dk, dv, dx1, projection, vectors)

    scalars = jnp.stack([loss[0, 0], jnp.sum(1 + splits).astype(f32), jnp.sum(pair_grad * pair_grad)])
    late = jnp.concatenate([rest_start, jnp.pad(scalars[None], ((0, 7), (0, model - 3)))], axis=0)
    size = 1
    while size < devices:
        late = late + lax.ppermute(late, everywhere, [(i, i ^ size) for i in range(devices)])
        size *= 2
    loss_total, crops, ffn_total = late[VPAD + 8, 0], late[VPAD + 8, 1], late[VPAD + 8, 2]

    full = spread(jnp.concatenate([in_mine, rest_mine], axis=1), "core", 2).astype(f32)
    groups = heads // per_call
    piece = per_call * HEAD_DIM
    in_full = jnp.concatenate(
        [full[: model + 8, g * width + part * piece : g * width + (part + 1) * piece] for part in range(3) for g in range(groups)],
        axis=1,
    )
    rest_full = full[: model + 128, groups * width :]
    in_grad = in_full[:model]
    out_grad = rest_full[:model]
    table_grad = rest_full[model + REST_TABLE : model + REST_TABLE + vocab] + late[:vocab]
    vector_grad = jnp.concatenate(
        [late[VPAD : VPAD + 2], in_full[model].reshape(3, model), rest_full[model : model + 6 + bias_rows]], axis=0
    )
    rep_grads = (table_grad, in_grad, out_grad, vector_grad)
    squares = ffn_total
    for grad in rep_grads:
        squares = squares + jnp.sum(grad * grad)
    share = 1.0 / crops
    grad_norm = jnp.sqrt(squares) * share
    factor = jnp.minimum(1.0, CLIP_NORM / (grad_norm + 1e-06)) * share
    replicated = (embedding, projection, outward, vectors)
    drifts = (embedding_drift, projection_drift, outward_drift, vectors_drift)
    spreads = (embedding_spread, projection_spread, outward_spread, vectors_spread)
    rep_out = [
        adam_step(weight, grad * factor, drift, spread, rate)
        for weight, grad, drift, spread, rate in zip(replicated, rep_grads, drifts, spreads, (0.05, 0.05, 0.1, 0.2))
    ]
    ffn_out = adam_step(feedforward, pair_grad * factor, feedforward_drift, feedforward_spread, 0.05)
    results = [jnp.stack([loss_total, crops]), grad_norm]
    for fresh, moved, varied in (rep_out[0], rep_out[1], rep_out[2], ffn_out, rep_out[3]):
        results.extend([fresh, moved, varied, fresh.astype(bf16)])
    return tuple(results)


def solution(mesh):
    columns, row = mesh.shape["col"], mesh.shape["row"]
    fine = jax.sharding.Mesh(mesh.devices.reshape(columns, row // 2, 2), ("col", "deep", "core"))
    split_all, tiles, full = P(("col", "deep", "core")), P(None, ("deep", "core"), "col"), P()
    return jax.shard_map(
        functools.partial(body, columns, row // 2),
        mesh=fine,
        in_specs=(split_all,) * 5 + (full,) * 3 + (tiles,) + (full,) * 7 + (tiles,) * 2 + (full,) * 2,
        out_specs=(full,) * 14 + (tiles,) * 4 + (full,) * 4,
        check_vma=False,
    )
```

time: 2020 us -> 628 us (0.31); the launches traced: 1990 us -> 620 us
  matrix products: 647 us -> 0 us
  local copies, waits for them, and re-layouts: 450 us -> 23.9 us
  waiting for transfers between devices: 463 us -> 140 us
  Pallas kernels: 0 us -> 294 us
  other arithmetic: 318 us -> 58.5 us
  starting transfers between devices: 0.29 us -> 47.5 us
  blocking collectives: 81.9 us -> 35.3 us
    dot_general x31 -> x0, matrix products: 647 us -> none  [the longest x4 123 us: slot_scores(): jnp.einsum('qhe,khe->hqk', queries, key_rows, preferred_element_type=jnp....]
    dynamic_update_slice x13 -> x0, local copies, waits for them, and re-layouts: 297 us -> none  [the longest x12 297 us: body(): lax.map(slot_backward, (by_slot(queries), by_slot(key_rows), by_slot(valu...]
    pallas_call x0 -> x9, Pallas kernels: none -> 294 us  [the longest x5 113 us: body(): pl.pallas_call(functools.partial(attention_back_kernel, chunk=half, chain...]
    all_gather x3 -> x1, waiting for transfers between devices: 213 us -> 0.01 us  [body(): lax.all_gather(feedforward.astype(bf16), everywhere, axis=1, tiled=True)]
    convert_element_type x12 -> x8, other arithmetic: 170 us -> 24.7 us  [the longest x5 20.7 us: body(): results.extend([fresh, moved, varied, fresh.astype(bf16)])]
    reduce_scatter x3 -> x0, waiting for transfers between devices: 135 us -> none  [the longest x1 73.6 us: body(): lax.psum_scatter(contract_cols(part, ffn_tile[0]).astype(jnp.bfloat16), '...]
    all_to_all x0 -> x10, waiting for transfers between devices: none -> 127 us  [swap(): return lax.all_to_all(values, axes, 0, 0, tiled=True)]
    psum x1 -> x0, waiting for transfers between devices: 115 us -> none  [body(): lax.psum((table_grad, in_grad, out_grad, vector_grad, ffn_square, loss_lo...]
  transfers between devices with their start and end apart: 7 -> 16, of which waited for: 5 -> 13; matrix products, arithmetic and copies ran while one was open for 61% -> 8% of each run, Pallas kernels for 0% -> 34%
where the time goes in v1:
time: 628 us; the launch traced here: 620 us
  Pallas kernels  294 us (47%)
  waiting for transfers between devices  140 us (22%)
  other arithmetic  58.5 us (9%)
  starting transfers between devices  47.5 us (8%)
  blocking collectives  35.3 us (6%)
  local copies, waits for them, and re-layouts  23.9 us (4%)
  between operations  20.7 us (3%)
    all_to_all x10, waiting for transfers between devices, swap(): return lax.all_to_all(values, axes, 0, 0, tiled=True)  127 us
    pallas_call x5, Pallas kernels, body(): pl.pallas_call(functools.partial(attention_back_kernel, chunk=half, chain...  113 us
    pallas_call x1, Pallas kernels, body(): pl.pallas_call(middle_kernel, grid=(blocks,), in_specs=[by_block(8), by_b...  85.3 us
    pallas_call x1, Pallas kernels, body(): pl.pallas_call(attention_kernel, grid=(slots, heads // per), in_specs=[he...  61.4 us
    all_to_all x10, starting transfers between devices, swap(): return lax.all_to_all(values, axes, 0, 0, tiled=True)  44.7 us
    all_to_all x7, blocking collectives, swap(): return lax.all_to_all(values, axes, 0, 0, tiled=True)  35.3 us
    convert_element_type x5, other arithmetic, body(): results.extend([fresh, moved, varied, fresh.astype(bf16)])  20.7 us
    pallas_call x1, Pallas kernels, body(): pl.pallas_call(input_back_kernel, grid=(blocks,), in_specs=[by_block(8)]...  17.7 us
  transfers between devices with their start and end apart: 16, of which 13 were waited for; matrix products, arithmetic and copies ran while one was open for 8% of the time, Pallas kernels for 34%

profile of v1, /device:TPU:0, one launch (start us, length us, event | category | flops | bytes accessed | tf_op | source)
XLA Modules:
  0.0 619.7 jit_solution(1886189728386440795)
XLA Ops:
  7.2 1.7 convert_element_type.95
  12.9 15.8 %embed_and_qkv.1 = (f32[640,2048]{1,0:T(8,128)}, bf16[656,2048]{1,0:T(8,128)(2,1)}, bf16[20,48,2048]{2,1,0:T(8,128)(2,1)}, bf16[20,48,2048]{2,1,0:T(8,128)(2,1)}, bf16[20,48,2048]{2,1,0:T(8,128)(2,1)}) custom-call(f32[8,2048]{1,0:T(8,128)} %stack.27.meta, f32[33,640]{1,0:T(8,128)} %embedding.3, f32[640,1920]{1,0:T(8,128)} %projection.3, f32[15,640]{1,0:T(8,128)} %vectors.5, ...), custom_call_target="tpu_custom_call" | custom-call | flops 5033164800 | bytes 26214400 | tf_op jit(solution)/shard_map/embed_and_qkv/pallas_call | solution.py:447
  28.7 61.4 %attention.1 = (bf16[20,32,2048]{2,1,0:T(8,128)(2,1)}, bf16[20,48,2048]{2,1,0:T(8,128)(2,1)}) custom-call(bf16[20,48,2048]{2,1,0:T(8,128)(2,1)} %get-tuple-element.55.q_ext, bf16[20,48,2048]{2,1,0:T(8,128)(2,1)} %get-tuple-element.56.k_ext, bf16[20,48,2048]{2,1,0:T(8,128)(2,1)} %get-tuple-element.57.v_ext), custom_call_target="tpu_custom_call" | custom-call | flops 42949672960 | bytes 15728640 | tf_op jit(solution)/shard_map/attention/pallas_call | solution.py:467
  90.1 85.3 %feedforward_and_head.1 = (f32[640,2048]{1,0:T(8,128)}, bf16[20,48,2048]{2,1,0:T(8,128)(2,1)}, bf16[2,4,640,640]{3,2,1,0:T(8,128)(2,1)}, bf16[768,640]{1,0:T(8,128)(2,1)}, f32[8,128]{1,0:T(8,128)}) custom-call(f32[8,2048]{1,0:T(8,128)} %stack.27.meta, f32[640,2048]{1,0:T(8,128)} %get-tuple-element.54.x0, bf16[640,2048]{1,0:T(8,128)(2,1)} %bitcast.67, ...), custom_call_target="tpu_custom_call" | custom-call | flops 45298483200 | bytes 44564480 | tf_op jit(solution)/shard_map/feedforward_and_head/pallas_call | solution.py:482
  175.4 3.6 all-to-all-start.13
  179.0 22.4 %attention_back.5 = (bf16[20,32,2048]{2,1,0:T(8,128)(2,1)}, bf16[20,32,2048]{2,1,0:T(8,128)(2,1)}, bf16[20,32,2048]{2,1,0:T(8,128)(2,1)}, bf16[768,384]{1,0:T(8,128)(2,1)}) custom-call(bf16[20,48,2048]{2,1,0:T(8,128)(2,1)} %get-tuple-element.58.q_ext, bf16[20,48,2048]{2,1,0:T(8,128)(2,1)} %get-tuple-element.56.k_ext, ...), custom_call_target="tpu_custom_call" | custom-call | flops 21474836480 | bytes 15728640 | tf_op jit(solution)/shard_map/attention_back/pallas_call | solution.py:545
  201.5 22.7 %attention_back.6 = (bf16[20,32,2048]{2,1,0:T(8,128)(2,1)}, bf16[20,32,2048]{2,1,0:T(8,128)(2,1)}, bf16[20,32,2048]{2,1,0:T(8,128)(2,1)}, bf16[768,384]{1,0:T(8,128)(2,1)}) custom-call(bf16[20,48,2048]{2,1,0:T(8,128)(2,1)} %get-tuple-element.58.q_ext, ...), custom_call_target="tpu_custom_call", output_to_operand_aliasing={{0}: (10, {}), {1}: (11, {}), {2}: (12, {})} | custom-call | flops 21474836480 | bytes 15728640 | tf_op jit(solution)/shard_map/attention_back/pallas_call | solution.py:545
  224.2 22.7 %attention_back.7 = (bf16[20,32,2048]{2,1,0:T(8,128)(2,1)}, bf16[20,32,2048]{2,1,0:T(8,128)(2,1)}, bf16[20,32,2048]{2,1,0:T(8,128)(2,1)}, bf16[768,384]{1,0:T(8,128)(2,1)}) custom-call(bf16[20,48,2048]{2,1,0:T(8,128)(2,1)} %get-tuple-element.58.q_ext, ...), custom_call_target="tpu_custom_call", output_to_operand_aliasing={{0}: (10, {}), {1}: (11, {}), {2}: (12, {})} | custom-call | flops 21474836480 | bytes 15728640 | tf_op jit(solution)/shard_map/attention_back/pallas_call | solution.py:545
  246.9 22.9 %attention_back.8 = (bf16[20,32,2048]{2,1,0:T(8,128)(2,1)}, bf16[20,32,2048]{2,1,0:T(8,128)(2,1)}, bf16[20,32,2048]{2,1,0:T(8,128)(2,1)}, bf16[768,384]{1,0:T(8,128)(2,1)}) custom-call(bf16[20,48,2048]{2,1,0:T(8,128)(2,1)} %get-tuple-element.58.q_ext, ...), custom_call_target="tpu_custom_call", output_to_operand_aliasing={{0}: (10, {}), {1}: (11, {}), {2}: (12, {})} | custom-call | flops 21474836480 | bytes 15728640 | tf_op jit(solution)/shard_map/attention_back/pallas_call | solution.py:545
  269.8 22.6 %attention_back.9 = (bf16[20,32,2048]{2,1,0:T(8,128)(2,1)}, bf16[20,32,2048]{2,1,0:T(8,128)(2,1)}, bf16[20,32,2048]{2,1,0:T(8,128)(2,1)}, bf16[768,384]{1,0:T(8,128)(2,1)}) custom-call(bf16[20,48,2048]{2,1,0:T(8,128)(2,1)} %get-tuple-element.58.q_ext, ...), custom_call_target="tpu_custom_call", output_to_operand_aliasing={{0}: (10, {}), {1}: (11, {}), {2}: (12, {})} | custom-call | flops 21474836480 | bytes 15728640 | tf_op jit(solution)/shard_map/attention_back/pallas_call | solution.py:545
  292.4 6.6 %all-to-all-start = ((bf16[2,2560,640]{2,1,0:T(8,128)(2,1)}), bf16[2,2560,640]{2,1,0:T(8,128)(2,1)}, u32[]{:S(2)}, u32[]{:S(2)}) async-start(bf16[2,2560,640]{2,1,0:T(8,128)(2,1)} %bitcast.46), calls=%async_computation | async-start | bytes 13107200 | tf_op jit(solution)/shard_map/all_to_all | solution.py:505
  300.1 5.1 all-to-all-done
  305.2 4.2 all_to_all.150
  309.4 4.2 all_to_all.151
  313.6 4.2 all_to_all.152
  317.8 5.3 all_to_all.153
  323.1 5.3 all_to_all.154
  328.4 8.4 %all-to-all-start.14 = ((bf16[16,24,640]{2,1,0:T(8,128)(2,1)}), bf16[16,24,640]{2,1,0:T(8,128)(2,1)}, u32[]{:S(2)}, u32[]{:S(2)}) async-start(bf16[16,24,640]{2,1,0:T(8,128)(2,1)} %bitcast.52), calls=%async_computation.14 | async-start | bytes 983040 | tf_op jit(solution)/shard_map/all_to_all | solution.py:505
  338.0 14.6 %all-to-all-done.14 = bf16[16,24,640]{2,1,0:T(8,128)(2,1)} async-done(((bf16[16,24,640]{2,1,0:T(8,128)(2,1)}), bf16[16,24,640]{2,1,0:T(8,128)(2,1)}, u32[]{:S(2)}, u32[]{:S(2)}) %all-to-all-start.14) | async-done | bytes 491552 | tf_op jit(solution)/shard_map/all_to_all | solution.py:505
  352.6 3.6 all-to-all-start.11
  357.7 15.5 %all-to-all-done.11 = bf16[16,24,768]{2,1,0:T(8,128)(2,1)S(1)} async-done(((bf16[16,24,768]{2,1,0:T(8,128)(2,1)}), bf16[16,24,768]{2,1,0:T(8,128)(2,1)S(1)}, u32[]{:S(2)}, u32[]{:S(2)}) %all-to-all-start.11) | async-done | bytes 589856 | tf_op jit(solution)/shard_map/all_to_all | solution.py:505
  373.2 3.6 all-to-all-start.7
  377.9 22.0 %all-to-all-done.7 = bf16[16,24,1152]{2,1,0:T(8,128)(2,1)S(1)} async-done(((bf16[16,24,1152]{2,1,0:T(8,128)(2,1)}), bf16[16,24,1152]{2,1,0:T(8,128)(2,1)S(1)}, u32[]{:S(2)}, u32[]{:S(2)}) %all-to-all-start.7) | async-done | bytes 884768 | tf_op jit(solution)/shard_map/all_to_all | solution.py:505
  400.8 3.6 all-to-all-start.15
  404.5 14.6 %all-to-all-done.15 = bf16[16,24,640]{2,1,0:T(8,128)(2,1)S(1)} async-done(((bf16[16,24,640]{2,1,0:T(8,128)(2,1)}), bf16[16,24,640]{2,1,0:T(8,128)(2,1)S(1)}, u32[]{:S(2)}, u32[]{:S(2)}) %all-to-all-start.15) | async-done | bytes 491552 | tf_op jit(solution)/shard_map/all_to_all | solution.py:505
  419.9 3.8 all-to-all-start.12
  423.7 6.6 %reduce_sum.216 = bf16[2560,640]{1,0:T(8,128)(2,1)} reduce(bf16[2,2560,640]{2,1,0:T(8,128)(2,1)} %all-to-all-done, bf16[]{:T(256)} %constant.34.clone.1), dimensions={0}, to_apply=%region_3.4 | reduce | flops 1638400 | bytes 9830402 | tf_op jit(solution)/shard_map/reduce_sum | solution.py:508
  430.3 10.2 %all-to-all-done.12 = bf16[16,24,768]{2,1,0:T(8,128)(2,1)S(1)} async-done(((bf16[16,24,768]{2,1,0:T(8,128)(2,1)}), bf16[16,24,768]{2,1,0:T(8,128)(2,1)S(1)}, u32[]{:S(2)}, u32[]{:S(2)}) %all-to-all-start.12) | async-done | bytes 589856 | tf_op jit(solution)/shard_map/all_to_all | solution.py:505
  441.3 3.7 all-to-all-start.1
  446.3 35.4 %all-to-all-done.1 = bf16[4,640,640]{2,1,0:T(8,128)(2,1)S(1)} async-done(((bf16[4,640,640]{2,1,0:T(8,128)(2,1)}), bf16[4,640,640]{2,1,0:T(8,128)(2,1)S(1)}, u32[]{:S(2)}, u32[]{:S(2)}) %all-to-all-start.1) | async-done | bytes 3276832 | tf_op jit(solution)/shard_map/all_to_all | solution.py:505
  482.7 4.3 all-to-all-start.8
  489.5 17.7 %input_back.1 = f32[56,640]{1,0:T(8,128)} custom-call(f32[8,2048]{1,0:T(8,128)} %stack.27.meta, f32[640,2048]{1,0:T(8,128)} %get-tuple-element.54.x0, bf16[640,2048]{1,0:T(8,128)(2,1)} %bitcast.47, bf16[640,2048]{1,0:T(8,128)(2,1)} %bitcast.48, bf16[640,2048]{1,0:T(8,128)(2,1)} %bitcast.49, f32[640,2048]{1,0:T(8,128)} %get-tuple-element.77.dx1, ...), custom_call_target="tpu_custom_call" | custom-call | flops 5033164800 | bytes 26214400 | tf_op jit(solution)/shard_map/input_back/pallas_call | solution.py:570
  512.3 7.9 %all_to_all.155 = bf16[2,384,2560]{2,1,0:T(8,128)(2,1)} all-to-all(bf16[2,384,2560]{2,1,0:T(8,128)(2,1)S(1)} %broadcast_in_dim.59), channel_id=1, replica_groups=mesh['col'=4,'deep'=4,'core'=2] {'core'}, dimensions={0} | all-to-all | bytes 7864320 | tf_op jit(solution)/shard_map/all_to_all | solution.py:505
  520.2 3.5 all-to-all-start.2
  523.7 3.2 bitcast_convert_fusion
  537.2 7.8 %all-to-all-done.2 = bf16[4,160,640]{2,1,0:T(8,128)(2,1)S(1)} async-done(((bf16[4,160,640]{2,1,0:T(8,128)(2,1)}), bf16[4,160,640]{2,1,0:T(8,128)(2,1)S(1)}, u32[]{:S(2)}, u32[]{:S(2)}) %all-to-all-start.2) | async-done | bytes 819232 | tf_op jit(solution)/shard_map/all_to_all | solution.py:505
  545.2 4.3 all_to_all.156
  551.7 1.7 slice_dynamic-update-slice_fusion.2
  553.6 1.8 slice_dynamic-update-slice_fusion.1
  555.4 4.6 collective-permute-done.1
  560.4 1.8 slice_dynamic-update-slice_fusion
  563.9 6.2 %collective-permute-done.2 = f32[64,640]{1,0:T(8,128)S(1)} collective-permute-done((f32[64,640]{1,0:T(8,128)S(1)}, f32[64,640]{1,0:T(8,128)S(1)}, u32[]{:S(2)}, u32[]{:S(2)}) %collective-permute-start.2) | collective-permute-done | bytes 163872 | tf_op jit(solution)/shard_map/ppermute | solution.py:587
  571.2 4.3 multiply_reduce_fusion
  577.5 2.5 multiply_reduce_fusion.1
  579.9 1.8 collective-permute-done.4
  588.6 1.9 pad_maximum_fusion.4
  592.8 6.0 fusion.12
  598.9 11.0 %fusion.14 = (bf16[640,1920]{1,0:T(8,128)(2,1)}, f32[640,1920]{1,0:T(8,128)}, f32[640,1920]{1,0:T(8,128)}, f32[640,1920]{1,0:T(8,128)}) fusion(f32[640,1920]{1,0:T(8,128)S(1)} %bitcast.44, f32[]{:T(128)S(6)} %mul.209, f32[648,1920]{1,0:T(8,128)} %slice_dynamic-update-slice_fusion, f32[640,1920]{1,0:T(8,128)} %param.36, f32[640,1920]{1,0:T(8,128)} %param.37), kind=kLoop, calls=%fused_computation.68 | loop fusion | flops 19660800 | bytes 36864004 | tf_op jit(solution)/shard_map/convert_element_type | solution.py:622
  (118 shorter events, 45.1 us)
Async XLA Ops:
  7.2 82.9 %all-gather.2.cloned.1.call-start = ((), (), s32[]{:S(2)}) async-start(), calls=%async_computation.17 | async-start | bytes 6758400 | tf_op jit(solution)/shard_map/all_gather | solution.py:418
  175.4 116.9 %all-to-all-start.13 = ((bf16[2,384,640]{2,1,0:T(8,128)(2,1)}), bf16[2,384,640]{2,1,0:T(8,128)(2,1)S(1)}, u32[]{:S(2)}, u32[]{:S(2)}) async-start(bf16[2,384,640]{2,1,0:T(8,128)(2,1)} %bitcast.54), calls=%async_computation.13 | async-start | bytes 1966080 | tf_op jit(solution)/shard_map/all_to_all | solution.py:505
  292.4 12.8 %copy-start.7 = (bf16[768,384]{1,0:T(8,128)(2,1)S(1)}, bf16[768,384]{1,0:T(8,128)(2,1)}, u32[]{:S(2)}) copy-start(bf16[768,384]{1,0:T(8,128)(2,1)} %get-tuple-element.80) | copy-start | bytes 1769476
  292.4 17.0 %copy-start.8 = (bf16[768,384]{1,0:T(8,128)(2,1)S(1)}, bf16[768,384]{1,0:T(8,128)(2,1)}, u32[]{:S(2)}) copy-start(bf16[768,384]{1,0:T(8,128)(2,1)} %get-tuple-element.81) | copy-start | bytes 1769476
  292.4 21.2 %copy-start.9 = (bf16[768,384]{1,0:T(8,128)(2,1)S(1)}, bf16[768,384]{1,0:T(8,128)(2,1)}, u32[]{:S(2)}) copy-start(bf16[768,384]{1,0:T(8,128)(2,1)} %get-tuple-element.82) | copy-start | bytes 1769476
  292.4 12.8 %all-to-all-start = ((bf16[2,2560,640]{2,1,0:T(8,128)(2,1)}), bf16[2,2560,640]{2,1,0:T(8,128)(2,1)}, u32[]{:S(2)}, u32[]{:S(2)}) async-start(bf16[2,2560,640]{2,1,0:T(8,128)(2,1)} %bitcast.46), calls=%async_computation | async-start | bytes 13107200 | tf_op jit(solution)/shard_map/all_to_all | solution.py:505
  328.4 24.2 %all-to-all-start.14 = ((bf16[16,24,640]{2,1,0:T(8,128)(2,1)}), bf16[16,24,640]{2,1,0:T(8,128)(2,1)}, u32[]{:S(2)}, u32[]{:S(2)}) async-start(bf16[16,24,640]{2,1,0:T(8,128)(2,1)} %bitcast.52), calls=%async_computation.14 | async-start | bytes 983040 | tf_op jit(solution)/shard_map/all_to_all | solution.py:505
  352.6 20.6 %all-to-all-start.11 = ((bf16[16,24,768]{2,1,0:T(8,128)(2,1)}), bf16[16,24,768]{2,1,0:T(8,128)(2,1)S(1)}, u32[]{:S(2)}, u32[]{:S(2)}) async-start(bf16[16,24,768]{2,1,0:T(8,128)(2,1)} %bitcast.26), calls=%async_computation.11 | async-start | bytes 1179648 | tf_op jit(solution)/shard_map/all_to_all | solution.py:505
  373.2 26.7 %all-to-all-start.7 = ((bf16[16,24,1152]{2,1,0:T(8,128)(2,1)}), bf16[16,24,1152]{2,1,0:T(8,128)(2,1)S(1)}, u32[]{:S(2)}, u32[]{:S(2)}) async-start(bf16[16,24,1152]{2,1,0:T(8,128)(2,1)} %bitcast.22), calls=%async_computation.7 | async-start | bytes 1769472 | tf_op jit(solution)/shard_map/all_to_all | solution.py:505
  399.9 30.4 %copy-start.1 = (bf16[16,24,1152]{2,1,0:T(8,128)(2,1)}, bf16[16,24,1152]{2,1,0:T(8,128)(2,1)S(1)}, u32[]{:S(2)}) copy-start(bf16[16,24,1152]{2,1,0:T(8,128)(2,1)S(1)} %all-to-all-done.7) | copy-start | bytes 2654212
  400.8 18.2 %all-to-all-start.15 = ((bf16[16,24,640]{2,1,0:T(8,128)(2,1)}), bf16[16,24,640]{2,1,0:T(8,128)(2,1)S(1)}, u32[]{:S(2)}, u32[]{:S(2)}) async-start(bf16[16,24,640]{2,1,0:T(8,128)(2,1)} %broadcast_in_dim.58), calls=%async_computation.15 | async-start | bytes 983040 | tf_op jit(solution)/shard_map/all_to_all | solution.py:505
  419.0 11.3 %copy-start.3 = (bf16[16,24,640]{2,1,0:T(8,128)(2,1)}, bf16[16,24,640]{2,1,0:T(8,128)(2,1)S(1)}, u32[]{:S(2)}) copy-start(bf16[16,24,640]{2,1,0:T(8,128)(2,1)S(1)} %all-to-all-done.15) | copy-start | bytes 1474564
  419.9 20.6 %all-to-all-start.12 = ((bf16[16,24,768]{2,1,0:T(8,128)(2,1)}), bf16[16,24,768]{2,1,0:T(8,128)(2,1)S(1)}, u32[]{:S(2)}, u32[]{:S(2)}) async-start(bf16[16,24,768]{2,1,0:T(8,128)(2,1)} %broadcast_in_dim.35), calls=%async_computation.12 | async-start | bytes 1179648 | tf_op jit(solution)/shard_map/all_to_all | solution.py:505
  440.5 0.8 copy-start.2
  440.5 46.5 %copy-start.18 = (s32[2]{0:T(128)S(1)}, s32[2]{0:T(128)}, u32[]{:S(2)}) copy-start(s32[2]{0:T(128)} %param.28) | copy-start | bytes 28
  441.3 40.4 %all-to-all-start.1 = ((bf16[4,640,640]{2,1,0:T(8,128)(2,1)}), bf16[4,640,640]{2,1,0:T(8,128)(2,1)S(1)}, u32[]{:S(2)}, u32[]{:S(2)}) async-start(bf16[4,640,640]{2,1,0:T(8,128)(2,1)} %bitcast.45), calls=%async_computation.1 | async-start | bytes 6553600 | tf_op jit(solution)/shard_map/all_to_all | solution.py:505
  482.7 27.7 %all-to-all-start.8 = ((bf16[16,24,1152]{2,1,0:T(8,128)(2,1)}), bf16[16,24,1152]{2,1,0:T(8,128)(2,1)}, u32[]{:S(2)}, u32[]{:S(2)}) async-start(bf16[16,24,1152]{2,1,0:T(8,128)(2,1)} %broadcast_in_dim.34), calls=%async_computation.8 | async-start | bytes 1769472 | tf_op jit(solution)/shard_map/all_to_all | solution.py:505
  520.2 24.9 %all-to-all-start.2 = ((bf16[4,160,640]{2,1,0:T(8,128)(2,1)}), bf16[4,160,640]{2,1,0:T(8,128)(2,1)S(1)}, u32[]{:S(2)}, u32[]{:S(2)}) async-start(bf16[4,160,640]{2,1,0:T(8,128)(2,1)} %bitcast.12), calls=%async_computation.2 | async-start | bytes 1638400 | tf_op jit(solution)/shard_map/all_to_all | solution.py:505
  526.9 9.4 %copy-start = (f32[768,2560]{1,0:T(8,128)}, f32[768,2560]{1,0:T(8,128)S(1)}, u32[]{:S(2)}) copy-start(f32[768,2560]{1,0:T(8,128)S(1)} %bitcast_convert_fusion) | copy-start | bytes 23592964
  527.7 23.8 %copy-start.6 = (f32[56,640]{1,0:T(8,128)S(1)}, f32[56,640]{1,0:T(8,128)}, u32[]{:S(2)}) copy-start(f32[56,640]{1,0:T(8,128)} %input_back.1) | copy-start | bytes 430084
  551.5 1.9 collective-permute-start
  553.5 6.5 %collective-permute-start.1 = (f32[64,640]{1,0:T(8,128)S(1)}, f32[64,640]{1,0:T(8,128)S(1)}, u32[]{:S(2)}, u32[]{:S(2)}) collective-permute-start(f32[64,640]{1,0:T(8,128)S(1)} %fusion.6), channel_id=1, source_target_pairs={{0,2},{1,3},{2,0},{3,1},{4,6},{5,7},{6,4},{7,5},{8,10},{9,11},{10,... | collective-permute-start | bytes 491528 | tf_op jit(solution)/shard_map/ppermute | solution.py:587
  555.4 35.1 %copy-start.12 = (f32[15,640]{1,0:T(8,128)S(1)}, f32[15,640]{1,0:T(8,128)}, u32[]{:S(2)}) copy-start(f32[15,640]{1,0:T(8,128)} %vectors.5) | copy-start | bytes 115204
  555.4 35.1 %copy-start.16 = (f32[15,640]{1,0:T(8,128)S(1)}, f32[15,640]{1,0:T(8,128)}, u32[]{:S(2)}) copy-start(f32[15,640]{1,0:T(8,128)} %param.42) | copy-start | bytes 115204
  555.4 35.1 %copy-start.17 = (f32[15,640]{1,0:T(8,128)S(1)}, f32[15,640]{1,0:T(8,128)}, u32[]{:S(2)}) copy-start(f32[15,640]{1,0:T(8,128)} %param.43) | copy-start | bytes 115204
  555.4 35.7 %copy-start.13 = (f32[33,640]{1,0:T(8,128)S(1)}, f32[33,640]{1,0:T(8,128)}, u32[]{:S(2)}) copy-start(f32[33,640]{1,0:T(8,128)} %embedding.3) | copy-start | bytes 253444
  555.4 35.7 %copy-start.14 = (f32[33,640]{1,0:T(8,128)S(1)}, f32[33,640]{1,0:T(8,128)}, u32[]{:S(2)}) copy-start(f32[33,640]{1,0:T(8,128)} %param.34) | copy-start | bytes 253444
  555.4 35.7 %copy-start.15 = (f32[33,640]{1,0:T(8,128)S(1)}, f32[33,640]{1,0:T(8,128)}, u32[]{:S(2)}) copy-start(f32[33,640]{1,0:T(8,128)} %param.35) | copy-start | bytes 253444
  560.1 10.1 %collective-permute-start.2 = (f32[64,640]{1,0:T(8,128)S(1)}, f32[64,640]{1,0:T(8,128)S(1)}, u32[]{:S(2)}, u32[]{:S(2)}) collective-permute-start(f32[64,640]{1,0:T(8,128)S(1)} %add.115), channel_id=1, source_target_pairs={{0,4},{1,5},{2,6},{3,7},{4,0},{5,1},{6,2},{7,3},{8,12},{9,13},{10,... | collective-permute-start | bytes 491528 | tf_op jit(solution)/shard_map/ppermute | solution.py:587
  562.2 30.6 %copy-start.4 = (f32[640,640]{1,0:T(8,128)S(1)}, f32[640,640]{1,0:T(8,128)}, u32[]{:S(2)}) copy-start(f32[640,640]{1,0:T(8,128)} %outward.1) | copy-start | bytes 4915204
  570.2 6.2 collective-permute-start.3
  571.2 27.6 %slice-start = ((s8[4915200]{0:T(1024)(128)(4,1)}), s8[720896]{0:T(1024)(128)(4,1)S(1)}, s32[]{:S(2)}) async-start(s8[4915200]{0:T(1024)(128)(4,1)} %bitcast.43), calls=%async_computation.18 | async-start | bytes 1441792
  576.4 5.4 collective-permute-start.4
  592.8 6.0 slice-start.1
  598.8 11.0 %copy-start.5 = (f32[2,80,640]{2,1,0:T(8,128)S(1)}, f32[2,80,640]{2,1,0:T(8,128)}, u32[]{:S(2)}) copy-start(f32[2,80,640]{2,1,0:T(8,128)} %param.32) | copy-start | bytes 1228804
  598.9 11.0 %copy-start.10 = (f32[2,80,640]{2,1,0:T(8,128)S(1)}, f32[2,80,640]{2,1,0:T(8,128)}, u32[]{:S(2)}) copy-start(f32[2,80,640]{2,1,0:T(8,128)} %param.40) | copy-start | bytes 1228804
  598.9 11.0 %copy-start.11 = (f32[2,80,640]{2,1,0:T(8,128)S(1)}, f32[2,80,640]{2,1,0:T(8,128)}, u32[]{:S(2)}) copy-start(f32[2,80,640]{2,1,0:T(8,128)} %param.41) | copy-start | bytes 1228804
Sparse Core Ops, SparseCore 0:
  11.5 73.2 all-gather.1

commit v2 on v1

--- a/solution.py
+++ b/solution.py
@@ -15,6 +15,9 @@
 FF = 2560
 STEP = 10
 VPAD = 48
+VOCAB_ROWS = 40
+TAIL = 24
+UNITS = 1280
 THIRD = 40
 REST_TABLE = 32
 
@@ -67,6 +70,14 @@
 
 def rows_of(count, width):
     return lax.broadcasted_iota(jnp.int32, (count, width), 0)
+
+
+def split_halves(total, keep, send):
+    rows = keep.shape[0]
+    first, second = total[0:rows, :], total[rows:, :]
+    is_first = lax.axis_index("core") == 0
+    keep[...] = jnp.where(is_first, first, second).astype(bf16)
+    send[...] = jnp.where(is_first, second, first).astype(bf16)
 
 
 def lane_sum(values):
@@ -137,9 +148,12 @@
 def attention_kernel(q_ext, k_ext, v_ext, out, q_next):
     heads, _, width = q_ext.shape
     factor = LOG2E * SCALE
+    upcoming = dot(k_ext[0], q_ext[0], TN)
     for head in range(heads):
         queries = q_ext[head]
-        scores = dot(k_ext[head], queries, TN)
+        scores = upcoming
+        if head + 1 < heads:
+            upcoming = dot(k_ext[head + 1], q_ext[head + 1], TN)
         top = jnp.max(scores, axis=0, keepdims=True)
         weights = jnp.exp2((scores - top) * factor).astype(bf16)
         mixed = dot(v_ext[head], weights)
@@ -156,7 +170,7 @@
 def attention_back_kernel(
     q_ext, k_ext, v_ext, do_ext, low, meta, cos_a, cos_b, sin_a, sin_b, *rest, chunk, chained
 ):
-    dq, dk, dv, dweight, grads, total = rest[3:] if chained else rest
+    dq, dk, dv, keep, send, grads, total = rest[3:] if chained else rest
     slot = pl.program_id(0)
     heads, _, width = q_ext.shape
     in_second = meta[2:3, :] > 0.5
@@ -191,34 +205,43 @@
 
     @pl.when(slot == 0)
     def _():
-        total[...] = share
+        total[0:rows, :] = share
 
     @pl.when(slot > 0)
     def _():
-        total[...] += share
+        total[0:rows, :] += share
 
     @pl.when(slot == pl.num_programs(0) - 1)
     def _():
-        dweight[...] = jnp.zeros_like(dweight)
-        dweight[0:rows, :] = total[...].astype(bf16)
+        half_rows = keep.shape[0]
+        total[rows:, :] = jnp.zeros((2 * half_rows - rows, total.shape[1]), f32)
+        split_halves(total, keep, send)
 
 
 def middle_kernel(
-    meta, x0, attended, outward, w_up, w_down, embedding, vectors,
-    dx1, do_ext, dw_pair, dw_rest, loss,
-    up_t, down_t, act, slope, dw_up, dw_down, dw_out, dtable, dvec, vec, wide, table, table_t, w_out, w_out_t, sems,
+    meta, x0, attended, outward, pair_all, embedding, vectors,
+    dx1, do_ext, keep_pair, send_pair, keep_rest, send_rest, loss,
+    w_up, w_down, up_t, down_t, act, slope, dw_up, dw_down, dw_out, dtable, dvec, vec, wide, table, table_t, w_out, w_out_t,
+    sems,
 ):
     step = pl.program_id(0)
-    chunks = w_up.shape[0]
+    chunks = pair_all.shape[1]
     model, width = x0.shape
+    hidden_units = w_up.shape[1]
+    unit = hidden_units // chunks
     heads = do_ext.shape[0]
     vocab = embedding.shape[0]
 
     @pl.when(step == 0)
     def _():
-        for part in range(chunks):
-            up_t[part] = w_up[part].T
-            down_t[part] = w_down[part].T
+        fetches = []
+        for side, into in enumerate((w_up, w_down)):
+            for part in range(chunks):
+                fetch = pltpu.make_async_copy(
+                    pair_all.at[side, part], into.at[:, pl.ds(part * unit, unit)], sems.at[2 + side * chunks + part]
+                )
+                fetch.start()
+                fetches.append(fetch)
         vec[...] = columns_of(vectors, wide)
         wide[...] = jnp.zeros_like(wide)
         wide[0:vocab, :] = embedding[...]
@@ -232,6 +255,12 @@
         dtable[...] = jnp.zeros_like(dtable)
         dvec[...] = jnp.zeros_like(dvec)
         loss[...] = jnp.zeros_like(loss)
+        for fetch in fetches:
+            fetch.wait()
+        for part in range(chunks):
+            span = slice(part * unit, (part + 1) * unit)
+            up_t[span, :] = w_up[:, span].T
+            down_t[span, :] = w_down[:, span].T
 
     def col(index):
         return vec[:, index : index + 1]
@@ -240,16 +269,15 @@
     x1 = x0[...] + dot(w_out_t[...], attended[...]) + col(5)
     hat_two, inverse_two = norm_stats(x1)
     c_low = (hat_two * col(6) + col(7)).astype(bf16)
-    branch = None
-    for part in range(chunks):
-        hidden = dot(up_t[part], c_low) + col(8 + part)
-        cdf = 0.5 + 0.5 * lax.erf(hidden * (0.5**0.5))
-        density = jnp.exp(hidden * hidden * -0.5) * (1.0 / math.sqrt(2.0 * math.pi))
-        act[part] = (hidden * cdf).astype(bf16)
-        slope[part] = (cdf + hidden * density).astype(bf16)
-        share = dot(w_down[part], act[part])
-        branch = share if branch is None else branch + share
-    x2 = x1 + branch + col(after)
+    for first in range(0, hidden_units, UNITS):
+        inner = dot(up_t[first : first + UNITS, :], c_low)
+        for at in range(first, first + UNITS, model):
+            hidden = inner[at - first : at - first + model, :] + col(8 + at // model)
+            cdf = 0.5 + 0.5 * lax.erf(hidden * (0.5**0.5))
+            density = jnp.exp(hidden * hidden * -0.5) * (1.0 / math.sqrt(2.0 * math.pi))
+            act[at : at + model, :] = (hidden * cdf).astype(bf16)
+            slope[at : at + model, :] = (cdf + hidden * density).astype(bf16)
+    x2 = x1 + dot(w_down[...], act[...]) + col(after)
     hat_end, inverse_end = norm_stats(x2)
     f_low = (hat_end * col(after + 1) + col(after + 2)).astype(bf16)
     vocab_rows = rows_of(VPAD, width)
@@ -269,21 +297,21 @@
     x2_grad = norm_back(f_grad, hat_end, inverse_end, col(after + 1))
     g_low = x2_grad.astype(bf16)
     dvec[:, 3 + chunks : 4 + chunks] += lane_sum(g_low.astype(f32))
-    c_grad = None
-    for part in range(chunks):
-        hidden_grad = (dot(down_t[part], g_low) * slope[part]).astype(bf16)
-        dw_up[part] += dot(c_low, hidden_grad, NT)
-        dw_down[part] += dot(g_low, act[part], NT)
-        dvec[:, 3 + part : 4 + part] += lane_sum(hidden_grad.astype(f32))
-        share = dot(w_up[part], hidden_grad)
-        c_grad = share if c_grad is None else c_grad + share
+    dw_down[...] += dot(g_low, act[...], NT)
+    for first in range(0, hidden_units, UNITS):
+        span = slice(first, first + UNITS)
+        act[span, :] = (dot(down_t[span, :], g_low) * slope[span, :]).astype(bf16)
+    c_grad = dot(w_up[...], act[...])
+    dw_up[...] += dot(c_low, act[...], NT)
+    for part in range(hidden_units // model):
+        dvec[:, 3 + part : 4 + part] += lane_sum(act[part * model : (part + 1) * model, :].astype(f32))
     dvec[:, 1:2] += lane_sum(c_grad * hat_two)
     dvec[:, 2:3] += lane_sum(c_grad)
     x1_grad = x2_grad + norm_back(c_grad, hat_two, inverse_two, col(6))
     dx1[...] = x1_grad
     x1_low = x1_grad.astype(bf16)
     dvec[:, 0:1] += lane_sum(x1_low.astype(f32))
-    dw_out[...] += dot(attended[...], x1_low, NT)
+    dw_out[0:model, :] += dot(attended[...], x1_low, NT)
     o_grad = dot(w_out[...], x1_low).astype(bf16)
     inner = o_grad.astype(f32) * attended[...].astype(f32)
     row = rows_of(EXT - HEAD_DIM, width)
@@ -296,16 +324,20 @@
 
     @pl.when(step == pl.num_programs(0) - 1)
     def _():
+        is_first = lax.axis_index("core") == 0
         copies = []
-        for side, (low, grad) in enumerate(((up_t, dw_up), (down_t, dw_down))):
-            low[...] = grad[...].astype(bf16)
-            copies.append(pltpu.make_async_copy(low, dw_pair.at[side], sems.at[side]))
+        for side, (low, here, there, out) in enumerate(
+            ((down_t, dw_down, dw_up, send_pair), (up_t, dw_up, dw_down, keep_pair))
+        ):
+            for part in range(chunks):
+                span = slice(part * unit, (part + 1) * unit)
+                low[part * model : (part + 1) * model, :] = jnp.where(is_first, here[:, span], there[:, span]).astype(bf16)
+            copies.append(pltpu.make_async_copy(low, out, sems.at[side]))
             copies[side].start()
-        dw_rest[...] = jnp.zeros_like(dw_rest)
-        dw_rest[0:model, :] = dw_out[...].astype(bf16)
         wide[...] = dvec[...].T
         wide[REST_TABLE : REST_TABLE + VPAD, :] = dtable[...]
-        dw_rest[model : model + 128, :] = wide[...].astype(bf16)
+        dw_out[model:, :] = wide[...]
+        split_halves(dw_out, keep_rest, send_rest)
         for copy in copies:
             copy.wait()
 
@@ -314,7 +346,11 @@
     return FF // model
 
 
-def input_back_kernel(meta, x0, dq, dk, dv, dx1, projection, vectors, rest, weight, vec, wide, dvec, dtable):
+def input_back_kernel(meta, x0, dq, dk, dv, dx1, projection, vectors, *rest, last):
+    if last:
+        loss, dvec_in, dtable_in, tail, weight, vec, wide, dvec, dtable = rest
+    else:
+        dvec, dtable, weight, vec, wide = rest
     step = pl.program_id(0)
     model, width = x0.shape
 
@@ -322,42 +358,86 @@
     def _():
         vec[...] = columns_of(vectors, wide)
         weight[...] = projection[...].astype(bf16)
-        dtable[...] = jnp.zeros_like(dtable)
-        dvec[...] = jnp.zeros_like(dvec)
+        dtable[...] = dtable_in[...] if last else jnp.zeros_like(dtable)
+        dvec[...] = dvec_in[...] if last else jnp.zeros_like(dvec)
 
     back = None
     for part, grad in enumerate((dq, dk, dv)):
         share = dot(weight[:, part * model : (part + 1) * model], grad[...])
         back = share if back is None else back + share
     hat, inverse = norm_stats(x0[...])
-    dvec[:, VPAD : VPAD + 1] += lane_sum(back * hat)
-    dvec[:, VPAD + 1 : VPAD + 2] += lane_sum(back)
+    dvec[:, 0:1] += lane_sum(back * hat)
+    dvec[:, 1:2] += lane_sum(back)
+    dvec[0:1, 2:3] += lane_sum(meta[4:5, :])
     x0_grad = dx1[...] + norm_back(back, hat, inverse, vec[:, 0:1])
     onehot = (rows_of(VPAD, width) == meta[0:1, :].astype(jnp.int32)).astype(f32).astype(bf16)
     for piece in split3(x0_grad):
         dtable[...] += dot(onehot, piece.astype(bf16), NT)
 
-    @pl.when(step == pl.num_programs(0) - 1)
-    def _():
-        wide[...] = dvec[...].T
-        rest[0:VPAD, :] = dtable[...]
-        rest[VPAD:, :] = wide[VPAD : VPAD + 8, :]
-
-
-def whole(shape):
-    return pl.BlockSpec(shape, lambda *_: (0,) * len(shape), pipeline_mode=pl.Buffered(1))
-
-
-def shaped(shape, dtype):
-    return jax.ShapeDtypeStruct(shape, dtype)
-
-
-def limits(mib):
-    return pltpu.CompilerParams(vmem_limit_bytes=mib * MIB)
-
-
-def cost(flops, moved, transcendentals=0):
-    return pl.CostEstimate(flops=int(flops), bytes_accessed=int(moved), transcendentals=int(transcendentals))
+    if last:
+
+        @pl.when(step == pl.num_programs(0) - 1)
+        def _():
+            columns = dvec[...].T[0:8, :]
+            tail[:, 0:model] = dtable[0:TAIL, :]
+            tail[0 : VOCAB_ROWS - TAIL, model : 2 * model] = dtable[TAIL:VOCAB_ROWS, :]
+            tail[VOCAB_ROWS - TAIL :, model : 2 * model] = jnp.where(rows_of(8, model) < 2, columns, 0.0)
+            lane = lax.broadcasted_iota(jnp.int32, (TAIL, 128), 1)
+            first = rows_of(TAIL, 128) == 0
+            numbers = jnp.where(lane == 0, loss[0:1, 0:1], jnp.where(lane == 1, columns[2:3, 0:1], 0.0))
+            tail[:, 2 * model :] = jnp.where(first, numbers, 0.0)
+
+
+def encode(tail):
+    wide = tail.shape[1] - 128
+    row = rows_of(tail.shape[0], 128)
+    high, middle, rest = split3(tail[0:1, wide:])
+    scalars = jnp.where(row == 0, high, jnp.where(row == 1, middle, jnp.where(row == 2, rest, 0.0)))
+    return jnp.concatenate([tail[:, :wide], scalars], axis=1)
+
+
+def decode(tail):
+    wide = tail.shape[1] - 128
+    row = rows_of(tail.shape[0], 128)
+    total = tail[0:1, wide:] + tail[1:2, wide:] + tail[2:3, wide:]
+    return jnp.concatenate([tail[:, :wide], jnp.where(row == 0, total, 0.0)], axis=1)
+
+
+def pack_kernel(swapped, pair, tail, out, keep, send, *, pieces):
+    owned = pair.shape[0] - 2 * keep.shape[0]
+    shares = swapped[...].astype(f32)
+    rows = shares.shape[0] // pieces
+    total = None
+    for at in range(pieces):
+        share = shares[at * rows : (at + 1) * rows, :]
+        total = share if total is None else total + share
+    both = pair[...].astype(f32)
+    half = keep.shape[0]
+    first, second = both[0:half, :], both[half : 2 * half, :]
+    square = jnp.sum(lane_sum(first * first + second * second), axis=0, keepdims=True)
+    is_first = lax.axis_index("core") == 0
+    keep[...] = jnp.where(is_first, first, second).astype(bf16)
+    send[...] = jnp.where(is_first, second, first).astype(bf16)
+    values = tail[...]
+    wide = values.shape[1] - 128
+    at_square = (rows_of(values.shape[0], 128) == 0) & (lax.broadcasted_iota(jnp.int32, (values.shape[0], 128), 1) == 2)
+    values = jnp.concatenate([values[:, :wide], values[:, wide:] + jnp.where(at_square, square, 0.0)], axis=1)
+    mine = jnp.concatenate([total, both[2 * half : 2 * half + owned, :]], axis=1)
+    out[...] = jnp.concatenate([mine, encode(values)], axis=0).astype(bf16)
+
+
+def stage_kernel(own, one, two, three, out, *, axis):
+    index = lax.axis_index(axis)
+    odd, high = lax.rem(index, 2) == 1, index >= 2
+    values = [ref[...].astype(f32) for ref in (own, one, two, three)]
+    rows = values[0].shape[0] - TAIL
+    parts = [value[0:rows, :] for value in values]
+    near = jnp.where(odd, parts[1], parts[0]), jnp.where(odd, parts[0], parts[1])
+    far = jnp.where(odd, parts[3], parts[2]), jnp.where(odd, parts[2], parts[3])
+    placed = [jnp.where(high, far[i], near[i]) for i in range(2)] + [jnp.where(high, near[i], far[i]) for i in range(2)]
+    tails = [decode(value[rows:, :]) for value in values]
+    total = (tails[0] + tails[1]) + (tails[2] + tails[3])
+    out[...] = jnp.concatenate([*placed, encode(total)], axis=0).astype(bf16)
 
 
 def adam_step(weight, grad, drift, spread, rate):
@@ -369,6 +449,130 @@
         / (jnp.sqrt(spread / (1.0 - SECOND_DECAY**STEP)) + ADAM_EPS)
     )
     return (weight - rate * (adjusted + WEIGHT_DECAY * weight), drift, spread)
+
+
+def update_kernel(*refs, groups, early_groups):
+    early_mine, early_other, last_mine, last_other, pair_keep, pair_sent = refs[:6]
+    ins, outs = refs[6:21], refs[21:41]
+    pair_out, norm_out, g_in, g_out, g_table, g_vec, scale, sems = refs[41:49]
+    held = refs[49:]
+    step = pl.program_id(0)
+    steps = g_in.shape[0] // outs[4].shape[0]
+
+    def copy(array, chunk):
+        span = pl.ds(chunk * outs[4].shape[0], outs[4].shape[0])
+        return pltpu.make_async_copy(ins[3 + array].at[span], held[array].at[span], sems.at[array, chunk])
+
+    @pl.when(step == 0)
+    def _():
+        for chunk in range(steps):
+            for array in range(6):
+                copy(array, chunk).start()
+
+    vocab, model = ins[0].shape
+    half_rows = early_mine.shape[0]
+    piece = model // groups
+    last_width = 3 * piece * (groups - early_groups)
+    after = model - half_rows
+
+    @pl.when(step == 0)
+    def _():
+        is_first = lax.axis_index("core") == 0
+
+        def halves(mine, other):
+            mine, other = mine[0:half_rows, :].astype(f32), other[0:half_rows, :].astype(f32)
+            return jnp.where(is_first, mine, other), jnp.where(is_first, other, mine)
+
+        squares = jnp.zeros((1, 128), f32)
+
+        def add_squares(values):
+            rows = jnp.sum(values * values, axis=0, keepdims=True)
+            total = None
+            for at in range(0, rows.shape[1], 128):
+                total = rows[:, at : at + 128] if total is None else total + rows[:, at : at + 128]
+            return total
+
+        for mine, other, first, size in (
+            (early_mine, early_other, 0, early_groups),
+            (last_mine, last_other, early_groups, groups - early_groups),
+        ):
+            upper, lower = halves(mine, other)
+            rest_upper, rest_lower = upper[:, last_width:], lower[:, last_width:]
+            upper, lower = upper[:, : 3 * piece * size], lower[:, : 3 * piece * size]
+            squares += add_squares(upper) + add_squares(lower)
+            for group in range(size):
+                for part in range(3):
+                    source = slice((group * 3 + part) * piece, (group * 3 + part + 1) * piece)
+                    at = part * model + (first + group) * piece
+                    g_in[0:half_rows, at : at + piece] = upper[:, source]
+                    g_in[half_rows:model, at : at + piece] = lower[0:after, source]
+                    into = slice((first + group) * piece, (first + group + 1) * piece)
+                    g_vec[2 + part : 3 + part, into] = lower[after : after + 1, source]
+        upper, lower = rest_upper, rest_lower
+        g_out[0:half_rows, :] = upper
+        g_out[half_rows:, :] = lower[0:after, :]
+        others = lower[after : after + REST_TABLE, :]
+        g_vec[5:15, :] = others[0:10, :]
+        tails = [decode(ref[half_rows:, :].astype(f32)) for ref in (last_mine, last_other)]
+        final = tails[0] + tails[1]
+        scalars = final[:, 2 * model :]
+        late = jnp.concatenate([final[:, 0:model], final[0 : VOCAB_ROWS - TAIL, model : 2 * model]], axis=0)
+        table = late + lower[after + REST_TABLE : after + REST_TABLE + VOCAB_ROWS, :]
+        g_table[...] = table
+        tail = final[VOCAB_ROWS - TAIL :, model : 2 * model]
+        g_vec[0:2, :] = tail[0:2, :]
+        squares += add_squares(upper) + add_squares(lower[0:after, :]) + add_squares(others) + add_squares(table)
+        squares += add_squares(tail[0:2, :])
+        total = lane_sum(squares) + scalars[0:1, 2:3]
+        crops = scalars[0:1, 1:2]
+        norm = jnp.sqrt(total) / crops
+        scale[...] = jnp.broadcast_to(jnp.minimum(1.0, CLIP_NORM / (norm + 1e-06)) / crops, scale.shape)
+        pair_out[0] = jnp.sum(scalars[0:1, 0:1])
+        pair_out[1] = jnp.sum(crops)
+        norm_out[0] = jnp.sum(norm)
+
+    factor = scale[0:1, 0:1]
+
+    def update(which, grad, rate, span=...):
+        source = held[which * 3 - 3 : which * 3] if span is not ... else ins[which * 3 : which * 3 + 3]
+        weight, drift, spread = (ref[span] for ref in source)
+        fresh, drift, spread = adam_step(weight, grad * factor, drift, spread, rate)
+        out = outs[which * 4 : which * 4 + 4]
+        out[0][...] = fresh
+        out[1][...] = drift
+        out[2][...] = spread
+        out[3][...] = fresh.astype(bf16)
+
+    @pl.when(step == 0)
+    def _():
+        update(0, g_table[0:vocab, :], 0.05)
+        keep, sent = pair_keep[...].astype(f32), pair_sent[...].astype(f32)
+        is_first = lax.axis_index("core") == 0
+        update(3, jnp.stack([jnp.where(is_first, keep, sent), jnp.where(is_first, sent, keep)]), 0.05)
+        update(4, g_vec[0:15, :], 0.2)
+
+    for array in range(6):
+        copy(array, step).wait()
+    rows = outs[4].shape[0]
+    span = pl.ds(pl.multiple_of(step * rows, rows), rows)
+    update(1, g_in[span, :], 0.05, span)
+    update(2, g_out[span, :], 0.1, span)
+
+
+def whole(shape):
+    return pl.BlockSpec(shape, lambda *_: (0,) * len(shape), pipeline_mode=pl.Buffered(1))
+
+
+def shaped(shape, dtype):
+    return jax.ShapeDtypeStruct(shape, dtype)
+
+
+def limits(mib):
+    return pltpu.CompilerParams(vmem_limit_bytes=mib * MIB)
+
+
+def cost(flops, moved, transcendentals=0):
+    return pl.CostEstimate(flops=int(flops), bytes_accessed=int(moved), transcendentals=int(transcendentals))
 
 
 def rotary_constants(rows):
@@ -429,8 +633,9 @@
     half_counts = jnp.where(split > 0.5, half_counts, jnp.sum(half_counts, axis=1, keepdims=True))
     token_weight = (pick.reshape(slots, 2, half) / half_counts[:, :, None]).reshape(tokens)
     zero = jnp.zeros((tokens,), f32)
+    crop_share = jnp.broadcast_to((1 + splits).astype(f32)[:, None] * (1.0 / rows), (slots, rows)).reshape(tokens)
     meta = jnp.stack(
-        [input_ids.astype(f32), true_ids.astype(f32), second.reshape(-1), token_weight, zero, zero, zero, zero]
+        [input_ids.astype(f32), true_ids.astype(f32), second.reshape(-1), token_weight, crop_share, zero, zero, zero]
     )
     cos_np, sin_np = rotary_constants(rows)
     cos_table, sin_table = jnp.asarray(cos_np), jnp.asarray(sin_np)
@@ -476,66 +681,77 @@
     )(q_ext, k_ext, v_ext)
     attended = attended.reshape(model, tokens)
 
-    shard = -(-(model + 128) // devices)
-    shard = -(-shard // 8) * 8
-    padded = shard * devices
-    dx1, do_ext, dw_pair, dw_rest, loss = pl.pallas_call(
+    half_rows = (model + 128) // 2
+    owned = -(-half_rows // (8 * columns * deep)) * 8
+    dx1, do_ext, keep_pair, send_pair, keep_rest, send_rest, loss = pl.pallas_call(
         middle_kernel,
         grid=(blocks,),
         in_specs=[by_block(8), by_block(model), by_block(model), whole((model, model)),
-                  pl.BlockSpec((None, columns, model, wide), lambda i: (0, 0, 0, 0), pipeline_mode=pl.Buffered(1)),
-                  pl.BlockSpec((None, columns, model, wide), lambda i: (1, 0, 0, 0), pipeline_mode=pl.Buffered(1)),
-                  whole((vocab, model)), whole(vectors.shape)],
-        out_specs=[by_block(model), heads_block(EXT), pl.BlockSpec(memory_space=pl.ANY), whole((model + 128, model)), whole((8, 128))],
-        out_shape=[shaped((model, tokens), f32), shaped((heads, EXT, tokens), bf16), shaped((2, columns, model, wide), bf16),
-                   shaped((model + 128, model), bf16), shaped((8, 128), f32)],
-        scratch_shapes=[pltpu.VMEM((columns, wide, model), bf16), pltpu.VMEM((columns, wide, model), bf16),
-                        pltpu.VMEM((columns, wide, block), bf16), pltpu.VMEM((columns, wide, block), bf16),
-                        pltpu.VMEM((columns, model, wide), f32), pltpu.VMEM((columns, model, wide), f32),
-                        pltpu.VMEM((model, model), f32), pltpu.VMEM((VPAD, model), f32), pltpu.VMEM((model, 128), f32),
+                  pl.BlockSpec(memory_space=pl.ANY), whole((vocab, model)), whole(vectors.shape)],
+        out_specs=[by_block(model), heads_block(EXT), pl.BlockSpec(memory_space=pl.ANY), pl.BlockSpec(memory_space=pl.ANY),
+                   whole((half_rows, model)), whole((half_rows, model)), whole((8, 128))],
+        out_shape=[shaped((model, tokens), f32), shaped((heads, EXT, tokens), bf16), shaped((columns * model, wide), bf16),
+                   shaped((columns * model, wide), bf16), shaped((half_rows, model), bf16), shaped((half_rows, model), bf16),
+                   shaped((8, 128), f32)],
+        scratch_shapes=[pltpu.VMEM((model, FF), bf16), pltpu.VMEM((model, FF), bf16), pltpu.VMEM((FF, model), bf16),
+                        pltpu.VMEM((FF, model), bf16), pltpu.VMEM((FF, block), bf16), pltpu.VMEM((FF, block), bf16),
+                        pltpu.VMEM((model, FF), f32), pltpu.VMEM((model, FF), f32),
+                        pltpu.VMEM((model + 128, model), f32), pltpu.VMEM((VPAD, model), f32), pltpu.VMEM((model, 128), f32),
                         pltpu.VMEM((model, 128), f32), pltpu.VMEM((128, model), f32),
                         pltpu.VMEM((VPAD, model), bf16), pltpu.VMEM((model, 128), bf16),
-                        pltpu.VMEM((model, model), bf16), pltpu.VMEM((model, model), bf16), pltpu.SemaphoreType.DMA((2,))],
+                        pltpu.VMEM((model, model), bf16), pltpu.VMEM((model, model), bf16), pltpu.SemaphoreType.DMA((2 + 2 * columns,))],
         compiler_params=limits(62),
         cost_estimate=cost(2 * tokens * model * (6 * FF + 3 * model), 14 * model * tokens + 16 * model * FF, FF * tokens),
         name="feedforward_and_head",
-    )(meta, x0, attended, outward, pair_all, pair_all, embedding, vectors)
+    )(meta, x0, attended, outward, pair_all, embedding, vectors)
+
+    count = columns * deep
 
     def swap(values, axes):
         return lax.all_to_all(values, axes, 0, 0, tiled=True)
 
+    def over_core(values):
+        return lax.ppermute(values, "core", [(0, 1), (1, 0)])
+
     def add_up(values, pieces):
         return jnp.sum(values.reshape((pieces, -1) + values.shape[1:]).astype(f32), axis=0)
 
+    def pair_sum(keep, sent):
+        return (keep.astype(f32) + sent.astype(f32)).astype(bf16)
+
     def pad_rows(values):
-        return jnp.pad(values, ((0, padded - values.shape[0]), (0, 0))) if padded > values.shape[0] else values
-
-    def reduce_core(values):
-        return add_up(swap(values, "core"), 2).astype(bf16)
-
-    def spread(values, axes, count):
-        return swap(jnp.broadcast_to(values[None], (count,) + values.shape).reshape((-1,) + values.shape[1:]), axes)
-
-    pair = dw_pair.reshape(2 * columns * model, wide)
-    pair = reduce_core(pair)
-    pair = add_up(swap(pair, "col"), columns).astype(bf16)
-    pair = add_up(swap(pair, "deep"), deep)
-    pair_grad = swap(pair, "core").reshape(feedforward.shape)
+        return jnp.pad(values, ((0, owned * count - half_rows), (0, 0)))
 
     def to_owner(values):
-        return add_up(swap(values, chips), columns * deep).astype(bf16)
-
-    def to_chips(values):
-        return spread(values, chips, columns * deep)
-
-    rest_mine = reduce_core(pad_rows(dw_rest))
-    rest_mine = to_chips(to_owner(rest_mine))
-
+        return swap(pad_rows(values), chips)
+
+    def gather4(values, axis):
+        one, two, three = (lax.ppermute(values, axis, [(i, i ^ d) for i in range(4)]) for d in (1, 2, 3))
+        index = lax.axis_index(axis)
+        odd, high = index % 2 == 1, index >= 2
+        near = jnp.where(odd, one, values), jnp.where(odd, values, one)
+        far = jnp.where(odd, three, two), jnp.where(odd, two, three)
+        return jnp.concatenate(
+            [jnp.where(high, far[i], near[i]) for i in range(2)] + [jnp.where(high, near[i], far[i]) for i in range(2)],
+            axis=0,
+        )
+
+    def gather_deep(values):
+        return gather4(values, "deep") if deep == 4 else lax.all_gather(values, "deep", axis=0, tiled=True)
+
+    def gather_col(values):
+        return (gather4(values, "col") if columns == 4 else lax.all_gather(values, "col", axis=0, tiled=True))[:half_rows]
+
+    def together(first, *others):
+        return lax.optimization_barrier((first, *others))
+
+    pair_sent, rest_sent = over_core(send_pair), over_core(send_rest)
     per_call = 4
     width = 3 * per_call * HEAD_DIM
     grads = None
-    in_parts = []
-    for first in range(0, heads // per_call):
+    keeps, sents = [], []
+    groups = heads // per_call
+    for first in range(groups):
         chained = grads is not None
 
         def group(count, first=first):
@@ -549,78 +765,135 @@
             + [pl.BlockSpec((model + 16, rows), lambda s: (0, s)), pl.BlockSpec((8, rows), lambda s: (0, s))]
             + [table_spec] * 4
             + [pl.BlockSpec(memory_space=pl.ANY)] * (3 if chained else 0),
-            out_specs=[group(HEAD_DIM)] * 3 + [pl.BlockSpec((model + 128, width), lambda s: (0, 0))],
-            out_shape=[shaped((heads, HEAD_DIM, tokens), bf16)] * 3 + [shaped((model + 128, width), bf16)],
-            scratch_shapes=[pltpu.VMEM((width, rows), bf16), pltpu.VMEM((model + 16, width), f32)],
+            out_specs=[group(HEAD_DIM)] * 3 + [pl.BlockSpec((half_rows, width), lambda s: (0, 0))] * 2,
+            out_shape=[shaped((heads, HEAD_DIM, tokens), bf16)] * 3 + [shaped((half_rows, width), bf16)] * 2,
+            scratch_shapes=[pltpu.VMEM((width, rows), bf16), pltpu.VMEM((2 * half_rows, width), f32)],
             input_output_aliases={10: 0, 11: 1, 12: 2} if chained else {},
             compiler_params=limits(56),
             cost_estimate=cost(2 * 40 * width // 3 * rows * tokens, 20 * width * tokens, per_call * rows * tokens),
             name="attention_back",
         )(q_next, k_ext, v_ext, do_ext, normed, meta, twice_cos, cos_table, twice_sin, sin_table, *(grads or ()))
         grads = outs[:3]
-        in_parts.append(pad_rows(outs[3]))
+        keeps.append(outs[3])
+        sents.append(over_core(outs[4]))
+        if first == 0:
+            pair = pair_sum(keep_pair.reshape(count, -1, wide), pair_sent.reshape(count, -1, wide))
+            rest_half = pad_rows(pair_sum(keep_rest, rest_sent)).reshape(count, owned, model)
+            pair = jnp.concatenate([pair, rest_half], axis=1).reshape(-1, wide)
+            do_ext, pair = together(do_ext, pair)
+            pair = lax.psum_scatter(pair, chips, scatter_dimension=0, tiled=True)
+        elif first == groups - 2:
+            early = jnp.concatenate([pair_sum(keeps[i], sents[i]) for i in range(groups - 2)], axis=1)
+            do_ext, early = together(do_ext, early)
+            early = to_owner(early)
+        elif first == groups - 1:
+            late_half = jnp.concatenate([pair_sum(keeps[i], sents[i]) for i in range(groups - 2, groups)], axis=1)
+            early = add_up(early, count).astype(bf16)
+            dx1, late_half, early = together(dx1, late_half, early)
+            late_half = to_owner(late_half)
+            early = gather_deep(early)
     dq, dk, dv = (grad.reshape(model, tokens) for grad in grads)
-    early = len(in_parts) - 2
-    in_mine = []
-    for parts in (in_parts[:early], in_parts[early:]):
-        merged = jnp.concatenate([reduce_core(part) for part in parts], axis=1)
-        in_mine.append(to_chips(to_owner(merged)))
-    in_mine = jnp.concatenate(in_mine, axis=1)
-
-    rest_start = pl.pallas_call(
-        input_back_kernel,
-        grid=(blocks,),
-        in_specs=[by_block(8)] + [by_block(model)] * 5 + [whole((model, 3 * model)), whole(vectors.shape)],
-        out_specs=whole((VPAD + 8, model)),
-        out_shape=shaped((VPAD + 8, model), f32),
-        scratch_shapes=[pltpu.VMEM((model, 3 * model), bf16), pltpu.VMEM((model, 128), f32), pltpu.VMEM((128, model), f32),
-                        pltpu.VMEM((model, 128), f32), pltpu.VMEM((VPAD, model), f32)],
+
+    back_out = [shaped((model, 128), f32), shaped((VPAD, model), f32)]
+    back_room = [pltpu.VMEM((model, 3 * model), bf16), pltpu.VMEM((model, 128), f32), pltpu.VMEM((128, model), f32)]
+
+    def input_back(part, extra):
+        def by_part(rows_):
+            return pl.BlockSpec((rows_, block), lambda i: (0, i + part * (blocks // 2)))
+
+        last = part == 1
+        room = [pltpu.VMEM(shape.shape, f32) for shape in back_out]
+        return pl.pallas_call(
+            functools.partial(input_back_kernel, last=last),
+            grid=(blocks // 2,),
+            in_specs=[by_part(8)] + [by_part(model)] * 5 + [whole((model, 3 * model)), whole(vectors.shape)]
+            + [whole(array.shape) for array in extra],
+            out_specs=[whole((TAIL, 2 * model + 128))] if last else [whole(shape.shape) for shape in back_out],
+            out_shape=[shaped((TAIL, 2 * model + 128), f32)] if last else back_out,
+            scratch_shapes=back_room + (room if last else []),
+            compiler_params=limits(56),
+            cost_estimate=cost(3 * model * model * tokens, 10 * model * tokens),
+            name="input_back",
+        )(meta, x0, dq, dk, dv, dx1, projection, vectors, *extra)
+
+    halfway = input_back(0, ())
+    dvec_half, dtable_half, early = together(*halfway, early)
+    early = gather_col(early)
+    (tail,) = input_back(1, (loss, dvec_half, dtable_half))
+    tail, pair, early, late_half = together(tail, pair, early, late_half)
+    early_other = over_core(early)
+
+    def call_small(kernel, args, outs, name):
+        return pl.pallas_call(
+            kernel,
+            in_specs=[pl.BlockSpec(memory_space=pltpu.VMEM)] * len(args),
+            out_specs=[pl.BlockSpec(memory_space=pltpu.VMEM)] * len(outs),
+            out_shape=[shaped(shape, bf16) for shape in outs],
+            compiler_params=limits(40),
+            cost_estimate=cost(1e6, 4e6),
+            name=name,
+        )(*args)
+
+    own = (pair.shape[0] - owned) // 2
+    last_width = late_half.shape[1] + model
+    if columns == 4 and deep == 4 and owned == TAIL and last_width == tail.shape[1]:
+        packed, pair_keep, pair_sent = call_small(
+            functools.partial(pack_kernel, pieces=count), (late_half, pair, tail),
+            [(owned + TAIL, last_width), (own, wide), (own, wide)], "pack",
+        )
+        pair_sent = over_core(pair_sent)
+        for axis in ("deep", "col"):
+            got = [lax.ppermute(packed, axis, [(i, i ^ d) for i in range(4)]) for d in (1, 2, 3)]
+            merged = 4 * (packed.shape[0] - TAIL) + TAIL
+            (packed,) = call_small(functools.partial(stage_kernel, axis=axis), (packed, *got), [(merged, last_width)], "stage")
+    else:
+        is_first = lax.axis_index("core") == 0
+        pair_keep = jnp.where(is_first, pair[:own], pair[own : 2 * own])
+        pair_sent = over_core(jnp.where(is_first, pair[own : 2 * own], pair[:own]))
+        square = jnp.sum(jnp.square(pair[: 2 * own].astype(f32)))
+        tail = lax.psum(tail.at[0, 2 * model + 2].add(square), chips)
+        scalars = tail[0:1, 2 * model :]
+        high = lax.reduce_precision(scalars, 8, 7)
+        middle = lax.reduce_precision(scalars - high, 8, 7)
+        numbers = jnp.concatenate([high, middle, scalars - high - middle, jnp.zeros((TAIL - 3, 128), f32)], axis=0)
+        tail = jnp.pad(jnp.concatenate([tail[:, : 2 * model], numbers], axis=1), ((0, 0), (0, last_width - tail.shape[1])))
+        packed = jnp.concatenate([add_up(late_half, count).astype(bf16), pair[2 * own :]], axis=1)
+        packed = jnp.concatenate([gather_col(gather_deep(packed)), tail.astype(bf16)], axis=0)
+    packed_other = over_core(packed)
+
+    steps = 10
+    state = (
+        (embedding, embedding_drift, embedding_spread),
+        (projection, projection_drift, projection_spread),
+        (outward, outward_drift, outward_spread),
+        (feedforward, feedforward_drift, feedforward_spread),
+        (vectors, vectors_drift, vectors_spread),
+    )
+
+    def state_spec(array):
+        if array.shape[0] == model:
+            return pl.BlockSpec((model // steps, array.shape[1]), lambda i: (i, 0))
+        return whole(array.shape)
+
+    grads_in = (early, early_other, packed, packed_other, pair_keep, pair_sent)
+    results = pl.pallas_call(
+        functools.partial(update_kernel, groups=groups, early_groups=groups - 2),
+        grid=(steps,),
+        in_specs=[whole(array.shape) for array in grads_in] + [
+            pl.BlockSpec(memory_space=pl.ANY) if array.shape[0] == model else whole(array.shape) for three in state for array in three
+        ],
+        out_specs=[state_spec(three[0]) for three in state for _ in range(4)]
+        + [pl.BlockSpec(memory_space=pltpu.SMEM)] * 2,
+        out_shape=[shaped(three[0].shape, dtype) for three in state for dtype in (f32, f32, f32, bf16)]
+        + [shaped((2,), f32), shaped((1,), f32)],
+        scratch_shapes=[pltpu.VMEM((model, 3 * model), f32), pltpu.VMEM((model, model), f32), pltpu.VMEM((VOCAB_ROWS, model), f32),
+                        pltpu.VMEM((16, model), f32), pltpu.VMEM((8, 128), f32), pltpu.SemaphoreType.DMA((6, steps))]
+        + [pltpu.VMEM(array.shape, f32) for three in state[1:3] for array in three],
         compiler_params=limits(56),
-        cost_estimate=cost(2 * 3 * model * model * tokens, 20 * model * tokens),
-        name="input_back",
-    )(meta, x0, dq, dk, dv, dx1, projection, vectors)
-
-    scalars = jnp.stack([loss[0, 0], jnp.sum(1 + splits).astype(f32), jnp.sum(pair_grad * pair_grad)])
-    late = jnp.concatenate([rest_start, jnp.pad(scalars[None], ((0, 7), (0, model - 3)))], axis=0)
-    size = 1
-    while size < devices:
-        late = late + lax.ppermute(late, everywhere, [(i, i ^ size) for i in range(devices)])
-        size *= 2
-    loss_total, crops, ffn_total = late[VPAD + 8, 0], late[VPAD + 8, 1], late[VPAD + 8, 2]
-
-    full = spread(jnp.concatenate([in_mine, rest_mine], axis=1), "core", 2).astype(f32)
-    groups = heads // per_call
-    piece = per_call * HEAD_DIM
-    in_full = jnp.concatenate(
-        [full[: model + 8, g * width + part * piece : g * width + (part + 1) * piece] for part in range(3) for g in range(groups)],
-        axis=1,
-    )
-    rest_full = full[: model + 128, groups * width :]
-    in_grad = in_full[:model]
-    out_grad = rest_full[:model]
-    table_grad = rest_full[model + REST_TABLE : model + REST_TABLE + vocab] + late[:vocab]
-    vector_grad = jnp.concatenate(
-        [late[VPAD : VPAD + 2], in_full[model].reshape(3, model), rest_full[model : model + 6 + bias_rows]], axis=0
-    )
-    rep_grads = (table_grad, in_grad, out_grad, vector_grad)
-    squares = ffn_total
-    for grad in rep_grads:
-        squares = squares + jnp.sum(grad * grad)
-    share = 1.0 / crops
-    grad_norm = jnp.sqrt(squares) * share
-    factor = jnp.minimum(1.0, CLIP_NORM / (grad_norm + 1e-06)) * share
-    replicated = (embedding, projection, outward, vectors)
-    drifts = (embedding_drift, projection_drift, outward_drift, vectors_drift)
-    spreads = (embedding_spread, projection_spread, outward_spread, vectors_spread)
-    rep_out = [
-        adam_step(weight, grad * factor, drift, spread, rate)
-        for weight, grad, drift, spread, rate in zip(replicated, rep_grads, drifts, spreads, (0.05, 0.05, 0.1, 0.2))
-    ]
-    ffn_out = adam_step(feedforward, pair_grad * factor, feedforward_drift, feedforward_spread, 0.05)
-    results = [jnp.stack([loss_total, crops]), grad_norm]
-    for fresh, moved, varied in (rep_out[0], rep_out[1], rep_out[2], ffn_out, rep_out[3]):
-        results.extend([fresh, moved, varied, fresh.astype(bf16)])
-    return tuple(results)
+        cost_estimate=cost(60 * 4 * model * model, 4 * 30 * model * model),
+        name="clip_and_adamw",
+    )(*grads_in, *(array for three in state for array in three))
+    return (results[20], results[21].reshape(()), *results[:20])
 
 
 def solution(mesh):

time: 628 us -> 424 us (0.68)
  waiting for transfers between devices: 140 us -> 39.9 us
  other arithmetic: 58.5 us -> 13.1 us
  blocking collectives: 35.3 us -> 0 us
  Pallas kernels: 294 us -> 315 us
  local copies, waits for them, and re-layouts: 23.9 us -> 4.41 us
  starting transfers between devices: 47.5 us -> 30.9 us
    all_to_all x10 -> x2, waiting for transfers between devices: 127 us -> 10.5 us  [swap(): return lax.all_to_all(values, axes, 0, 0, tiled=True)]
    all_to_all x7 -> x0, blocking collectives: 35.3 us -> none  [swap(): return lax.all_to_all(values, axes, 0, 0, tiled=True)]
    all_to_all x10 -> x2, starting transfers between devices: 44.7 us -> 12.3 us  [swap(): return lax.all_to_all(values, axes, 0, 0, tiled=True)]
    pallas_call x1 -> x6, Pallas kernels: 17.7 us -> 43.6 us  [the longest x2 23.3 us: input_back(): pl.pallas_call(functools.partial(input_back_kernel, last=last), grid=(blo...]
    convert_element_type x6 -> x7, other arithmetic: 23.9 us -> 3.24 us  [pair_sum(): return (keep.astype(f32) + sent.astype(f32)).astype(bf16)]
    ppermute x5 -> x22, waiting for transfers between devices: 13.5 us -> 29.4 us  [the longest x6 22.8 us: body(): lax.ppermute(packed, axis, [(i, i ^ d) for i in range(4)])]
    ppermute x5 -> x22, starting transfers between devices: 2.77 us -> 18.6 us  [the longest x6 8 us: gather4(): lax.ppermute(values, axis, [(i, i ^ d) for i in range(4)])]
    reduce_sum x12 -> x1, other arithmetic: 12.7 us -> 0.12 us  [add_up(): jnp.sum(values.reshape((pieces, -1) + values.shape[1:]).astype(f32), axis=0)]
  transfers between devices with their start and end apart: 16 -> 26, of which waited for: 13 -> 8; matrix products, arithmetic and copies ran while one was open for 8% -> 2% of each run, Pallas kernels for 34% -> 50%
where the time goes in v2:
time: 424 us; the launch traced here: 418 us
  Pallas kernels  315 us (74%)
  waiting for transfers between devices  39.9 us (9%)
  starting transfers between devices  30.9 us (7%)
  between operations  14.9 us (4%)
  other arithmetic  13.1 us (3%)
  local copies, waits for them, and re-layouts  4.41 us (1%)
    pallas_call x5, Pallas kernels, body(): pl.pallas_call(functools.partial(attention_back_kernel, chunk=half, chain...  113 us
    pallas_call x1, Pallas kernels, body(): pl.pallas_call(middle_kernel, grid=(blocks,), in_specs=[by_block(8), by_b...  85.8 us
    pallas_call x1, Pallas kernels, body(): pl.pallas_call(attention_kernel, grid=(slots, heads // per), in_specs=[he...  55.9 us
    pallas_call x2, Pallas kernels, input_back(): pl.pallas_call(functools.partial(input_back_kernel, last=last), grid=(blo...  23.3 us
    ppermute x6, waiting for transfers between devices, body(): lax.ppermute(packed, axis, [(i, i ^ d) for i in range(4)])  22.8 us
    pallas_call x1, Pallas kernels, body(): pl.pallas_call(functools.partial(update_kernel, groups=groups, early_grou...  19.4 us
    pallas_call x1, Pallas kernels, body(): pl.pallas_call(qkv_kernel, grid=(blocks,), in_specs=[by_block(8), whole((...  15.8 us
    all_to_all x2, starting transfers between devices, swap(): return lax.all_to_all(values, axes, 0, 0, tiled=True)  12.3 us
  transfers between devices with their start and end apart: 26, of which 8 were waited for; matrix products, arithmetic and copies ran while one was open for 2% of the time, Pallas kernels for 50%

profile of v2, /device:TPU:0, one launch (start us, length us, event | category | flops | bytes accessed | tf_op | source)
XLA Modules:
  0.0 417.8 jit_solution(12008546663411373106)
XLA Ops:
  7.2 1.7 convert_element_type.118
  9.0 0.7 convert_bitcast_fusion
  9.8 0.7 convert_multiply_fusion
  10.5 0.8 fusion.2
  11.4 0.7 convert_compare_fusion
  12.3 0.7 convert_divide_fusion
  13.0 0.7 stack.15.meta
  13.7 15.8 %embed_and_qkv.1 = (f32[640,2048]{1,0:T(8,128)}, bf16[656,2048]{1,0:T(8,128)(2,1)}, bf16[20,48,2048]{2,1,0:T(8,128)(2,1)}, bf16[20,48,2048]{2,1,0:T(8,128)(2,1)}, bf16[20,48,2048]{2,1,0:T(8,128)(2,1)}) custom-call(f32[8,2048]{1,0:T(8,128)} %stack.15.meta, f32[33,640]{1,0:T(8,128)} %refs_6_.1, f32[640,1920]{1,0:T(8,128)} %refs_9_.1, f32[15,640]{1,0:T(8,128)} %refs_18_.1, ...), custom_call_target="tpu_custom_call" | custom-call | flops 5033164800 | bytes 26214400 | tf_op jit(solution)/shard_map/embed_and_qkv/pallas_call | solution.py:652
  29.5 55.9 %attention.1 = (bf16[20,32,2048]{2,1,0:T(8,128)(2,1)}, bf16[20,48,2048]{2,1,0:T(8,128)(2,1)}) custom-call(bf16[20,48,2048]{2,1,0:T(8,128)(2,1)} %get-tuple-element.103.q_ext, bf16[20,48,2048]{2,1,0:T(8,128)(2,1)} %get-tuple-element.104.k_ext, bf16[20,48,2048]{2,1,0:T(8,128)(2,1)} %get-tuple-element.105.v_ext), custom_call_target="tpu_custom_call" | custom-call | flops 42949672960 | bytes 15728640 | tf_op jit(solution)/shard_map/attention/pallas_call | solution.py:672
  85.4 85.8 %feedforward_and_head.1 = (f32[640,2048]{1,0:T(8,128)}, bf16[20,48,2048]{2,1,0:T(8,128)(2,1)}, bf16[2560,640]{1,0:T(8,128)(2,1)}, bf16[2560,640]{1,0:T(8,128)(2,...) custom-call(f32[8,2048]{1,0:T(8,128)} %stack.15.meta, ...), custom_call_target="tpu_custom_call" | custom-call | flops 45298483200 | bytes 44564480 | tf_op jit(solution)/shard_map/feedforward_and_head/pallas_call | solution.py:686
  171.2 0.5 collective-permute-start
  171.8 22.6 %attention_back.5 = (bf16[20,32,2048]{2,1,0:T(8,128)(2,1)}, bf16[20,32,2048]{2,1,0:T(8,128)(2,1)}, bf16[20,32,2048]{2,1,0:T(8,128)(2,1)}, bf16[384,384]{1,0:T(8,128)(2,1)}, bf16[384,384]{1,0:T(8,128)(2,1)}) custom-call(bf16[20,48,2048]{2,1,0:T(8,128)(2,1)} %get-tuple-element.106.q_ext, bf16[20,48,2048]{2,1,0:T(8,128)(2,1)} %get-tuple-element.104.k_ext, ...), custom_call_target="tpu_custom_call" | custom-call | flops 21474836480 | bytes 15728640 | tf_op jit(solution)/shard_map/attention_back/pallas_call | solution.py:761
  194.9 1.3 collective-permute-done.2
  196.2 1.0 add_convert_fusion.6
  197.4 0.8 add_convert_fusion
  198.3 2.2 pad_maximum_fusion
  200.5 22.7 %attention_back.6 = (bf16[20,32,2048]{2,1,0:T(8,128)(2,1)}, bf16[20,32,2048]{2,1,0:T(8,128)(2,1)}, bf16[20,32,2048]{2,1,0:T(8,128)(2,1)}, bf16[384,384]{1,0:T(8,128)(2,1)}, bf16[384,384]{1,0:T(8,128)(2,1)}) custom-call(bf16[20,48,2048]{2,1,0:T(8,128)(2,1)} %get-tuple-element.106.q_ext, ...), custom_call_target="tpu_custom_call", output_to_operand_aliasing={{0}: (10, {}), {1}: (11, {}), {2}: (12, {})} | custom-call | flops 21474836480 | bytes 15728640 | tf_op jit(solution)/shard_map/attention_back/pallas_call | solution.py:761
  223.4 22.9 %attention_back.7 = (bf16[20,32,2048]{2,1,0:T(8,128)(2,1)}, bf16[20,32,2048]{2,1,0:T(8,128)(2,1)}, bf16[20,32,2048]{2,1,0:T(8,128)(2,1)}, bf16[384,384]{1,0:T(8,128)(2,1)}, bf16[384,384]{1,0:T(8,128)(2,1)}) custom-call(bf16[20,48,2048]{2,1,0:T(8,128)(2,1)} %get-tuple-element.106.q_ext, ...), custom_call_target="tpu_custom_call", output_to_operand_aliasing={{0}: (10, {}), {1}: (11, {}), {2}: (12, {})} | custom-call | flops 21474836480 | bytes 15728640 | tf_op jit(solution)/shard_map/attention_back/pallas_call | solution.py:761
  246.7 22.7 %attention_back.8 = (bf16[20,32,2048]{2,1,0:T(8,128)(2,1)}, bf16[20,32,2048]{2,1,0:T(8,128)(2,1)}, bf16[20,32,2048]{2,1,0:T(8,128)(2,1)}, bf16[384,384]{1,0:T(8,128)(2,1)}, bf16[384,384]{1,0:T(8,128)(2,1)}) custom-call(bf16[20,48,2048]{2,1,0:T(8,128)(2,1)} %get-tuple-element.106.q_ext, ...), custom_call_target="tpu_custom_call", output_to_operand_aliasing={{0}: (10, {}), {1}: (11, {}), {2}: (12, {})} | custom-call | flops 21474836480 | bytes 15728640 | tf_op jit(solution)/shard_map/attention_back/pallas_call | solution.py:761
  269.8 1.0 pad_maximum_fusion.1
  270.8 8.4 %all-to-all-start = ((bf16[16,24,1152]{2,1,0:T(8,128)(2,1)}), bf16[16,24,1152]{2,1,0:T(8,128)(2,1)S(1)}, u32[]{:S(2)}, u32[]{:S(2)}) async-start(bf16[16,24,1152]{2,1,0:T(8,128)(2,1)} %bitcast.11), calls=%async_computation | async-start | bytes 1769472 | tf_op jit(solution)/shard_map/all_to_all | solution.py:711
  279.3 22.5 %attention_back.9 = (bf16[20,32,2048]{2,1,0:T(8,128)(2,1)}, bf16[20,32,2048]{2,1,0:T(8,128)(2,1)}, bf16[20,32,2048]{2,1,0:T(8,128)(2,1)}, bf16[384,384]{1,0:T(8,128)(2,1)}, bf16[384,384]{1,0:T(8,128)(2,1)}) custom-call(bf16[20,48,2048]{2,1,0:T(8,128)(2,1)} %get-tuple-element.106.q_ext, ...), custom_call_target="tpu_custom_call", output_to_operand_aliasing={{0}: (10, {}), {1}: (11, {}), {2}: (12, {})} | custom-call | flops 21474836480 | bytes 15728640 | tf_op jit(solution)/shard_map/attention_back/pallas_call | solution.py:761
  302.0 1.7 collective-permute-done.6
  303.7 1.0 add_convert_fusion.2
  304.7 0.9 pad_maximum_fusion.3
  305.6 10.5 %all-to-all-done = bf16[16,24,1152]{2,1,0:T(8,128)(2,1)S(1)} async-done(((bf16[16,24,1152]{2,1,0:T(8,128)(2,1)}), bf16[16,24,1152]{2,1,0:T(8,128)(2,1)S(1)}, u32[]{:S(2)}, u32[]{:S(2)}) %all-to-all-start) | async-done | bytes 884768 | tf_op jit(solution)/shard_map/all_to_all | solution.py:711
  316.2 0.6 collective-permute-start.8
  316.8 3.8 collective-permute-start.7
  320.6 3.8 all-to-all-start.1
  324.4 11.6 %input_back.2 = (f32[640,128]{1,0:T(8,128)}, f32[48,640]{1,0:T(8,128)}) custom-call(f32[8,2048]{1,0:T(8,128)} %stack.15.meta, f32[640,2048]{1,0:T(8,128)} %get-tuple-element.102.x0, bf16[640,2048]{1,0:T(8,128)(2,1)} %bitcast.30, bf16[640,2048]{1,0:T(8,128)(2,1)} %bitcast.32, bf16[640,2048]{1,0:T(8,128)(2,1)} %bitcast.34, ...), custom_call_target="tpu_custom_call" | custom-call | flops 2516582400 | bytes 13107200 | tf_op jit(solution)/shard_map/input_back/pallas_call | solution.py:806
  336.1 2.0 collective-permute-start.12
  338.1 1.5 collective-permute-start.11
  339.6 11.8 %input_back.3.tail = f32[24,1408]{1,0:T(8,128)} custom-call(f32[8,2048]{1,0:T(8,128)} %stack.15.meta, f32[640,2048]{1,0:T(8,128)} %get-tuple-element.102.x0, bf16[640,2048]{1,0:T(8,128)(2,1)} %bitcast.31, bf16[640,2048]{1,0:T(8,128)(2,1)} %bitcast.33, bf16[640,2048]{1,0:T(8,128)(2,1)} %bitcast.35, f32[640,2048]{1,0:T(8,128)} %get-tuple-element.143.dx1, ...), custom_call_target="tpu_custom_call" | custom-call | flops 2516582400 | bytes 13107200 | tf_op jit(solution)/shard_map/input_back/pallas_call | solution.py:806
  351.7 0.6 copy-done.1
  352.3 0.9 copy-done.2
  353.5 0.6 copy-done.3
  354.1 3.7 collective-permute-start.16
  357.8 0.7 collective-permute-start.14
  358.5 3.6 collective-permute-done.16.three
  362.1 5.5 %collective-permute-done.15.two = bf16[48,1408]{1,0:T(8,128)(2,1)S(1)} collective-permute-done((bf16[48,1408]{1,0:T(8,128)(2,1)S(1)}, bf16[48,1408]{1,0:T(8,128)(2,1)S(1)}, u32[]{:S(2)}, u32[]{:S(2)}) %collective-permute-start.15) | collective-permute-done | bytes 135200 | tf_op jit(solution)/shard_map/ppermute | solution.py:846
  367.7 2.5 collective-permute-start.19
  370.2 0.5 collective-permute-start.18
  370.7 0.5 collective-permute-start.17
  371.3 8.3 %collective-permute-done.19.three = bf16[120,1408]{1,0:T(8,128)(2,1)S(1)} collective-permute-done((bf16[120,1408]{1,0:T(8,128)(2,1)S(1)}, bf16[120,1408]{1,0:T(8,128)(2,1)S(1)}, u32[]{:S(2)}, u32[]{:S(2)}) %collective-permute-start.19) | collective-permute-done | bytes 337952 | tf_op jit(solution)/shard_map/ppermute | solution.py:846
  379.6 5.4 %collective-permute-done.18.two = bf16[120,1408]{1,0:T(8,128)(2,1)S(1)} collective-permute-done((bf16[120,1408]{1,0:T(8,128)(2,1)S(1)}, bf16[120,1408]{1,0:T(8,128)(2,1)S(1)}, u32[]{:S(2)}, u32[]{:S(2)}) %collective-permute-start.18) | collective-permute-done | bytes 337952 | tf_op jit(solution)/shard_map/ppermute | solution.py:846
  386.1 3.6 collective-permute-done.21.refs_5_
  389.8 0.6 copy-done.12
  391.1 19.4 %clip_and_adamw.1 = (f32[33,640]{1,0:T(8,128)}, f32[33,640]{1,0:T(8,128)}, f32[33,640]{1,0:T(8,128)}, bf16[33,640]{1,0:T(8,128)(2,1)}, f32[640,1920]{1,0:T(8,128...) custom-call(bf16[384,1152]{1,0:T(8,128)(2,1)} %copy-done.4, ...), custom_call_target="tpu_custom_call" | custom-call | flops 98304000 | bytes 49152000 | tf_op jit(solution)/shard_map/clip_and_adamw/pallas_call | solution.py:879
  (81 shorter events, 5.1 us)
Async XLA Ops:
  7.2 78.3 %all-gather.2.cloned.1.call-start = ((), (), s32[]{:S(2)}) async-start(), calls=%async_computation.3 | async-start | bytes 6758400 | tf_op jit(solution)/shard_map/all_gather | solution.py:622
  9.0 342.7 %reduce-scatter.5.cloned.1.call-start = ((), (), s32[]{:S(2)}) async-start(), calls=%async_computation.4 | async-start | bytes 4003840
  171.2 26.2 %collective-permute-start = (bf16[2560,640]{1,0:T(8,128)(2,1)}, bf16[2560,640]{1,0:T(8,128)(2,1)S(1)}, u32[]{:S(2)}, u32[]{:S(2)}) collective-permute-start(bf16[2560,640]{1,0:T(8,128)(2,1)} %get-tuple-element.110), channel_id=1, source_target_pairs={{0,1},{1,0},{2,3},{3,2},{4,5},{5,4},{6,7},{7,6},{8,9},{9,8},{10,11... | collective-permute-start | bytes 9830408 | tf_op jit(solution)/shard_map/ppermute | solution.py:714
  171.7 22.8 %copy-start.13 = (bf16[384,640]{1,0:T(8,128)(2,1)S(1)}, bf16[384,640]{1,0:T(8,128)(2,1)}, u32[]{:S(2)}) copy-start(bf16[384,640]{1,0:T(8,128)(2,1)} %get-tuple-element.112) | copy-start | bytes 1474564
  171.7 25.5 %copy-start.8 = (bf16[384,640]{1,0:T(8,128)(2,1)S(1)}, bf16[384,640]{1,0:T(8,128)(2,1)}, u32[]{:S(2)}) copy-start(bf16[384,640]{1,0:T(8,128)(2,1)} %get-tuple-element.111) | copy-start | bytes 1474564
  171.7 25.7 %copy-start.5 = (bf16[2560,640]{1,0:T(8,128)(2,1)S(1)}, bf16[2560,640]{1,0:T(8,128)(2,1)}, u32[]{:S(2)}) copy-start(bf16[2560,640]{1,0:T(8,128)(2,1)} %get-tuple-element.109) | copy-start | bytes 9830404
  194.4 1.9 collective-permute-start.2
  194.5 2.8 collective-permute-start.1
  223.2 46.5 %collective-permute-start.3 = (bf16[384,384]{1,0:T(8,128)(2,1)}, bf16[384,384]{1,0:T(8,128)(2,1)S(1)}, u32[]{:S(2)}, u32[]{:S(2)}) collective-permute-start(bf16[384,384]{1,0:T(8,128)(2,1)} %get-tuple-element.121), channel_id=1, source_target_pairs={{0,1},{1,0},{2,3},{3,2},{4,5},{5,4},{6,7},{7,6},{8,9},{9,8},{10,11... | collective-permute-start | bytes 884744 | tf_op jit(solution)/shard_map/ppermute | solution.py:714
  246.3 23.4 %collective-permute-start.4 = (bf16[384,384]{1,0:T(8,128)(2,1)}, bf16[384,384]{1,0:T(8,128)(2,1)S(1)}, u32[]{:S(2)}, u32[]{:S(2)}) collective-permute-start(bf16[384,384]{1,0:T(8,128)(2,1)} %get-tuple-element.126), channel_id=1, source_target_pairs={{0,1},{1,0},{2,3},{3,2},{4,5},{5,4},{6,7},{7,6},{8,9},{9,8},{10,11... | collective-permute-start | bytes 884744 | tf_op jit(solution)/shard_map/ppermute | solution.py:714
  246.7 22.9 %copy-start.10 = (bf16[384,384]{1,0:T(8,128)(2,1)S(1)}, bf16[384,384]{1,0:T(8,128)(2,1)}, u32[]{:S(2)}) copy-start(bf16[384,384]{1,0:T(8,128)(2,1)} %get-tuple-element.120) | copy-start | bytes 884740
  246.7 23.0 %copy-start.11 = (bf16[384,384]{1,0:T(8,128)(2,1)S(1)}, bf16[384,384]{1,0:T(8,128)(2,1)}, u32[]{:S(2)}) copy-start(bf16[384,384]{1,0:T(8,128)(2,1)} %get-tuple-element.125) | copy-start | bytes 884740
  269.4 32.5 %collective-permute-start.5 = (bf16[384,384]{1,0:T(8,128)(2,1)}, bf16[384,384]{1,0:T(8,128)(2,1)S(1)}, u32[]{:S(2)}, u32[]{:S(2)}) collective-permute-start(bf16[384,384]{1,0:T(8,128)(2,1)} %get-tuple-element.139), channel_id=1, source_target_pairs={{0,1},{1,0},{2,3},{3,2},{4,5},{5,4},{6,7},{7,6},{8,9},{9,8},{10,11... | collective-permute-start | bytes 884744 | tf_op jit(solution)/shard_map/ppermute | solution.py:714
  270.8 45.2 %all-to-all-start = ((bf16[16,24,1152]{2,1,0:T(8,128)(2,1)}), bf16[16,24,1152]{2,1,0:T(8,128)(2,1)S(1)}, u32[]{:S(2)}, u32[]{:S(2)}) async-start(bf16[16,24,1152]{2,1,0:T(8,128)(2,1)} %bitcast.11), calls=%async_computation | async-start | bytes 1769472 | tf_op jit(solution)/shard_map/all_to_all | solution.py:711
  279.2 22.7 %copy-start.9 = (bf16[384,384]{1,0:T(8,128)(2,1)S(1)}, bf16[384,384]{1,0:T(8,128)(2,1)}, u32[]{:S(2)}) copy-start(bf16[384,384]{1,0:T(8,128)(2,1)} %get-tuple-element.138) | copy-start | bytes 884740
  301.8 1.9 collective-permute-start.6
  316.1 19.9 %collective-permute-start.9 = (bf16[24,1152]{1,0:T(8,128)(2,1)S(1)}, bf16[24,1152]{1,0:T(8,128)(2,1)S(1)}, u32[]{:S(2)}, u32[]{:S(2)}) collective-permute-start(bf16[24,1152]{1,0:T(8,128)(2,1)S(1)} %reduce_sum.32), channel_id=1, source_target_pairs={{0,2},{2,0},{4,6},{6,4},{1,3},{3,1},{5,7},{7,5},{8,10},{10,8},{12,... | collective-permute-start | bytes 165896 | tf_op jit(solution)/shard_map/ppermute | solution.py:729
  316.2 19.8 %collective-permute-start.8 = (bf16[24,1152]{1,0:T(8,128)(2,1)S(1)}, bf16[24,1152]{1,0:T(8,128)(2,1)S(1)}, u32[]{:S(2)}, u32[]{:S(2)}) collective-permute-start(bf16[24,1152]{1,0:T(8,128)(2,1)S(1)} %reduce_sum.32), channel_id=1, source_target_pairs={{0,4},{2,6},{4,0},{6,2},{1,5},{3,7},{5,1},{7,3},{8,12},{10,14},{12... | collective-permute-start | bytes 165896 | tf_op jit(solution)/shard_map/ppermute | solution.py:729
  316.8 19.2 %collective-permute-start.7 = (bf16[24,1152]{1,0:T(8,128)(2,1)S(1)}, bf16[24,1152]{1,0:T(8,128)(2,1)S(1)}, u32[]{:S(2)}, u32[]{:S(2)}) collective-permute-start(bf16[24,1152]{1,0:T(8,128)(2,1)S(1)} %reduce_sum.32), channel_id=1, source_target_pairs={{0,6},{2,4},{4,2},{6,0},{1,7},{3,5},{5,3},{7,1},{8,14},{10,12},{12... | collective-permute-start | bytes 165896 | tf_op jit(solution)/shard_map/ppermute | solution.py:729
  320.6 31.1 %all-to-all-start.1 = ((bf16[16,24,768]{2,1,0:T(8,128)(2,1)}), bf16[16,24,768]{2,1,0:T(8,128)(2,1)S(1)}, u32[]{:S(2)}, u32[]{:S(2)}) async-start(bf16[16,24,768]{2,1,0:T(8,128)(2,1)} %bitcast.13), calls=%async_computation.1 | async-start | bytes 1179648 | tf_op jit(solution)/shard_map/all_to_all | solution.py:711
  336.1 15.3 %collective-permute-start.12 = (bf16[96,1152]{1,0:T(8,128)(2,1)S(1)}, bf16[96,1152]{1,0:T(8,128)(2,1)S(1)}, u32[]{:S(2)}, u32[]{:S(2)}) collective-permute-start(bf16[96,1152]{1,0:T(8,128)(2,1)S(1)} %pad_maximum_fusion.4), channel_id=1, source_target_pairs={{0,8},{8,0},{16,24},{24,16},{1,9},{9,1},{17,25},{25,17},{2,10},{10... | collective-permute-start | bytes 663560 | tf_op jit(solution)/shard_map/ppermute | solution.py:729
  338.1 13.3 %collective-permute-start.11 = (bf16[96,1152]{1,0:T(8,128)(2,1)S(1)}, bf16[96,1152]{1,0:T(8,128)(2,1)S(1)}, u32[]{:S(2)}, u32[]{:S(2)}) collective-permute-start(bf16[96,1152]{1,0:T(8,128)(2,1)S(1)} %pad_maximum_fusion.4), channel_id=1, source_target_pairs={{0,16},{8,24},{16,0},{24,8},{1,17},{9,25},{17,1},{25,9},{2,18},{10... | collective-permute-start | bytes 663560 | tf_op jit(solution)/shard_map/ppermute | solution.py:729
  339.6 11.8 %collective-permute-start.10 = (bf16[96,1152]{1,0:T(8,128)(2,1)S(1)}, bf16[96,1152]{1,0:T(8,128)(2,1)S(1)}, u32[]{:S(2)}, u32[]{:S(2)}) collective-permute-start(bf16[96,1152]{1,0:T(8,128)(2,1)S(1)} %pad_maximum_fusion.4), channel_id=1, source_target_pairs={{0,24},{8,16},{16,8},{24,0},{1,25},{9,17},{17,9},{25,1},{2,26},{10... | collective-permute-start | bytes 663560 | tf_op jit(solution)/shard_map/ppermute | solution.py:729
  351.4 0.9 copy-start.1
  351.6 38.1 %copy-start.4 = (bf16[384,1152]{1,0:T(8,128)(2,1)}, bf16[384,1152]{1,0:T(8,128)(2,1)S(1)}, u32[]{:S(2)}) copy-start(bf16[384,1152]{1,0:T(8,128)(2,1)S(1)} %pad_maximum_fusion.2.refs_0_) | copy-start | bytes 2654212
  352.3 0.9 copy-start.2
  353.4 0.6 copy-start.3
  354.1 8.0 %collective-permute-start.16 = (bf16[48,1408]{1,0:T(8,128)(2,1)S(1)}, bf16[48,1408]{1,0:T(8,128)(2,1)S(1)}, u32[]{:S(2)}, u32[]{:S(2)}) collective-permute-start(bf16[48,1408]{1,0:T(8,128)(2,1)S(1)} %get-tuple-element.157.own), channel_id=1, source_target_pairs={{0,6},{2,4},{4,2},{6,0},{1,7},{3,5},{5,3},{7,1},{8,14},{10,12},{12... | collective-permute-start | bytes 405512 | tf_op jit(solution)/shard_map/ppermute | solution.py:846
  357.8 9.8 %collective-permute-start.15 = (bf16[48,1408]{1,0:T(8,128)(2,1)S(1)}, bf16[48,1408]{1,0:T(8,128)(2,1)S(1)}, u32[]{:S(2)}, u32[]{:S(2)}) collective-permute-start(bf16[48,1408]{1,0:T(8,128)(2,1)S(1)} %get-tuple-element.157.own), channel_id=1, source_target_pairs={{0,4},{2,6},{4,0},{6,2},{1,5},{3,7},{5,1},{7,3},{8,12},{10,14},{12... | collective-permute-start | bytes 405512 | tf_op jit(solution)/shard_map/ppermute | solution.py:846
  357.8 9.8 %collective-permute-start.14 = (bf16[48,1408]{1,0:T(8,128)(2,1)S(1)}, bf16[48,1408]{1,0:T(8,128)(2,1)S(1)}, u32[]{:S(2)}, u32[]{:S(2)}) collective-permute-start(bf16[48,1408]{1,0:T(8,128)(2,1)S(1)} %get-tuple-element.157.own), channel_id=1, source_target_pairs={{0,2},{2,0},{4,6},{6,4},{1,3},{3,1},{5,7},{7,5},{8,10},{10,8},{12,... | collective-permute-start | bytes 405512 | tf_op jit(solution)/shard_map/ppermute | solution.py:846
  367.7 11.9 %collective-permute-start.19 = (bf16[120,1408]{1,0:T(8,128)(2,1)S(1)}, bf16[120,1408]{1,0:T(8,128)(2,1)S(1)}, u32[]{:S(2)}, u32[]{:S(2)}) collective-permute-start(bf16[120,1408]{1,0:T(8,128)(2,1)S(1)} %stage.2.own), channel_id=1, source_target_pairs={{0,24},{8,16},{16,8},{24,0},{1,25},{9,17},{17,9},{25,1},{2,26},{10... | collective-permute-start | bytes 1013768 | tf_op jit(solution)/shard_map/ppermute | solution.py:846
  370.2 14.7 %collective-permute-start.18 = (bf16[120,1408]{1,0:T(8,128)(2,1)S(1)}, bf16[120,1408]{1,0:T(8,128)(2,1)S(1)}, u32[]{:S(2)}, u32[]{:S(2)}) collective-permute-start(bf16[120,1408]{1,0:T(8,128)(2,1)S(1)} %stage.2.own), channel_id=1, source_target_pairs={{0,16},{8,24},{16,0},{24,8},{1,17},{9,25},{17,1},{25,9},{2,18},{10... | collective-permute-start | bytes 1013768 | tf_op jit(solution)/shard_map/ppermute | solution.py:846
  370.7 14.2 %collective-permute-start.17 = (bf16[120,1408]{1,0:T(8,128)(2,1)S(1)}, bf16[120,1408]{1,0:T(8,128)(2,1)S(1)}, u32[]{:S(2)}, u32[]{:S(2)}) collective-permute-start(bf16[120,1408]{1,0:T(8,128)(2,1)S(1)} %stage.2.own), channel_id=1, source_target_pairs={{0,8},{8,0},{16,24},{24,16},{1,9},{9,1},{17,25},{25,17},{2,10},{10... | collective-permute-start | bytes 1013768 | tf_op jit(solution)/shard_map/ppermute | solution.py:846
  385.4 4.3 %copy-start = (bf16[408,1408]{1,0:T(8,128)(2,1)}, bf16[408,1408]{1,0:T(8,128)(2,1)S(1)}, u32[]{:S(2)}) copy-start(bf16[408,1408]{1,0:T(8,128)(2,1)S(1)} %stage.3.refs_2_) | copy-start | bytes 3446788
  385.5 4.3 %collective-permute-start.20 = (bf16[408,1408]{1,0:T(8,128)(2,1)S(1)}, bf16[408,1408]{1,0:T(8,128)(2,1)S(1)}, u32[]{:S(2)}, u32[]{:S(2)}) collective-permute-start(bf16[408,1408]{1,0:T(8,128)(2,1)S(1)} %stage.3.refs_2_), channel_id=1, source_target_pairs={{0,1},{1,0},{2,3},{3,2},{4,5},{5,4},{6,7},{7,6},{8,9},{9,8},{10,11... | collective-permute-start | bytes 3446792 | tf_op jit(solution)/shard_map/ppermute | solution.py:714
  385.5 4.2 %collective-permute-start.13 = (bf16[384,1152]{1,0:T(8,128)(2,1)S(1)}, bf16[384,1152]{1,0:T(8,128)(2,1)S(1)}, u32[]{:S(2)}, u32[]{:S(2)}) collective-permute-start(bf16[384,1152]{1,0:T(8,128)(2,1)S(1)} %pad_maximum_fusion.2.refs_0_), channel_id=1, source_target_pairs={{0,1},{1,0},{2,3},{3,2},{4,5},{5,4},{6,7},{7,6},{8,9},{9,8},{10,11... | collective-permute-start | bytes 2654216 | tf_op jit(solution)/shard_map/ppermute | solution.py:714
  386.0 3.7 collective-permute-start.21
  389.7 0.6 copy-start.12
  389.7 1.0 copy-start.7
  389.8 1.3 copy-start.6
Sparse Core Ops, SparseCore 0:
  11.5 73.4 all-gather.1
  200.6 115.2 reduce-scatter.4

commit v3 on v2

--- a/solution.py
+++ b/solution.py
@@ -16,10 +16,9 @@
 STEP = 10
 VPAD = 48
 VOCAB_ROWS = 40
-TAIL = 24
-UNITS = 1280
+TAIL = 48
+UNITS = 640
 THIRD = 40
-REST_TABLE = 32
 
 EPS_NORM = 1e-05
 CLIP_NORM = 0.002
@@ -29,6 +28,7 @@
 WEIGHT_DECAY = 0.01
 MASK_ID = 32
 MASKED = 1e30
+SAFE_EXPONENT = 40.0
 
 LOG2E = math.log2(math.e)
 SCALE = HEAD_DIM ** (-0.5)
@@ -91,14 +91,15 @@
 
 
 def qkv_kernel(
-    meta, embedding, projection, vectors, cos_a, cos_b, sin_a, sin_b,
-    x0, low, q_ext, k_ext, v_ext,
+    true_ids, picked, kinds, random_ids, slot_picked, splits, embedding, projection, vectors, cos_a, cos_b, sin_a, sin_b,
+    meta, x0, low, q_ext, k_ext, v_ext, rounded,
     table, weight, vec, wide,
 ):
-    width = meta.shape[1]
+    width = true_ids.shape[1]
     heads = q_ext.shape[0]
     model = x0.shape[0]
     vocab = embedding.shape[0]
+    block = pl.program_id(0)
 
     @pl.when(pl.program_id(0) == 0)
     def _():
@@ -109,9 +110,21 @@
         table[...] = wide[...].T.astype(bf16)
         for part in range(3):
             span = slice(part * model, (part + 1) * model)
-            weight[span, :] = projection[:, span].astype(bf16).T
-
-    ids = meta[0:1, :].astype(jnp.int32)
+            rounded[:, span] = projection[:, span].astype(bf16)
+            weight[span, :] = rounded[:, span].T
+
+    is_pick = picked[...] == 1
+    masked, swapped = is_pick & (kinds[...] < 8), is_pick & (kinds[...] == 8)
+    ids = jnp.where(masked, MASK_ID, jnp.where(swapped, random_ids[...], true_ids[...]))
+    split = splits[block // 2]
+    second = jnp.full((1, width), split * (block % 2), jnp.int32).astype(f32)
+    picks = picked[...].astype(f32)
+    counts = lane_sum(jnp.where(split > 0, picks, 0.0))
+    counts += lane_sum(jnp.where(split > 0, 0.0, slot_picked[...].astype(f32)))
+    crop_share = jnp.full((1, width), 1 + split, jnp.int32).astype(f32) * (1.0 / slot_picked.shape[1])
+    at = rows_of(8, width)
+    rows = jnp.where(at == 0, ids.astype(f32), jnp.where(at == 1, true_ids[...].astype(f32), jnp.where(at == 2, second, 0.0)))
+    meta[...] = jnp.where(at == 3, picks / counts, jnp.where(at == 4, crop_share, rows))
     vocab3 = rows_of(128, width)
     onehot = ((vocab3 == ids) | (vocab3 == ids + THIRD) | (vocab3 == ids + 2 * THIRD)).astype(f32).astype(bf16)
     embedded = dot(table[...], onehot)
@@ -121,7 +134,6 @@
     row = rows_of(EXT - HEAD_DIM, width)
     low[0:model, :] = normed
     low[model : model + 16, :] = jnp.where(row == 0, 1.0, 0.0).astype(bf16)
-    second = meta[2:3, :]
     in_second = second > 0.5
     cos = jnp.where(in_second, cos_a[...], cos_b[...])
     sin = jnp.where(in_second, sin_a[...], sin_b[...])
@@ -145,50 +157,78 @@
             out[head, HEAD_DIM:EXT, :] = extra
 
 
-def attention_kernel(q_ext, k_ext, v_ext, out, q_next):
+def attention_kernel(q_ext, k_ext, v_ext, out, raised, inverse):
     heads, _, width = q_ext.shape
     factor = LOG2E * SCALE
-    upcoming = dot(k_ext[0], q_ext[0], TN)
-    for head in range(heads):
-        queries = q_ext[head]
-        scores = upcoming
-        if head + 1 < heads:
-            upcoming = dot(k_ext[head + 1], q_ext[head + 1], TN)
-        top = jnp.max(scores, axis=0, keepdims=True)
-        weights = jnp.exp2((scores - top) * factor).astype(bf16)
-        mixed = dot(v_ext[head], weights)
-        total = mixed[HEAD_DIM : HEAD_DIM + 1, :]
-        out[head] = (mixed[0:HEAD_DIM, :] / total).astype(bf16)
-        high, middle, rest = split3(-(top + jnp.log2(total) * (1.0 / factor)))
-        q_next[head, 0:HEAD_DIM, :] = queries[0:HEAD_DIM, :]
-        row = rows_of(EXT - HEAD_DIM, width)
-        tail = queries[HEAD_DIM:EXT, :].astype(f32)
-        tail = jnp.where(row == 2, high, jnp.where(row == 3, middle, jnp.where(row == 4, rest, tail)))
-        q_next[head, HEAD_DIM:EXT, :] = tail.astype(bf16)
+
+    def longest(array):
+        values = array[:, 0:HEAD_DIM, :].astype(f32)
+        return jnp.max(jnp.sum(values * values, axis=1))
+
+    def finish(head):
+        mixed = dot(v_ext[head], raised[head], NT)
+        share = 1.0 / mixed[HEAD_DIM : HEAD_DIM + 1, :]
+        out[head] = (mixed[0:HEAD_DIM, :] * share).astype(bf16)
+        inverse[head] = jnp.broadcast_to(share, (8, width))
+
+    small = longest(q_ext) * longest(k_ext) * factor**2 <= SAFE_EXPONENT**2
+
+    @pl.when(small)
+    def _():
+        for head in range(heads):
+            raised[head] = jnp.exp2(dot(q_ext[head], k_ext[head], TN) * factor).astype(bf16)
+            finish(head)
+
+    @pl.when(jnp.logical_not(small))
+    def _():
+        for head in range(heads):
+            scores = dot(q_ext[head], k_ext[head], TN)
+            top = jnp.max(scores, axis=1, keepdims=True)
+            raised[head] = jnp.exp2((scores - top) * factor).astype(bf16)
+            finish(head)
 
 
 def attention_back_kernel(
-    q_ext, k_ext, v_ext, do_ext, low, meta, cos_a, cos_b, sin_a, sin_b, *rest, chunk, chained
+    q_ext, k_ext, v_ext, do_ext, raised, low, meta, cos_a, cos_b, sin_a, sin_b, *rest,
+    chunk, chained, carried, finished, first_head, from_slot,
 ):
-    dq, dk, dv, keep, send, grads, total = rest[3:] if chained else rest
+    rest = list(rest[3:] if chained else rest)
+    before = rest.pop(0) if carried else None
+    dq, dk, dv = rest[:3]
+    if finished:
+        keep, send, grads, held, sems, total = rest[3:]
+    else:
+        total, grads, held, sems = rest[3:]
     slot = pl.program_id(0)
     heads, _, width = q_ext.shape
+
+    def fetch(which, head):
+        source = raised.at[first_head + head, pl.ds((from_slot + which) * width, width)]
+        return pltpu.make_async_copy(source, held.at[which * heads + head], sems.at[which * heads + head])
+
+    @pl.when(slot == 0)
+    def _():
+        for which in range(held.shape[0] // heads):
+            for head in range(heads):
+                fetch(which, head).start()
+
     in_second = meta[2:3, :] > 0.5
     cos = jnp.where(in_second, cos_a[...], cos_b[...])
     sin = jnp.where(in_second, sin_a[...], sin_b[...])
     for head in range(heads):
+        fetch(slot, head).wait()
         keys = k_ext[head]
         q_parts = []
         k_total = v_total = None
         for at in range(0, width, chunk):
             piece = slice(at, at + chunk)
             queries, outs = q_ext[head, :, piece], do_ext[head, :, piece]
-            prob = jnp.exp2(dot(queries, keys, TN) * (LOG2E * SCALE))
+            prob = held[slot * heads + head, piece, :]
             inner = dot(outs, v_ext[head], TN)
-            score_grad = (prob * inner).astype(bf16)
+            score_grad = (prob.astype(f32) * inner).astype(bf16)
             q_parts.append(dot(keys[0:HEAD_DIM, :], score_grad, NT))
             k_part = dot(queries[0:HEAD_DIM, :], score_grad)
-            v_part = dot(outs[0:HEAD_DIM, :], prob.astype(bf16))
+            v_part = dot(outs[0:HEAD_DIM, :], prob)
             k_total = k_part if k_total is None else k_total + k_part
             v_total = v_part if v_total is None else v_total + v_part
         for part, (out, grad) in enumerate(((dq, jnp.concatenate(q_parts, axis=1)), (dk, k_total), (dv, v_total))):
@@ -205,23 +245,24 @@
 
     @pl.when(slot == 0)
     def _():
-        total[0:rows, :] = share
+        total[0:rows, :] = before[0:rows, :] + share if carried else share
 
     @pl.when(slot > 0)
     def _():
         total[0:rows, :] += share
 
-    @pl.when(slot == pl.num_programs(0) - 1)
-    def _():
-        half_rows = keep.shape[0]
-        total[rows:, :] = jnp.zeros((2 * half_rows - rows, total.shape[1]), f32)
-        split_halves(total, keep, send)
+    if finished:
+
+        @pl.when(slot == pl.num_programs(0) - 1)
+        def _():
+            total[rows:, :] = jnp.zeros((total.shape[0] - rows, total.shape[1]), f32)
+            split_halves(total, keep, send)
 
 
 def middle_kernel(
-    meta, x0, attended, outward, pair_all, embedding, vectors,
-    dx1, do_ext, keep_pair, send_pair, keep_rest, send_rest, loss,
-    w_up, w_down, up_t, down_t, act, slope, dw_up, dw_down, dw_out, dtable, dvec, vec, wide, table, table_t, w_out, w_out_t,
+    meta, x0, attended, inverse, outward, pair_all, embedding, vectors,
+    dx1, do_ext, keep_pair, send_pair, keep_rest, send_rest, dtable, loss,
+    w_up, w_down, up_t, down_t, act, slope, dw_up, dw_down, dw_out, dvec, vec, wide, table, table_t, w_out, w_out_t,
     sems,
 ):
     step = pl.program_id(0)
@@ -305,6 +346,18 @@
     dw_up[...] += dot(c_low, act[...], NT)
     for part in range(hidden_units // model):
         dvec[:, 3 + part : 4 + part] += lane_sum(act[part * model : (part + 1) * model, :].astype(f32))
+
+    @pl.when(step == pl.num_programs(0) - 1)
+    def _():
+        is_first = lax.axis_index("core") == 0
+        for side, (low, here, there, out) in enumerate(
+            ((down_t, dw_down, dw_up, send_pair), (up_t, dw_up, dw_down, keep_pair))
+        ):
+            for part in range(chunks):
+                span = slice(part * unit, (part + 1) * unit)
+                low[part * model : (part + 1) * model, :] = jnp.where(is_first, here[:, span], there[:, span]).astype(bf16)
+            pltpu.make_async_copy(low, out, sems.at[side]).start()
+
     dvec[:, 1:2] += lane_sum(c_grad * hat_two)
     dvec[:, 2:3] += lane_sum(c_grad)
     x1_grad = x2_grad + norm_back(c_grad, hat_two, inverse_two, col(6))
@@ -312,53 +365,41 @@
     x1_low = x1_grad.astype(bf16)
     dvec[:, 0:1] += lane_sum(x1_low.astype(f32))
     dw_out[0:model, :] += dot(attended[...], x1_low, NT)
-    o_grad = dot(w_out[...], x1_low).astype(bf16)
-    inner = o_grad.astype(f32) * attended[...].astype(f32)
+    o_grad = dot(w_out[...], x1_low)
+    inner = o_grad * attended[...].astype(f32)
     row = rows_of(EXT - HEAD_DIM, width)
     for head in range(heads):
         span = slice(head * HEAD_DIM, (head + 1) * HEAD_DIM)
-        high, middle, rest = split3(-jnp.sum(inner[span, :], axis=0, keepdims=True))
-        do_ext[head, 0:HEAD_DIM, :] = o_grad[span, :]
+        share = inverse[head, 0:1, :]
+        high, middle, rest = split3(-jnp.sum(inner[span, :], axis=0, keepdims=True) * share)
+        do_ext[head, 0:HEAD_DIM, :] = (o_grad[span, :] * share).astype(bf16)
         tail = jnp.where(row == 0, high, jnp.where(row == 1, middle, jnp.where(row == 2, rest, 0.0)))
         do_ext[head, HEAD_DIM:EXT, :] = tail.astype(bf16)
 
     @pl.when(step == pl.num_programs(0) - 1)
     def _():
-        is_first = lax.axis_index("core") == 0
-        copies = []
-        for side, (low, here, there, out) in enumerate(
-            ((down_t, dw_down, dw_up, send_pair), (up_t, dw_up, dw_down, keep_pair))
-        ):
-            for part in range(chunks):
-                span = slice(part * unit, (part + 1) * unit)
-                low[part * model : (part + 1) * model, :] = jnp.where(is_first, here[:, span], there[:, span]).astype(bf16)
-            copies.append(pltpu.make_async_copy(low, out, sems.at[side]))
-            copies[side].start()
-        wide[...] = dvec[...].T
-        wide[REST_TABLE : REST_TABLE + VPAD, :] = dtable[...]
-        dw_out[model:, :] = wide[...]
+        dw_out[model:, :] = dvec[...].T
         split_halves(dw_out, keep_rest, send_rest)
-        for copy in copies:
-            copy.wait()
+        for side, (low, out) in enumerate(((down_t, send_pair), (up_t, keep_pair))):
+            pltpu.make_async_copy(low, out, sems.at[side]).wait()
 
 
 def chunks_of_bias(model):
     return FF // model
 
 
-def input_back_kernel(meta, x0, dq, dk, dv, dx1, projection, vectors, *rest, last):
+def input_back_kernel(meta, x0, dq, dk, dv, dx1, weight, vectors, dtable_in, *rest, last):
     if last:
-        loss, dvec_in, dtable_in, tail, weight, vec, wide, dvec, dtable = rest
+        loss, dvec_in, tail, vec, wide, dvec, dtable = rest
     else:
-        dvec, dtable, weight, vec, wide = rest
+        dvec, dtable, vec, wide = rest
     step = pl.program_id(0)
     model, width = x0.shape
 
     @pl.when(step == 0)
     def _():
         vec[...] = columns_of(vectors, wide)
-        weight[...] = projection[...].astype(bf16)
-        dtable[...] = dtable_in[...] if last else jnp.zeros_like(dtable)
+        dtable[...] = dtable_in[...]
         dvec[...] = dvec_in[...] if last else jnp.zeros_like(dvec)
 
     back = None
@@ -371,21 +412,20 @@
     dvec[0:1, 2:3] += lane_sum(meta[4:5, :])
     x0_grad = dx1[...] + norm_back(back, hat, inverse, vec[:, 0:1])
     onehot = (rows_of(VPAD, width) == meta[0:1, :].astype(jnp.int32)).astype(f32).astype(bf16)
-    for piece in split3(x0_grad):
-        dtable[...] += dot(onehot, piece.astype(bf16), NT)
+    high = x0_grad.astype(bf16)
+    for piece in (high, (x0_grad - high.astype(f32)).astype(bf16)):
+        dtable[...] += dot(onehot, piece, NT)
 
     if last:
 
         @pl.when(step == pl.num_programs(0) - 1)
         def _():
             columns = dvec[...].T[0:8, :]
-            tail[:, 0:model] = dtable[0:TAIL, :]
-            tail[0 : VOCAB_ROWS - TAIL, model : 2 * model] = dtable[TAIL:VOCAB_ROWS, :]
-            tail[VOCAB_ROWS - TAIL :, model : 2 * model] = jnp.where(rows_of(8, model) < 2, columns, 0.0)
+            tail[0:VOCAB_ROWS, 0:model] = dtable[0:VOCAB_ROWS, :]
+            tail[VOCAB_ROWS:, 0:model] = jnp.where(rows_of(8, model) < 2, columns, 0.0)
             lane = lax.broadcasted_iota(jnp.int32, (TAIL, 128), 1)
-            first = rows_of(TAIL, 128) == 0
             numbers = jnp.where(lane == 0, loss[0:1, 0:1], jnp.where(lane == 1, columns[2:3, 0:1], 0.0))
-            tail[:, 2 * model :] = jnp.where(first, numbers, 0.0)
+            tail[:, model:] = jnp.where(rows_of(TAIL, 128) == 0, numbers, 0.0)
 
 
 def encode(tail):
@@ -404,7 +444,6 @@
 
 
 def pack_kernel(swapped, pair, tail, out, keep, send, *, pieces):
-    owned = pair.shape[0] - 2 * keep.shape[0]
     shares = swapped[...].astype(f32)
     rows = shares.shape[0] // pieces
     total = None
@@ -413,7 +452,7 @@
         total = share if total is None else total + share
     both = pair[...].astype(f32)
     half = keep.shape[0]
-    first, second = both[0:half, :], both[half : 2 * half, :]
+    first, second = both[0:half, :], both[half:, :]
     square = jnp.sum(lane_sum(first * first + second * second), axis=0, keepdims=True)
     is_first = lax.axis_index("core") == 0
     keep[...] = jnp.where(is_first, first, second).astype(bf16)
@@ -422,8 +461,7 @@
     wide = values.shape[1] - 128
     at_square = (rows_of(values.shape[0], 128) == 0) & (lax.broadcasted_iota(jnp.int32, (values.shape[0], 128), 1) == 2)
     values = jnp.concatenate([values[:, :wide], values[:, wide:] + jnp.where(at_square, square, 0.0)], axis=1)
-    mine = jnp.concatenate([total, both[2 * half : 2 * half + owned, :]], axis=1)
-    out[...] = jnp.concatenate([mine, encode(values)], axis=0).astype(bf16)
+    out[...] = jnp.concatenate([total, encode(values)], axis=0).astype(bf16)
 
 
 def stage_kernel(own, one, two, three, out, *, axis):
@@ -472,7 +510,6 @@
     vocab, model = ins[0].shape
     half_rows = early_mine.shape[0]
     piece = model // groups
-    last_width = 3 * piece * (groups - early_groups)
     after = model - half_rows
 
     @pl.when(step == 0)
@@ -497,7 +534,8 @@
             (last_mine, last_other, early_groups, groups - early_groups),
         ):
             upper, lower = halves(mine, other)
-            rest_upper, rest_lower = upper[:, last_width:], lower[:, last_width:]
+            if first == 0:
+                rest_upper, rest_lower = upper[:, 3 * piece * size :], lower[:, 3 * piece * size :]
             upper, lower = upper[:, : 3 * piece * size], lower[:, : 3 * piece * size]
             squares += add_squares(upper) + add_squares(lower)
             for group in range(size):
@@ -511,15 +549,14 @@
         upper, lower = rest_upper, rest_lower
         g_out[0:half_rows, :] = upper
         g_out[half_rows:, :] = lower[0:after, :]
-        others = lower[after : after + REST_TABLE, :]
+        others = lower[after : after + 16, :]
         g_vec[5:15, :] = others[0:10, :]
         tails = [decode(ref[half_rows:, :].astype(f32)) for ref in (last_mine, last_other)]
         final = tails[0] + tails[1]
-        scalars = final[:, 2 * model :]
-        late = jnp.concatenate([final[:, 0:model], final[0 : VOCAB_ROWS - TAIL, model : 2 * model]], axis=0)
-        table = late + lower[after + REST_TABLE : after + REST_TABLE + VOCAB_ROWS, :]
+        scalars = final[:, model:]
+        table = final[0:VOCAB_ROWS, 0:model]
         g_table[...] = table
-        tail = final[VOCAB_ROWS - TAIL :, model : 2 * model]
+        tail = final[VOCAB_ROWS:, 0:model]
         g_vec[0:2, :] = tail[0:2, :]
         squares += add_squares(upper) + add_squares(lower[0:after, :]) + add_squares(others) + add_squares(table)
         squares += add_squares(tail[0:2, :])
@@ -622,21 +659,6 @@
     pair_all = lax.all_gather(feedforward.astype(bf16), everywhere, axis=1, tiled=True)
     pair_all = pair_all.reshape(2, columns, model, wide)
 
-    masked = (picked == 1) & (replace_kinds < 8)
-    swapped = (picked == 1) & (replace_kinds == 8)
-    input_ids = jnp.where(masked, MASK_ID, jnp.where(swapped, random_ids, true_ids))
-    within = jnp.arange(rows, dtype=jnp.int32)
-    second = ((within[None, :] >= half).astype(jnp.int32) * splits[:, None]).astype(f32)
-    pick = picked.astype(f32).reshape(slots, rows)
-    half_counts = jnp.sum(pick.reshape(slots, 2, half), axis=2)
-    split = splits[:, None].astype(f32)
-    half_counts = jnp.where(split > 0.5, half_counts, jnp.sum(half_counts, axis=1, keepdims=True))
-    token_weight = (pick.reshape(slots, 2, half) / half_counts[:, :, None]).reshape(tokens)
-    zero = jnp.zeros((tokens,), f32)
-    crop_share = jnp.broadcast_to((1 + splits).astype(f32)[:, None] * (1.0 / rows), (slots, rows)).reshape(tokens)
-    meta = jnp.stack(
-        [input_ids.astype(f32), true_ids.astype(f32), second.reshape(-1), token_weight, crop_share, zero, zero, zero]
-    )
     cos_np, sin_np = rotary_constants(rows)
     cos_table, sin_table = jnp.asarray(cos_np), jnp.asarray(sin_np)
     twice_cos, twice_sin = (jnp.asarray(np.tile(t[:, :half], (1, 2))) for t in (cos_np, sin_np))
@@ -649,61 +671,65 @@
 
     first_half = pl.BlockSpec((HALF, block), lambda i: (0, 0))
     own_half = pl.BlockSpec((HALF, block), lambda i: (0, i % 2))
-    x0, normed, q_ext, k_ext, v_ext = pl.pallas_call(
+    id_block = pl.BlockSpec((1, block), lambda i: (0, i))
+    meta, x0, normed, q_ext, k_ext, v_ext, qkv_low = pl.pallas_call(
         qkv_kernel,
         grid=(blocks,),
-        in_specs=[by_block(8), whole((vocab, model)), whole((model, 3 * model)), whole(vectors.shape),
+        in_specs=[id_block] * 4 + [pl.BlockSpec((1, rows), lambda i: (0, i // 2)), pl.BlockSpec(memory_space=pltpu.SMEM),
+                  whole((vocab, model)), whole((model, 3 * model)), whole(vectors.shape),
                   first_half, own_half, first_half, own_half],
-        out_specs=[by_block(model), by_block(model + 16), heads_block(EXT), heads_block(EXT), heads_block(EXT)],
-        out_shape=[shaped((model, tokens), f32), shaped((model + 16, tokens), bf16)]
-        + [shaped((heads, EXT, tokens), bf16)] * 3,
+        out_specs=[by_block(8), by_block(model), by_block(model + 16), heads_block(EXT), heads_block(EXT), heads_block(EXT),
+                   whole((model, 3 * model))],
+        out_shape=[shaped((8, tokens), f32), shaped((model, tokens), f32), shaped((model + 16, tokens), bf16)]
+        + [shaped((heads, EXT, tokens), bf16)] * 3 + [shaped((model, 3 * model), bf16)],
         scratch_shapes=[pltpu.VMEM((model, 128), bf16), pltpu.VMEM((3 * model, model), bf16), pltpu.VMEM((model, 128), f32),
                         pltpu.VMEM((128, model), f32)],
         compiler_params=limits(56),
         cost_estimate=cost(2 * 3 * model * model * tokens, 20 * model * tokens),
         name="embed_and_qkv",
-    )(meta, embedding, projection, vectors, cos_table, cos_table, sin_table, sin_table)
+    )(*(ids.reshape(1, tokens) for ids in (true_ids, picked, replace_kinds, random_ids, picked)), splits,
+      embedding, projection, vectors, cos_table, cos_table, sin_table, sin_table)
 
     per = 4
 
     def head_group(count, size, first=0):
         return pl.BlockSpec((size, count, rows), lambda s, g: (first + g, 0, s))
 
-    attended, q_next = pl.pallas_call(
+    attended, raised, inverse = pl.pallas_call(
         attention_kernel,
         grid=(slots, heads // per),
         in_specs=[head_group(EXT, per)] * 3,
-        out_specs=[head_group(HEAD_DIM, per), head_group(EXT, per)],
-        out_shape=[shaped((heads, HEAD_DIM, tokens), bf16), shaped((heads, EXT, tokens), bf16)],
+        out_specs=[head_group(HEAD_DIM, per), pl.BlockSpec((per, rows, rows), lambda s, g: (g, s, 0)), head_group(8, per)],
+        out_shape=[shaped((heads, HEAD_DIM, tokens), bf16), shaped((heads, tokens, rows), bf16), shaped((heads, 8, tokens), f32)],
         compiler_params=limits(56),
-        cost_estimate=cost(2 * 16 * model * rows * tokens, 12 * model * tokens, heads * rows * tokens),
+        cost_estimate=cost(2 * 16 * model * rows * tokens, 2 * heads * rows * tokens, heads * rows * tokens),
         name="attention",
     )(q_ext, k_ext, v_ext)
     attended = attended.reshape(model, tokens)
 
     half_rows = (model + 128) // 2
     owned = -(-half_rows // (8 * columns * deep)) * 8
-    dx1, do_ext, keep_pair, send_pair, keep_rest, send_rest, loss = pl.pallas_call(
+    dx1, do_ext, keep_pair, send_pair, keep_rest, send_rest, dtable_end, loss = pl.pallas_call(
         middle_kernel,
         grid=(blocks,),
-        in_specs=[by_block(8), by_block(model), by_block(model), whole((model, model)),
+        in_specs=[by_block(8), by_block(model), by_block(model), heads_block(8), whole((model, model)),
                   pl.BlockSpec(memory_space=pl.ANY), whole((vocab, model)), whole(vectors.shape)],
         out_specs=[by_block(model), heads_block(EXT), pl.BlockSpec(memory_space=pl.ANY), pl.BlockSpec(memory_space=pl.ANY),
-                   whole((half_rows, model)), whole((half_rows, model)), whole((8, 128))],
+                   whole((half_rows, model)), whole((half_rows, model)), whole((VPAD, model)), whole((8, 128))],
         out_shape=[shaped((model, tokens), f32), shaped((heads, EXT, tokens), bf16), shaped((columns * model, wide), bf16),
                    shaped((columns * model, wide), bf16), shaped((half_rows, model), bf16), shaped((half_rows, model), bf16),
-                   shaped((8, 128), f32)],
+                   shaped((VPAD, model), f32), shaped((8, 128), f32)],
         scratch_shapes=[pltpu.VMEM((model, FF), bf16), pltpu.VMEM((model, FF), bf16), pltpu.VMEM((FF, model), bf16),
                         pltpu.VMEM((FF, model), bf16), pltpu.VMEM((FF, block), bf16), pltpu.VMEM((FF, block), bf16),
                         pltpu.VMEM((model, FF), f32), pltpu.VMEM((model, FF), f32),
-                        pltpu.VMEM((model + 128, model), f32), pltpu.VMEM((VPAD, model), f32), pltpu.VMEM((model, 128), f32),
+                        pltpu.VMEM((model + 128, model), f32), pltpu.VMEM((model, 128), f32),
                         pltpu.VMEM((model, 128), f32), pltpu.VMEM((128, model), f32),
                         pltpu.VMEM((VPAD, model), bf16), pltpu.VMEM((model, 128), bf16),
                         pltpu.VMEM((model, model), bf16), pltpu.VMEM((model, model), bf16), pltpu.SemaphoreType.DMA((2 + 2 * columns,))],
         compiler_params=limits(62),
         cost_estimate=cost(2 * tokens * model * (6 * FF + 3 * model), 14 * model * tokens + 16 * model * FF, FF * tokens),
         name="feedforward_and_head",
-    )(meta, x0, attended, outward, pair_all, embedding, vectors)
+    )(meta, x0, attended, inverse, outward, pair_all, embedding, vectors)
 
     count = columns * deep
 
@@ -751,37 +777,53 @@
     grads = None
     keeps, sents = [], []
     groups = heads // per_call
-    for first in range(groups):
-        chained = grads is not None
-
-        def group(count, first=first):
-            return pl.BlockSpec((per_call, count, rows), lambda s: (first, 0, s))
+    calls = [(0, 0, 1), (0, 1, slots - 1)] + [(g, 0, slots) for g in range(1, groups)]
+    carry = None
+    for index, (first, from_slot, slot_count) in enumerate(calls):
+        chained, carried, finished = grads is not None, carry is not None, from_slot + slot_count == slots
+
+        def group(count, first=first, from_slot=from_slot):
+            return pl.BlockSpec((per_call, count, rows), lambda s: (first, 0, from_slot + s))
+
+        def by_slot(count, from_slot=from_slot):
+            return pl.BlockSpec((count, rows), lambda s: (0, from_slot + s))
 
         table_spec = pl.BlockSpec((HALF, rows), lambda s: (0, 0))
         outs = pl.pallas_call(
-            functools.partial(attention_back_kernel, chunk=half, chained=chained),
-            grid=(slots,),
-            in_specs=[group(EXT)] * 4
-            + [pl.BlockSpec((model + 16, rows), lambda s: (0, s)), pl.BlockSpec((8, rows), lambda s: (0, s))]
-            + [table_spec] * 4
-            + [pl.BlockSpec(memory_space=pl.ANY)] * (3 if chained else 0),
-            out_specs=[group(HEAD_DIM)] * 3 + [pl.BlockSpec((half_rows, width), lambda s: (0, 0))] * 2,
-            out_shape=[shaped((heads, HEAD_DIM, tokens), bf16)] * 3 + [shaped((half_rows, width), bf16)] * 2,
-            scratch_shapes=[pltpu.VMEM((width, rows), bf16), pltpu.VMEM((2 * half_rows, width), f32)],
-            input_output_aliases={10: 0, 11: 1, 12: 2} if chained else {},
+            functools.partial(attention_back_kernel, chunk=half, chained=chained, carried=carried, finished=finished,
+                              first_head=first * per_call, from_slot=from_slot),
+            grid=(slot_count,),
+            in_specs=[group(EXT)] * 4 + [pl.BlockSpec(memory_space=pl.ANY), by_slot(model + 16), by_slot(8)] + [table_spec] * 4
+            + [pl.BlockSpec(memory_space=pl.ANY)] * (3 if chained else 0)
+            + ([whole((2 * half_rows, width))] if carried else []),
+            out_specs=[group(HEAD_DIM)] * 3
+            + ([pl.BlockSpec((half_rows, width), lambda s: (0, 0))] * 2 if finished else [whole((2 * half_rows, width))]),
+            out_shape=[shaped((heads, HEAD_DIM, tokens), bf16)] * 3
+            + ([shaped((half_rows, width), bf16)] * 2 if finished else [shaped((2 * half_rows, width), f32)]),
+            scratch_shapes=[pltpu.VMEM((width, rows), bf16), pltpu.VMEM((slot_count * per_call, rows, rows), bf16),
+                            pltpu.SemaphoreType.DMA((slot_count * per_call,))]
+            + ([pltpu.VMEM((2 * half_rows, width), f32)] if finished else []),
+            input_output_aliases={11: 0, 12: 1, 13: 2} if chained else {},
             compiler_params=limits(56),
-            cost_estimate=cost(2 * 40 * width // 3 * rows * tokens, 20 * width * tokens, per_call * rows * tokens),
+            cost_estimate=cost(2 * 40 * width // 3 * rows * rows * slot_count, 20 * width * rows * slot_count, per_call * rows * rows * slot_count),
             name="attention_back",
-        )(q_next, k_ext, v_ext, do_ext, normed, meta, twice_cos, cos_table, twice_sin, sin_table, *(grads or ()))
-        grads = outs[:3]
-        keeps.append(outs[3])
-        sents.append(over_core(outs[4]))
-        if first == 0:
+        )(q_ext, k_ext, v_ext, do_ext, raised, normed, meta, twice_cos, cos_table, twice_sin, sin_table, *(grads or ()),
+          *((carry,) if carried else ()))
+        grads = list(outs[:3])
+        carry = None if finished else outs[3]
+        if finished:
+            keeps.append(outs[3])
+            sents.append(over_core(outs[4]))
+        if index == 0:
+            grads[0], pair_sent, rest_sent = together(grads[0], pair_sent, rest_sent)
             pair = pair_sum(keep_pair.reshape(count, -1, wide), pair_sent.reshape(count, -1, wide))
             rest_half = pad_rows(pair_sum(keep_rest, rest_sent)).reshape(count, owned, model)
             pair = jnp.concatenate([pair, rest_half], axis=1).reshape(-1, wide)
             do_ext, pair = together(do_ext, pair)
-            pair = lax.psum_scatter(pair, chips, scatter_dimension=0, tiled=True)
+            pair = lax.psum_scatter(pair, "col", scatter_dimension=0, tiled=True)
+        elif first == groups - 3:
+            do_ext, pair = together(do_ext, pair)
+            pair = lax.psum_scatter(pair, "deep", scatter_dimension=0, tiled=True)
         elif first == groups - 2:
             early = jnp.concatenate([pair_sum(keeps[i], sents[i]) for i in range(groups - 2)], axis=1)
             do_ext, early = together(do_ext, early)
@@ -789,13 +831,14 @@
         elif first == groups - 1:
             late_half = jnp.concatenate([pair_sum(keeps[i], sents[i]) for i in range(groups - 2, groups)], axis=1)
             early = add_up(early, count).astype(bf16)
-            dx1, late_half, early = together(dx1, late_half, early)
+            dx1, late_half, early, pair = together(dx1, late_half, early, pair)
             late_half = to_owner(late_half)
-            early = gather_deep(early)
+            early = gather_deep(jnp.concatenate([early, pair[-owned:]], axis=1))
+            pair = pair[:-owned]
     dq, dk, dv = (grad.reshape(model, tokens) for grad in grads)
 
     back_out = [shaped((model, 128), f32), shaped((VPAD, model), f32)]
-    back_room = [pltpu.VMEM((model, 3 * model), bf16), pltpu.VMEM((model, 128), f32), pltpu.VMEM((128, model), f32)]
+    back_room = [pltpu.VMEM((model, 128), f32), pltpu.VMEM((128, model), f32)]
 
     def input_back(part, extra):
         def by_part(rows_):
@@ -808,18 +851,18 @@
             grid=(blocks // 2,),
             in_specs=[by_part(8)] + [by_part(model)] * 5 + [whole((model, 3 * model)), whole(vectors.shape)]
             + [whole(array.shape) for array in extra],
-            out_specs=[whole((TAIL, 2 * model + 128))] if last else [whole(shape.shape) for shape in back_out],
-            out_shape=[shaped((TAIL, 2 * model + 128), f32)] if last else back_out,
+            out_specs=[whole((TAIL, model + 128))] if last else [whole(shape.shape) for shape in back_out],
+            out_shape=[shaped((TAIL, model + 128), f32)] if last else back_out,
             scratch_shapes=back_room + (room if last else []),
             compiler_params=limits(56),
-            cost_estimate=cost(3 * model * model * tokens, 10 * model * tokens),
+            cost_estimate=cost(model * model * tokens, 4 * model * tokens),
             name="input_back",
-        )(meta, x0, dq, dk, dv, dx1, projection, vectors, *extra)
-
-    halfway = input_back(0, ())
+        )(meta, x0, dq, dk, dv, dx1, qkv_low, vectors, *extra)
+
+    halfway = input_back(0, (dtable_end,))
     dvec_half, dtable_half, early = together(*halfway, early)
     early = gather_col(early)
-    (tail,) = input_back(1, (loss, dvec_half, dtable_half))
+    (tail,) = input_back(1, (dtable_half, loss, dvec_half))
     tail, pair, early, late_half = together(tail, pair, early, late_half)
     early_other = over_core(early)
 
@@ -834,9 +877,9 @@
             name=name,
         )(*args)
 
-    own = (pair.shape[0] - owned) // 2
-    last_width = late_half.shape[1] + model
-    if columns == 4 and deep == 4 and owned == TAIL and last_width == tail.shape[1]:
+    own = pair.shape[0] // 2
+    last_width = late_half.shape[1]
+    if columns == 4 and deep == 4 and last_width == tail.shape[1]:
         packed, pair_keep, pair_sent = call_small(
             functools.partial(pack_kernel, pieces=count), (late_half, pair, tail),
             [(owned + TAIL, last_width), (own, wide), (own, wide)], "pack",
@@ -848,17 +891,17 @@
             (packed,) = call_small(functools.partial(stage_kernel, axis=axis), (packed, *got), [(merged, last_width)], "stage")
     else:
         is_first = lax.axis_index("core") == 0
-        pair_keep = jnp.where(is_first, pair[:own], pair[own : 2 * own])
-        pair_sent = over_core(jnp.where(is_first, pair[own : 2 * own], pair[:own]))
-        square = jnp.sum(jnp.square(pair[: 2 * own].astype(f32)))
-        tail = lax.psum(tail.at[0, 2 * model + 2].add(square), chips)
-        scalars = tail[0:1, 2 * model :]
+        pair_keep = jnp.where(is_first, pair[:own], pair[own:])
+        pair_sent = over_core(jnp.where(is_first, pair[own:], pair[:own]))
+        square = jnp.sum(jnp.square(pair.astype(f32)))
+        tail = lax.psum(tail.at[0, model + 2].add(square), chips)
+        scalars = tail[0:1, model:]
         high = lax.reduce_precision(scalars, 8, 7)
         middle = lax.reduce_precision(scalars - high, 8, 7)
         numbers = jnp.concatenate([high, middle, scalars - high - middle, jnp.zeros((TAIL - 3, 128), f32)], axis=0)
-        tail = jnp.pad(jnp.concatenate([tail[:, : 2 * model], numbers], axis=1), ((0, 0), (0, last_width - tail.shape[1])))
-        packed = jnp.concatenate([add_up(late_half, count).astype(bf16), pair[2 * own :]], axis=1)
-        packed = jnp.concatenate([gather_col(gather_deep(packed)), tail.astype(bf16)], axis=0)
+        tail = jnp.pad(jnp.concatenate([tail[:, :model], numbers], axis=1), ((0, 0), (0, last_width - tail.shape[1])))
+        packed = gather_col(gather_deep(add_up(late_half, count).astype(bf16)))
+        packed = jnp.concatenate([packed, tail.astype(bf16)], axis=0)
     packed_other = over_core(packed)
 
     steps = 10

time: 424 us -> 402 us (0.948); the launches traced: 418 us -> 404 us
  waiting for transfers between devices: 39.9 us -> 30.9 us
    ppermute x6, waiting for transfers between devices: 22.8 us -> 15.2 us  [body(): lax.ppermute(packed, axis, [(i, i ^ d) for i in range(4)])]
    all_to_all x2, waiting for transfers between devices: 10.5 us -> 3.76 us  [swap(): return lax.all_to_all(values, axes, 0, 0, tiled=True)]
    all_gather x1, waiting for transfers between devices: 0.01 us -> 5.46 us  [body(): lax.all_gather(feedforward.astype(bf16), everywhere, axis=1, tiled=True)]
    pallas_call x5 -> x6, Pallas kernels: 113 us -> 116 us  [body(): pl.pallas_call(functools.partial(attention_back_kernel, chunk=half, chain...]
  transfers between devices with their start and end apart: 26 -> 27, of which waited for: 8 -> 12; matrix products, arithmetic and copies ran while one was open for 2% -> 1% of each run, Pallas kernels for 50% -> 51%
where the time goes in v3:
time: 402 us; the launch traced here: 404 us
  Pallas kernels  316 us (79%)
  waiting for transfers between devices  30.9 us (8%)
  starting transfers between devices  30.8 us (8%)
  between operations  14.4 us (4%)
  other arithmetic  9.47 us (2%)
    pallas_call x6, Pallas kernels, body(): pl.pallas_call(functools.partial(attention_back_kernel, chunk=half, chain...  116 us
    pallas_call x1, Pallas kernels, body(): pl.pallas_call(middle_kernel, grid=(blocks,), in_specs=[by_block(8), by_b...  89.5 us
    pallas_call x1, Pallas kernels, body(): pl.pallas_call(attention_kernel, grid=(slots, heads // per), in_specs=[he...  54.1 us
    pallas_call x2, Pallas kernels, input_back(): pl.pallas_call(functools.partial(input_back_kernel, last=last), grid=(blo...  20.5 us
    pallas_call x1, Pallas kernels, body(): pl.pallas_call(functools.partial(update_kernel, groups=groups, early_grou...  19.4 us
    pallas_call x1, Pallas kernels, body(): pl.pallas_call(qkv_kernel, grid=(blocks,), in_specs=[id_block] * 4 + [pl....  15.9 us
    ppermute x6, waiting for transfers between devices, body(): lax.ppermute(packed, axis, [(i, i ^ d) for i in range(4)])  15.2 us
    all_to_all x2, starting transfers between devices, swap(): return lax.all_to_all(values, axes, 0, 0, tiled=True)  12.1 us
  transfers between devices with their start and end apart: 27, of which 12 were waited for; matrix products, arithmetic and copies ran while one was open for 1% of the time, Pallas kernels for 51%

profile of v3, /device:TPU:0, one launch (start us, length us, event | category | flops | bytes accessed | tf_op | source)
XLA Modules:
  0.0 404.0 jit_solution(1949656700181100802)
XLA Ops:
  7.2 1.7 convert_element_type.73
  9.0 15.9 %embed_and_qkv.1 = (f32[8,2048]{1,0:T(8,128)}, f32[640,2048]{1,0:T(8,128)}, bf16[656,2048]{1,0:T(8,128)(2,1)}, bf16[20,48,2048]{2,1,0:T(8,128)(2,1)}, bf16[20,48...) custom-call(s32[1,2048]{1,0:T(1,128)} %bitcast.28, s32[1,2048]{1,0:T(1,128)} %bitcast.29, ...), custom_call_target="tpu_custom_call" | custom-call | flops 5033164800 | bytes 26214400 | tf_op jit(solution)/shard_map/embed_and_qkv/pallas_call | solution.py:675
  24.9 54.1 %attention.1 = (bf16[20,32,2048]{2,1,0:T(8,128)(2,1)}, bf16[20,2048,1024]{2,1,0:T(8,128)(2,1)}, f32[20,8,2048]{2,1,0:T(8,128)}) custom-call(bf16[20,48,2048]{2,1,0:T(8,128)(2,1)} %get-tuple-element.118.q_ext, bf16[20,48,2048]{2,1,0:T(8,128)(2,1)} %get-tuple-element.119.k_ext, bf16[20,48,2048]{2,1,0:T(8,128)(2,1)} %get-tuple-element.120.v_ext), custom_call_target="tpu_custom_call" | custom-call | flops 42949672960 | bytes 83886080 | tf_op jit(solution)/shard_map/attention/pallas_call | solution.py:698
  79.0 5.5 %all-gather.2.cloned.1.call-done = bf16[2,2560,640]{2,1,0:T(8,128)(2,1)} async-done(((bf16[2,80,640]{2,1,0:T(8,128)(2,1)}), bf16[2,2560,640]{2,1,0:T(8,128)(2,1)}) %all-gather.2.cloned.1.call-update) | async-done | bytes 6553616 | tf_op jit(solution)/shard_map/all_gather | solution.py:659
  84.5 89.5 %feedforward_and_head.1 = (f32[640,2048]{1,0:T(8,128)}, bf16[20,48,2048]{2,1,0:T(8,128)(2,1)}, bf16[2560,640]{1,0:T(8,128)(2,1)}, bf16[2560,640]{1,0:T(8,128)(2,...) custom-call(f32[8,2048]{1,0:T(8,128)} %get-tuple-element.116.meta, ...), custom_call_target="tpu_custom_call" | custom-call | flops 45298483200 | bytes 44564480 | tf_op jit(solution)/shard_map/feedforward_and_head/pallas_call | solution.py:712
  174.5 13.1 %attention_back.6 = (bf16[20,32,2048]{2,1,0:T(8,128)(2,1)}, bf16[20,32,2048]{2,1,0:T(8,128)(2,1)}, bf16[20,32,2048]{2,1,0:T(8,128)(2,1)}, f32[768,384]{1,0:T(8,128)}) custom-call(bf16[20,48,2048]{2,1,0:T(8,128)(2,1)} %get-tuple-element.118.q_ext, bf16[20,48,2048]{2,1,0:T(8,128)(2,1)} %get-tuple-element.119.k_ext, ...), custom_call_target="tpu_custom_call" | custom-call | flops 10737418240 | bytes 7864320 | tf_op jit(solution)/shard_map/attention_back/pallas_call | solution.py:792
  187.8 0.8 add_convert_fusion
  188.6 2.2 pad_maximum_fusion
  190.8 13.2 %attention_back.7 = (bf16[20,32,2048]{2,1,0:T(8,128)(2,1)}, bf16[20,32,2048]{2,1,0:T(8,128)(2,1)}, bf16[20,32,2048]{2,1,0:T(8,128)(2,1)}, bf16[384,384]{1,0:T(8,128)(2,1)}, bf16[384,384]{1,0:T(8,128)(2,1)}) custom-call(bf16[20,48,2048]{2,1,0:T(8,128)(2,1)} %get-tuple-element.118.q_ext, ...), custom_call_target="tpu_custom_call", output_to_operand_aliasing={{0}: (11, {}), {1}: (12, {}), {2}: (13, {})} | custom-call | flops 10737418240 | bytes 7864320 | tf_op jit(solution)/shard_map/attention_back/pallas_call | solution.py:792
  204.1 22.3 %attention_back.8 = (bf16[20,32,2048]{2,1,0:T(8,128)(2,1)}, bf16[20,32,2048]{2,1,0:T(8,128)(2,1)}, bf16[20,32,2048]{2,1,0:T(8,128)(2,1)}, bf16[384,384]{1,0:T(8,128)(2,1)}, bf16[384,384]{1,0:T(8,128)(2,1)}) custom-call(bf16[20,48,2048]{2,1,0:T(8,128)(2,1)} %get-tuple-element.118.q_ext, ...), custom_call_target="tpu_custom_call", output_to_operand_aliasing={{0}: (11, {}), {1}: (12, {}), {2}: (13, {})} | custom-call | flops 21474836480 | bytes 15728640 | tf_op jit(solution)/shard_map/attention_back/pallas_call | solution.py:792
  226.4 22.3 %attention_back.9 = (bf16[20,32,2048]{2,1,0:T(8,128)(2,1)}, bf16[20,32,2048]{2,1,0:T(8,128)(2,1)}, bf16[20,32,2048]{2,1,0:T(8,128)(2,1)}, bf16[384,384]{1,0:T(8,128)(2,1)}, bf16[384,384]{1,0:T(8,128)(2,1)}) custom-call(bf16[20,48,2048]{2,1,0:T(8,128)(2,1)} %get-tuple-element.118.q_ext, ...), custom_call_target="tpu_custom_call", output_to_operand_aliasing={{0}: (11, {}), {1}: (12, {}), {2}: (13, {})} | custom-call | flops 21474836480 | bytes 15728640 | tf_op jit(solution)/shard_map/attention_back/pallas_call | solution.py:792
  248.7 0.5 collective-permute-start.4
  249.7 0.9 collective-permute-done.4
  250.6 1.0 add_convert_fusion.4
  251.9 1.0 pad_maximum_fusion.2
  252.8 5.0 %all-to-all-start = ((bf16[16,24,1152]{2,1,0:T(8,128)(2,1)}), bf16[16,24,1152]{2,1,0:T(8,128)(2,1)S(1)}, u32[]{:S(2)}, u32[]{:S(2)}) async-start(bf16[16,24,1152]{2,1,0:T(8,128)(2,1)} %bitcast.12), calls=%async_computation.1 | async-start | bytes 1769472 | tf_op jit(solution)/shard_map/all_to_all | solution.py:737
  257.9 0.7 reduce-scatter.7.cloned.1.call-update
  258.6 22.3 %attention_back.10 = (bf16[20,32,2048]{2,1,0:T(8,128)(2,1)}, bf16[20,32,2048]{2,1,0:T(8,128)(2,1)}, bf16[20,32,2048]{2,1,0:T(8,128)(2,1)}, bf16[384,384]{1,0:T(8,128)(2,1)}, bf16[384,384]{1,0:T(8,128)(2,1)}) custom-call(bf16[20,48,2048]{2,1,0:T(8,128)(2,1)} %get-tuple-element.118.q_ext, ...), custom_call_target="tpu_custom_call", output_to_operand_aliasing={{0}: (11, {}), {1}: (12, {}), {2}: (13, {})} | custom-call | flops 21474836480 | bytes 15728640 | tf_op jit(solution)/shard_map/attention_back/pallas_call | solution.py:792
  280.9 22.5 %attention_back.11 = (bf16[20,32,2048]{2,1,0:T(8,128)(2,1)}, bf16[20,32,2048]{2,1,0:T(8,128)(2,1)}, bf16[20,32,2048]{2,1,0:T(8,128)(2,1)}, bf16[384,384]{1,0:T(8,128)(2,1)}, bf16[384,384]{1,0:T(8,128)(2,1)}) custom-call(bf16[20,48,2048]{2,1,0:T(8,128)(2,1)} %get-tuple-element.118.q_ext, ...), custom_call_target="tpu_custom_call", output_to_operand_aliasing={{0}: (11, {}), {1}: (12, {}), {2}: (13, {})} | custom-call | flops 21474836480 | bytes 15728640 | tf_op jit(solution)/shard_map/attention_back/pallas_call | solution.py:792
  304.1 1.3 collective-permute-done.6
  305.3 1.0 add_convert_fusion.2
  306.5 0.9 pad_maximum_fusion.3
  307.5 0.8 slice.6
  308.3 3.8 collective-permute-start.7
  312.0 0.7 collective-permute-start.9
  312.7 10.1 %input_back.2 = (f32[640,128]{1,0:T(8,128)}, f32[48,640]{1,0:T(8,128)}) custom-call(f32[8,2048]{1,0:T(8,128)} %get-tuple-element.116.meta, f32[640,2048]{1,0:T(8,128)} %get-tuple-element.117.x0, bf16[640,2048]{1,0:T(8,128)(2,1)} %bitcast.18, bf16[640,2048]{1,0:T(8,128)(2,1)} %bitcast.20, bf16[640,2048]{1,0:T(8,128)(2,1)} %bitcast.22, ...), custom_call_target="tpu_custom_call" | custom-call | flops 838860800 | bytes 5242880 | tf_op jit(solution)/shard_map/input_back/pallas_call | solution.py:849
  323.0 2.9 collective-permute-start.10
  325.9 0.6 collective-permute-start.11
  326.6 7.1 %all-to-all-start.1 = ((bf16[16,24,768]{2,1,0:T(8,128)(2,1)}), bf16[16,24,768]{2,1,0:T(8,128)(2,1)S(1)}, u32[]{:S(2)}, u32[]{:S(2)}) async-start(bf16[16,24,768]{2,1,0:T(8,128)(2,1)} %bitcast.14), calls=%async_computation.2 | async-start | bytes 1179648 | tf_op jit(solution)/shard_map/all_to_all | solution.py:737
  333.7 10.4 %input_back.3.tail = f32[48,768]{1,0:T(8,128)} custom-call(f32[8,2048]{1,0:T(8,128)} %get-tuple-element.116.meta, f32[640,2048]{1,0:T(8,128)} %get-tuple-element.117.x0, bf16[640,2048]{1,0:T(8,128)(2,1)} %bitcast.19, bf16[640,2048]{1,0:T(8,128)(2,1)} %bitcast.21, bf16[640,2048]{1,0:T(8,128)(2,1)} %bitcast.23, f32[640,2048]{1,0:T(8,128)} %get-tuple-element.169.dx1, ...), custom_call_target="tpu_custom_call" | custom-call | flops 838860800 | bytes 5242880 | tf_op jit(solution)/shard_map/input_back/pallas_call | solution.py:849
  344.1 1.2 collective-permute-done.11
  345.3 0.6 collective-permute-done.12
  346.1 3.8 all-to-all-done.1
  350.1 0.6 copy-done.2
  350.7 1.4 collective-permute-start.15
  352.1 3.0 collective-permute-start.16
  355.1 2.3 collective-permute-done.14.one
  357.4 4.8 %collective-permute-done.15.two = bf16[72,768]{1,0:T(8,128)(2,1)S(1)} collective-permute-done((bf16[72,768]{1,0:T(8,128)(2,1)S(1)}, bf16[72,768]{1,0:T(8,128)(2,1)S(1)}, u32[]{:S(2)}, u32[]{:S(2)}) %collective-permute-start.15) | collective-permute-done | bytes 110624 | tf_op jit(solution)/shard_map/ppermute | solution.py:889
  362.3 0.6 collective-permute-start.17
  363.0 1.2 collective-permute-start.18
  364.1 1.8 collective-permute-start.19
  365.9 4.9 %collective-permute-done.17.one = bf16[144,768]{1,0:T(8,128)(2,1)S(1)} collective-permute-done((bf16[144,768]{1,0:T(8,128)(2,1)S(1)}, bf16[144,768]{1,0:T(8,128)(2,1)S(1)}, u32[]{:S(2)}, u32[]{:S(2)}) %collective-permute-start.17) | collective-permute-done | bytes 221216 | tf_op jit(solution)/shard_map/ppermute | solution.py:889
  370.9 3.0 collective-permute-done.19.three
  374.3 0.5 collective-permute-start.21
  374.8 1.7 collective-permute-done.21.refs_5_
  376.5 0.6 copy-done.12
  377.4 0.5 copy-done.5
  377.8 19.4 %clip_and_adamw.1 = (f32[33,640]{1,0:T(8,128)}, f32[33,640]{1,0:T(8,128)}, f32[33,640]{1,0:T(8,128)}, bf16[33,640]{1,0:T(8,128)(2,1)}, f32[640,1920]{1,0:T(8,128...) custom-call(bf16[384,1792]{1,0:T(8,128)(2,1)} %copy-done.3, ...), custom_call_target="tpu_custom_call" | custom-call | flops 98304000 | bytes 49152000 | tf_op jit(solution)/shard_map/clip_and_adamw/pallas_call | solution.py:922
  (75 shorter events, 3.8 us)
Async XLA Ops:
  7.2 77.3 %all-gather.2.cloned.1.call-start = ((), (), s32[]{:S(2)}) async-start(), calls=%async_computation.4 | async-start | bytes 6758400 | tf_op jit(solution)/shard_map/all_gather | solution.py:659
  9.0 243.9 %reduce-scatter.5.cloned.1.call-start = ((), (), s32[]{:S(2)}) async-start(), calls=%async_computation.5 | async-start | bytes 4710400 | tf_op jit(solution)/shard_map/reduce_scatter | solution.py:823
  173.9 13.7 %collective-permute-start = (bf16[2560,640]{1,0:T(8,128)(2,1)}, bf16[2560,640]{1,0:T(8,128)(2,1)S(1)}, u32[]{:S(2)}, u32[]{:S(2)}) collective-permute-start(bf16[2560,640]{1,0:T(8,128)(2,1)} %get-tuple-element.128), channel_id=1, source_target_pairs={{0,1},{1,0},{2,3},{3,2},{4,5},{5,4},{6,7},{7,6},{8,9},{9,8},{10,11... | collective-permute-start | bytes 9830408 | tf_op jit(solution)/shard_map/ppermute | solution.py:740
  174.3 13.3 %collective-permute-start.1 = (bf16[384,640]{1,0:T(8,128)(2,1)}, bf16[384,640]{1,0:T(8,128)(2,1)S(1)}, u32[]{:S(2)}, u32[]{:S(2)}) collective-permute-start(bf16[384,640]{1,0:T(8,128)(2,1)} %get-tuple-element.129), channel_id=1, source_target_pairs={{0,1},{1,0},{2,3},{3,2},{4,5},{5,4},{6,7},{7,6},{8,9},{9,8},{10,11... | collective-permute-start | bytes 1474568 | tf_op jit(solution)/shard_map/ppermute | solution.py:740
  174.5 13.1 %copy-start.7 = (bf16[384,640]{1,0:T(8,128)(2,1)S(1)}, bf16[384,640]{1,0:T(8,128)(2,1)}, u32[]{:S(2)}) copy-start(bf16[384,640]{1,0:T(8,128)(2,1)} %get-tuple-element.131) | copy-start | bytes 1474564
  174.5 13.3 %copy-start.4 = (bf16[2560,640]{1,0:T(8,128)(2,1)S(1)}, bf16[2560,640]{1,0:T(8,128)(2,1)}, u32[]{:S(2)}) copy-start(bf16[2560,640]{1,0:T(8,128)(2,1)} %get-tuple-element.124) | copy-start | bytes 9830404
  226.4 22.8 %copy-start.15 = (bf16[384,384]{1,0:T(8,128)(2,1)S(1)}, bf16[384,384]{1,0:T(8,128)(2,1)}, u32[]{:S(2)}) copy-start(bf16[384,384]{1,0:T(8,128)(2,1)} %get-tuple-element.146) | copy-start | bytes 884740
  226.4 22.9 %copy-start.13 = (bf16[384,384]{1,0:T(8,128)(2,1)S(1)}, bf16[384,384]{1,0:T(8,128)(2,1)}, u32[]{:S(2)}) copy-start(bf16[384,384]{1,0:T(8,128)(2,1)} %get-tuple-element.141) | copy-start | bytes 884740
  226.4 25.3 %copy-start.10 = (bf16[384,384]{1,0:T(8,128)(2,1)S(1)}, bf16[384,384]{1,0:T(8,128)(2,1)}, u32[]{:S(2)}) copy-start(bf16[384,384]{1,0:T(8,128)(2,1)} %get-tuple-element.145) | copy-start | bytes 884740
  226.4 25.4 %copy-start.8 = (bf16[384,384]{1,0:T(8,128)(2,1)S(1)}, bf16[384,384]{1,0:T(8,128)(2,1)}, u32[]{:S(2)}) copy-start(bf16[384,384]{1,0:T(8,128)(2,1)} %get-tuple-element.140) | copy-start | bytes 884740
  248.7 1.9 collective-permute-start.4
  249.2 2.5 collective-permute-start.3
  249.3 2.4 collective-permute-start.2
  252.8 54.5 %all-to-all-start = ((bf16[16,24,1152]{2,1,0:T(8,128)(2,1)}), bf16[16,24,1152]{2,1,0:T(8,128)(2,1)S(1)}, u32[]{:S(2)}, u32[]{:S(2)}) async-start(bf16[16,24,1152]{2,1,0:T(8,128)(2,1)} %bitcast.12), calls=%async_computation.1 | async-start | bytes 1769472 | tf_op jit(solution)/shard_map/all_to_all | solution.py:737
  257.9 49.6 %reduce-scatter.7.cloned.1.call-start = ((), (), s32[]{:S(2)}) async-start(), calls=%async_computation.6 | async-start | bytes 1177600
  280.9 22.7 %copy-start.14 = (bf16[384,384]{1,0:T(8,128)(2,1)S(1)}, bf16[384,384]{1,0:T(8,128)(2,1)}, u32[]{:S(2)}) copy-start(bf16[384,384]{1,0:T(8,128)(2,1)} %get-tuple-element.164) | copy-start | bytes 884740
  280.9 25.5 %copy-start.9 = (bf16[384,384]{1,0:T(8,128)(2,1)S(1)}, bf16[384,384]{1,0:T(8,128)(2,1)}, u32[]{:S(2)}) copy-start(bf16[384,384]{1,0:T(8,128)(2,1)} %get-tuple-element.163) | copy-start | bytes 884740
  303.5 1.9 collective-permute-start.6
  303.6 2.8 collective-permute-start.5
  308.3 14.6 %collective-permute-start.7 = (bf16[24,1792]{1,0:T(8,128)(2,1)S(1)}, bf16[24,1792]{1,0:T(8,128)(2,1)S(1)}, u32[]{:S(2)}, u32[]{:S(2)}) collective-permute-start(bf16[24,1792]{1,0:T(8,128)(2,1)S(1)} %pad_maximum_fusion.5), channel_id=1, source_target_pairs={{0,6},{2,4},{4,2},{6,0},{1,7},{3,5},{5,3},{7,1},{8,14},{10,12},{12... | collective-permute-start | bytes 258056 | tf_op jit(solution)/shard_map/ppermute | solution.py:755
  312.0 10.8 %collective-permute-start.8 = (bf16[24,1792]{1,0:T(8,128)(2,1)S(1)}, bf16[24,1792]{1,0:T(8,128)(2,1)S(1)}, u32[]{:S(2)}, u32[]{:S(2)}) collective-permute-start(bf16[24,1792]{1,0:T(8,128)(2,1)S(1)} %pad_maximum_fusion.5), channel_id=1, source_target_pairs={{0,4},{2,6},{4,0},{6,2},{1,5},{3,7},{5,1},{7,3},{8,12},{10,14},{12... | collective-permute-start | bytes 258056 | tf_op jit(solution)/shard_map/ppermute | solution.py:755
  312.0 10.9 %collective-permute-start.9 = (bf16[24,1792]{1,0:T(8,128)(2,1)S(1)}, bf16[24,1792]{1,0:T(8,128)(2,1)S(1)}, u32[]{:S(2)}, u32[]{:S(2)}) collective-permute-start(bf16[24,1792]{1,0:T(8,128)(2,1)S(1)} %pad_maximum_fusion.5), channel_id=1, source_target_pairs={{0,2},{2,0},{4,6},{6,4},{1,3},{3,1},{5,7},{7,5},{8,10},{10,8},{12,... | collective-permute-start | bytes 258056 | tf_op jit(solution)/shard_map/ppermute | solution.py:755
  322.9 10.8 %copy-start.11 = (bf16[184,640]{1,0:T(8,128)(2,1)S(1)}, bf16[184,640]{1,0:T(8,128)(2,1)}, u32[]{:S(2)}) copy-start(bf16[184,640]{1,0:T(8,128)(2,1)} %reduce-scatter.7.cloned.1.call-done) | copy-start | bytes 706564
  323.0 21.1 %collective-permute-start.10 = (bf16[96,1792]{1,0:T(8,128)(2,1)S(1)}, bf16[96,1792]{1,0:T(8,128)(2,1)S(1)}, u32[]{:S(2)}, u32[]{:S(2)}) collective-permute-start(bf16[96,1792]{1,0:T(8,128)(2,1)S(1)} %pad_maximum_fusion.4), channel_id=1, source_target_pairs={{0,24},{8,16},{16,8},{24,0},{1,25},{9,17},{17,9},{25,1},{2,26},{10... | collective-permute-start | bytes 1032200 | tf_op jit(solution)/shard_map/ppermute | solution.py:755
  325.9 19.4 %collective-permute-start.11 = (bf16[96,1792]{1,0:T(8,128)(2,1)S(1)}, bf16[96,1792]{1,0:T(8,128)(2,1)S(1)}, u32[]{:S(2)}, u32[]{:S(2)}) collective-permute-start(bf16[96,1792]{1,0:T(8,128)(2,1)S(1)} %pad_maximum_fusion.4), channel_id=1, source_target_pairs={{0,16},{8,24},{16,0},{24,8},{1,17},{9,25},{17,1},{25,9},{2,18},{10... | collective-permute-start | bytes 1032200 | tf_op jit(solution)/shard_map/ppermute | solution.py:755
  326.5 19.4 %collective-permute-start.12 = (bf16[96,1792]{1,0:T(8,128)(2,1)S(1)}, bf16[96,1792]{1,0:T(8,128)(2,1)S(1)}, u32[]{:S(2)}, u32[]{:S(2)}) collective-permute-start(bf16[96,1792]{1,0:T(8,128)(2,1)S(1)} %pad_maximum_fusion.4), channel_id=1, source_target_pairs={{0,8},{8,0},{16,24},{24,16},{1,9},{9,1},{17,25},{25,17},{2,10},{10... | collective-permute-start | bytes 1032200 | tf_op jit(solution)/shard_map/ppermute | solution.py:755
  326.6 23.3 %all-to-all-start.1 = ((bf16[16,24,768]{2,1,0:T(8,128)(2,1)}), bf16[16,24,768]{2,1,0:T(8,128)(2,1)S(1)}, u32[]{:S(2)}, u32[]{:S(2)}) async-start(bf16[16,24,768]{2,1,0:T(8,128)(2,1)} %bitcast.14), calls=%async_computation.2 | async-start | bytes 1179648 | tf_op jit(solution)/shard_map/all_to_all | solution.py:737
  344.1 5.8 %copy-start.1 = (f32[48,768]{1,0:T(8,128)S(1)}, f32[48,768]{1,0:T(8,128)}, u32[]{:S(2)}) copy-start(f32[48,768]{1,0:T(8,128)} %input_back.3.tail) | copy-start | bytes 442372
  346.1 30.4 %copy-start.3 = (bf16[384,1792]{1,0:T(8,128)(2,1)}, bf16[384,1792]{1,0:T(8,128)(2,1)S(1)}, u32[]{:S(2)}) copy-start(bf16[384,1792]{1,0:T(8,128)(2,1)S(1)} %pad_maximum_fusion.1.refs_0_) | copy-start | bytes 4128772
  349.9 26.7 %collective-permute-start.13 = (bf16[384,1792]{1,0:T(8,128)(2,1)S(1)}, bf16[384,1792]{1,0:T(8,128)(2,1)S(1)}, u32[]{:S(2)}, u32[]{:S(2)}) collective-permute-start(bf16[384,1792]{1,0:T(8,128)(2,1)S(1)} %pad_maximum_fusion.1.refs_0_), channel_id=1, source_target_pairs={{0,1},{1,0},{2,3},{3,2},{4,5},{5,4},{6,7},{7,6},{8,9},{9,8},{10,11... | collective-permute-start | bytes 4128776 | tf_op jit(solution)/shard_map/ppermute | solution.py:740
  350.0 0.6 copy-start.2
  350.7 6.7 %collective-permute-start.14 = (bf16[72,768]{1,0:T(8,128)(2,1)S(1)}, bf16[72,768]{1,0:T(8,128)(2,1)S(1)}, u32[]{:S(2)}, u32[]{:S(2)}) collective-permute-start(bf16[72,768]{1,0:T(8,128)(2,1)S(1)} %get-tuple-element.185.own), channel_id=1, source_target_pairs={{0,2},{2,0},{4,6},{6,4},{1,3},{3,1},{5,7},{7,5},{8,10},{10,8},{12,... | collective-permute-start | bytes 331784 | tf_op jit(solution)/shard_map/ppermute | solution.py:889
  350.7 11.5 %collective-permute-start.15 = (bf16[72,768]{1,0:T(8,128)(2,1)S(1)}, bf16[72,768]{1,0:T(8,128)(2,1)S(1)}, u32[]{:S(2)}, u32[]{:S(2)}) collective-permute-start(bf16[72,768]{1,0:T(8,128)(2,1)S(1)} %get-tuple-element.185.own), channel_id=1, source_target_pairs={{0,4},{2,6},{4,0},{6,2},{1,5},{3,7},{5,1},{7,3},{8,12},{10,14},{12... | collective-permute-start | bytes 331784 | tf_op jit(solution)/shard_map/ppermute | solution.py:889
  352.1 10.1 %collective-permute-start.16 = (bf16[72,768]{1,0:T(8,128)(2,1)S(1)}, bf16[72,768]{1,0:T(8,128)(2,1)S(1)}, u32[]{:S(2)}, u32[]{:S(2)}) collective-permute-start(bf16[72,768]{1,0:T(8,128)(2,1)S(1)} %get-tuple-element.185.own), channel_id=1, source_target_pairs={{0,6},{2,4},{4,2},{6,0},{1,7},{3,5},{5,3},{7,1},{8,14},{10,12},{12... | collective-permute-start | bytes 331784 | tf_op jit(solution)/shard_map/ppermute | solution.py:889
  362.3 8.4 %collective-permute-start.17 = (bf16[144,768]{1,0:T(8,128)(2,1)S(1)}, bf16[144,768]{1,0:T(8,128)(2,1)S(1)}, u32[]{:S(2)}, u32[]{:S(2)}) collective-permute-start(bf16[144,768]{1,0:T(8,128)(2,1)S(1)} %stage.2.own), channel_id=1, source_target_pairs={{0,8},{8,0},{16,24},{24,16},{1,9},{9,1},{17,25},{25,17},{2,10},{10... | collective-permute-start | bytes 663560 | tf_op jit(solution)/shard_map/ppermute | solution.py:889
  363.0 7.9 %collective-permute-start.18 = (bf16[144,768]{1,0:T(8,128)(2,1)S(1)}, bf16[144,768]{1,0:T(8,128)(2,1)S(1)}, u32[]{:S(2)}, u32[]{:S(2)}) collective-permute-start(bf16[144,768]{1,0:T(8,128)(2,1)S(1)} %stage.2.own), channel_id=1, source_target_pairs={{0,16},{8,24},{16,0},{24,8},{1,17},{9,25},{17,1},{25,9},{2,18},{10... | collective-permute-start | bytes 663560 | tf_op jit(solution)/shard_map/ppermute | solution.py:889
  364.1 9.8 %collective-permute-start.19 = (bf16[144,768]{1,0:T(8,128)(2,1)S(1)}, bf16[144,768]{1,0:T(8,128)(2,1)S(1)}, u32[]{:S(2)}, u32[]{:S(2)}) collective-permute-start(bf16[144,768]{1,0:T(8,128)(2,1)S(1)} %stage.2.own), channel_id=1, source_target_pairs={{0,24},{8,16},{16,8},{24,0},{1,25},{9,17},{17,9},{25,1},{2,26},{10... | collective-permute-start | bytes 663560 | tf_op jit(solution)/shard_map/ppermute | solution.py:889
  374.2 2.4 copy-start
  374.2 2.3 collective-permute-start.20
  374.3 2.2 collective-permute-start.21
  376.5 0.6 copy-start.12
  376.5 0.9 copy-start.6
  376.5 1.3 copy-start.5
Sparse Core Ops, SparseCore 0:
  11.5 72.9 all-gather.1
  191.0 48.1 reduce-scatter.4
  261.0 35.5 reduce-scatter.6

commit v4 on v3

--- a/solution.py
+++ b/solution.py
@@ -777,7 +777,7 @@
     grads = None
     keeps, sents = [], []
     groups = heads // per_call
-    calls = [(0, 0, 1), (0, 1, slots - 1)] + [(g, 0, slots) for g in range(1, groups)]
+    calls = [(g, 0, slots) for g in range(groups)]
     carry = None
     for index, (first, from_slot, slot_count) in enumerate(calls):
         chained, carried, finished = grads is not None, carry is not None, from_slot + slot_count == slots

time: 402 us -> 393 us (0.978); the launches traced: 404 us -> 389 us
  Pallas kernels: 316 us -> 298 us
    pallas_call x1, Pallas kernels: 89.5 us -> 77 us  [body(): pl.pallas_call(middle_kernel, grid=(blocks,), in_specs=[by_block(8), by_b...]
    pallas_call x6 -> x5, Pallas kernels: 116 us -> 111 us  [body(): pl.pallas_call(functools.partial(attention_back_kernel, chunk=half, chain...]
  transfers between devices with their start and end apart: 27 -> 27, of which waited for: 12 -> 11; matrix products, arithmetic and copies ran while one was open for 1% -> 1% of each run, Pallas kernels for 51% -> 52%
where the time goes in v4:
time: 393 us; the launch traced here: 389 us
  Pallas kernels  298 us (76%)
  waiting for transfers between devices  32.9 us (8%)
  starting transfers between devices  30.4 us (8%)
  between operations  14.4 us (4%)
  other arithmetic  9.47 us (2%)
    pallas_call x5, Pallas kernels, body(): pl.pallas_call(functools.partial(attention_back_kernel, chunk=half, chain...  111 us
    pallas_call x1, Pallas kernels, body(): pl.pallas_call(middle_kernel, grid=(blocks,), in_specs=[by_block(8), by_b...  77 us
    pallas_call x1, Pallas kernels, body(): pl.pallas_call(attention_kernel, grid=(slots, heads // per), in_specs=[he...  53.9 us
    pallas_call x2, Pallas kernels, input_back(): pl.pallas_call(functools.partial(input_back_kernel, last=last), grid=(blo...  20.6 us
    pallas_call x1, Pallas kernels, body(): pl.pallas_call(functools.partial(update_kernel, groups=groups, early_grou...  19.4 us
    ppermute x6, waiting for transfers between devices, body(): lax.ppermute(packed, axis, [(i, i ^ d) for i in range(4)])  16.8 us
    pallas_call x1, Pallas kernels, body(): pl.pallas_call(qkv_kernel, grid=(blocks,), in_specs=[id_block] * 4 + [pl....  15.9 us
    all_to_all x2, starting transfers between devices, swap(): return lax.all_to_all(values, axes, 0, 0, tiled=True)  11.7 us
  transfers between devices with their start and end apart: 27, of which 11 were waited for; matrix products, arithmetic and copies ran while one was open for 1% of the time, Pallas kernels for 52%

profile of v4, /device:TPU:0, one launch (start us, length us, event | category | flops | bytes accessed | tf_op | source)
XLA Modules:
  0.0 389.4 jit_solution(18298146568319103436)
XLA Ops:
  7.2 1.7 convert_element_type.73
  9.0 15.9 %embed_and_qkv.1 = (f32[8,2048]{1,0:T(8,128)}, f32[640,2048]{1,0:T(8,128)}, bf16[656,2048]{1,0:T(8,128)(2,1)}, bf16[20,48,2048]{2,1,0:T(8,128)(2,1)}, bf16[20,48...) custom-call(s32[1,2048]{1,0:T(1,128)} %bitcast.28, s32[1,2048]{1,0:T(1,128)} %bitcast.29, ...), custom_call_target="tpu_custom_call" | custom-call | flops 5033164800 | bytes 26214400 | tf_op jit(solution)/shard_map/embed_and_qkv/pallas_call | solution.py:675
  24.9 53.9 %attention.1 = (bf16[20,32,2048]{2,1,0:T(8,128)(2,1)}, bf16[20,2048,1024]{2,1,0:T(8,128)(2,1)}, f32[20,8,2048]{2,1,0:T(8,128)}) custom-call(bf16[20,48,2048]{2,1,0:T(8,128)(2,1)} %get-tuple-element.114.q_ext, bf16[20,48,2048]{2,1,0:T(8,128)(2,1)} %get-tuple-element.115.k_ext, bf16[20,48,2048]{2,1,0:T(8,128)(2,1)} %get-tuple-element.116.v_ext), custom_call_target="tpu_custom_call" | custom-call | flops 42949672960 | bytes 83886080 | tf_op jit(solution)/shard_map/attention/pallas_call | solution.py:698
  78.8 6.1 %all-gather.2.cloned.1.call-done = bf16[2,2560,640]{2,1,0:T(8,128)(2,1)} async-done(((bf16[2,80,640]{2,1,0:T(8,128)(2,1)}), bf16[2,2560,640]{2,1,0:T(8,128)(2,1)}) %all-gather.2.cloned.1.call-update) | async-done | bytes 6553616 | tf_op jit(solution)/shard_map/all_gather | solution.py:659
  84.9 77.0 %feedforward_and_head.1 = (f32[640,2048]{1,0:T(8,128)}, bf16[20,48,2048]{2,1,0:T(8,128)(2,1)}, bf16[2560,640]{1,0:T(8,128)(2,1)}, bf16[2560,640]{1,0:T(8,128)(2,...) custom-call(f32[8,2048]{1,0:T(8,128)} %get-tuple-element.112.meta, ...), custom_call_target="tpu_custom_call" | custom-call | flops 45298483200 | bytes 44564480 | tf_op jit(solution)/shard_map/feedforward_and_head/pallas_call | solution.py:712
  161.9 0.3 collective-permute-start
  162.5 22.2 %attention_back.5 = (bf16[20,32,2048]{2,1,0:T(8,128)(2,1)}, bf16[20,32,2048]{2,1,0:T(8,128)(2,1)}, bf16[20,32,2048]{2,1,0:T(8,128)(2,1)}, bf16[384,384]{1,0:T(8,128)(2,1)}, bf16[384,384]{1,0:T(8,128)(2,1)}) custom-call(bf16[20,48,2048]{2,1,0:T(8,128)(2,1)} %get-tuple-element.114.q_ext, bf16[20,48,2048]{2,1,0:T(8,128)(2,1)} %get-tuple-element.115.k_ext, ...), custom_call_target="tpu_custom_call" | custom-call | flops 21474836480 | bytes 15728640 | tf_op jit(solution)/shard_map/attention_back/pallas_call | solution.py:792
  184.7 0.8 add_convert_fusion
  185.9 2.2 pad_maximum_fusion
  188.2 0.9 copy-done.13
  189.3 22.1 %attention_back.6 = (bf16[20,32,2048]{2,1,0:T(8,128)(2,1)}, bf16[20,32,2048]{2,1,0:T(8,128)(2,1)}, bf16[20,32,2048]{2,1,0:T(8,128)(2,1)}, bf16[384,384]{1,0:T(8,128)(2,1)}, bf16[384,384]{1,0:T(8,128)(2,1)}) custom-call(bf16[20,48,2048]{2,1,0:T(8,128)(2,1)} %get-tuple-element.114.q_ext, ...), custom_call_target="tpu_custom_call", output_to_operand_aliasing={{0}: (11, {}), {1}: (12, {}), {2}: (13, {})} | custom-call | flops 21474836480 | bytes 15728640 | tf_op jit(solution)/shard_map/attention_back/pallas_call | solution.py:792
  211.8 22.3 %attention_back.7 = (bf16[20,32,2048]{2,1,0:T(8,128)(2,1)}, bf16[20,32,2048]{2,1,0:T(8,128)(2,1)}, bf16[20,32,2048]{2,1,0:T(8,128)(2,1)}, bf16[384,384]{1,0:T(8,128)(2,1)}, bf16[384,384]{1,0:T(8,128)(2,1)}) custom-call(bf16[20,48,2048]{2,1,0:T(8,128)(2,1)} %get-tuple-element.114.q_ext, ...), custom_call_target="tpu_custom_call", output_to_operand_aliasing={{0}: (11, {}), {1}: (12, {}), {2}: (13, {})} | custom-call | flops 21474836480 | bytes 15728640 | tf_op jit(solution)/shard_map/attention_back/pallas_call | solution.py:792
  234.6 1.4 collective-permute-done.4
  235.9 1.0 add_convert_fusion.4
  237.0 1.0 pad_maximum_fusion.2
  238.0 4.6 %all-to-all-start = ((bf16[16,24,1152]{2,1,0:T(8,128)(2,1)}), bf16[16,24,1152]{2,1,0:T(8,128)(2,1)S(1)}, u32[]{:S(2)}, u32[]{:S(2)}) async-start(bf16[16,24,1152]{2,1,0:T(8,128)(2,1)} %bitcast.12), calls=%async_computation.1 | async-start | bytes 1769472 | tf_op jit(solution)/shard_map/all_to_all | solution.py:737
  242.6 22.2 %attention_back.8 = (bf16[20,32,2048]{2,1,0:T(8,128)(2,1)}, bf16[20,32,2048]{2,1,0:T(8,128)(2,1)}, bf16[20,32,2048]{2,1,0:T(8,128)(2,1)}, bf16[384,384]{1,0:T(8,128)(2,1)}, bf16[384,384]{1,0:T(8,128)(2,1)}) custom-call(bf16[20,48,2048]{2,1,0:T(8,128)(2,1)} %get-tuple-element.114.q_ext, ...), custom_call_target="tpu_custom_call", output_to_operand_aliasing={{0}: (11, {}), {1}: (12, {}), {2}: (13, {})} | custom-call | flops 21474836480 | bytes 15728640 | tf_op jit(solution)/shard_map/attention_back/pallas_call | solution.py:792
  264.8 22.2 %attention_back.9 = (bf16[20,32,2048]{2,1,0:T(8,128)(2,1)}, bf16[20,32,2048]{2,1,0:T(8,128)(2,1)}, bf16[20,32,2048]{2,1,0:T(8,128)(2,1)}, bf16[384,384]{1,0:T(8,128)(2,1)}, bf16[384,384]{1,0:T(8,128)(2,1)}) custom-call(bf16[20,48,2048]{2,1,0:T(8,128)(2,1)} %get-tuple-element.114.q_ext, ...), custom_call_target="tpu_custom_call", output_to_operand_aliasing={{0}: (11, {}), {1}: (12, {}), {2}: (13, {})} | custom-call | flops 21474836480 | bytes 15728640 | tf_op jit(solution)/shard_map/attention_back/pallas_call | solution.py:792
  287.1 0.5 collective-permute-start.5
  287.6 1.3 collective-permute-done.6
  288.9 1.0 add_convert_fusion.2
  290.0 0.9 pad_maximum_fusion.3
  291.1 0.8 slice.6
  291.8 2.1 collective-permute-start.9
  293.9 2.4 collective-permute-start.8
  296.4 10.2 %input_back.2 = (f32[640,128]{1,0:T(8,128)}, f32[48,640]{1,0:T(8,128)}) custom-call(f32[8,2048]{1,0:T(8,128)} %get-tuple-element.112.meta, f32[640,2048]{1,0:T(8,128)} %get-tuple-element.113.x0, bf16[640,2048]{1,0:T(8,128)(2,1)} %bitcast.18, bf16[640,2048]{1,0:T(8,128)(2,1)} %bitcast.20, bf16[640,2048]{1,0:T(8,128)(2,1)} %bitcast.22, ...), custom_call_target="tpu_custom_call" | custom-call | flops 838860800 | bytes 5242880 | tf_op jit(solution)/shard_map/input_back/pallas_call | solution.py:849
  306.7 2.0 collective-permute-start.12
  308.7 1.5 collective-permute-start.11
  310.3 7.1 %all-to-all-start.1 = ((bf16[16,24,768]{2,1,0:T(8,128)(2,1)}), bf16[16,24,768]{2,1,0:T(8,128)(2,1)S(1)}, u32[]{:S(2)}, u32[]{:S(2)}) async-start(bf16[16,24,768]{2,1,0:T(8,128)(2,1)} %bitcast.14), calls=%async_computation.2 | async-start | bytes 1179648 | tf_op jit(solution)/shard_map/all_to_all | solution.py:737
  317.5 10.3 %input_back.3.tail = f32[48,768]{1,0:T(8,128)} custom-call(f32[8,2048]{1,0:T(8,128)} %get-tuple-element.112.meta, f32[640,2048]{1,0:T(8,128)} %get-tuple-element.113.x0, bf16[640,2048]{1,0:T(8,128)(2,1)} %bitcast.19, bf16[640,2048]{1,0:T(8,128)(2,1)} %bitcast.21, bf16[640,2048]{1,0:T(8,128)(2,1)} %bitcast.23, f32[640,2048]{1,0:T(8,128)} %get-tuple-element.161.dx1, ...), custom_call_target="tpu_custom_call" | custom-call | flops 838860800 | bytes 5242880 | tf_op jit(solution)/shard_map/input_back/pallas_call | solution.py:849
  327.8 1.4 collective-permute-done.11
  329.2 1.0 collective-permute-done.10
  330.4 3.2 all-to-all-done.1
  333.8 0.6 copy-done.2
  334.5 1.3 collective-permute-start.16
  335.7 3.1 collective-permute-start.14
  338.8 3.4 collective-permute-done.16.three
  342.2 4.2 %collective-permute-done.15.two = bf16[72,768]{1,0:T(8,128)(2,1)S(1)} collective-permute-done((bf16[72,768]{1,0:T(8,128)(2,1)S(1)}, bf16[72,768]{1,0:T(8,128)(2,1)S(1)}, u32[]{:S(2)}, u32[]{:S(2)}) %collective-permute-start.15) | collective-permute-done | bytes 110624 | tf_op jit(solution)/shard_map/ppermute | solution.py:889
  346.6 0.8 collective-permute-start.19
  347.4 1.1 collective-permute-start.18
  348.4 1.7 collective-permute-start.17
  350.1 5.7 %collective-permute-done.19.three = bf16[144,768]{1,0:T(8,128)(2,1)S(1)} collective-permute-done((bf16[144,768]{1,0:T(8,128)(2,1)S(1)}, bf16[144,768]{1,0:T(8,128)(2,1)S(1)}, u32[]{:S(2)}, u32[]{:S(2)}) %collective-permute-start.19) | collective-permute-done | bytes 221216 | tf_op jit(solution)/shard_map/ppermute | solution.py:889
  355.8 3.4 collective-permute-done.18.two
  359.6 0.5 collective-permute-start.21
  360.1 1.7 collective-permute-done.21.refs_5_
  361.9 0.6 copy-done.12
  362.8 0.4 copy-done.5
  363.2 19.4 %clip_and_adamw.1 = (f32[33,640]{1,0:T(8,128)}, f32[33,640]{1,0:T(8,128)}, f32[33,640]{1,0:T(8,128)}, bf16[33,640]{1,0:T(8,128)(2,1)}, f32[640,1920]{1,0:T(8,128...) custom-call(bf16[384,1792]{1,0:T(8,128)(2,1)} %copy-done.3, ...), custom_call_target="tpu_custom_call" | custom-call | flops 98304000 | bytes 49152000 | tf_op jit(solution)/shard_map/clip_and_adamw/pallas_call | solution.py:922
  (72 shorter events, 3.5 us)
Async XLA Ops:
  7.2 77.7 %all-gather.2.cloned.1.call-start = ((), (), s32[]{:S(2)}) async-start(), calls=%async_computation.4 | async-start | bytes 6758400 | tf_op jit(solution)/shard_map/all_gather | solution.py:659
  9.0 229.0 %reduce-scatter.5.cloned.1.call-start = ((), (), s32[]{:S(2)}) async-start(), calls=%async_computation.5 | async-start | bytes 4710400 | tf_op jit(solution)/shard_map/reduce_scatter | solution.py:823
  161.9 22.8 %collective-permute-start = (bf16[2560,640]{1,0:T(8,128)(2,1)}, bf16[2560,640]{1,0:T(8,128)(2,1)S(1)}, u32[]{:S(2)}, u32[]{:S(2)}) collective-permute-start(bf16[2560,640]{1,0:T(8,128)(2,1)} %get-tuple-element.124), channel_id=1, source_target_pairs={{0,1},{1,0},{2,3},{3,2},{4,5},{5,4},{6,7},{7,6},{8,9},{9,8},{10,11... | collective-permute-start | bytes 9830408 | tf_op jit(solution)/shard_map/ppermute | solution.py:740
  162.3 22.4 %collective-permute-start.1 = (bf16[384,640]{1,0:T(8,128)(2,1)}, bf16[384,640]{1,0:T(8,128)(2,1)S(1)}, u32[]{:S(2)}, u32[]{:S(2)}) collective-permute-start(bf16[384,640]{1,0:T(8,128)(2,1)} %get-tuple-element.125), channel_id=1, source_target_pairs={{0,1},{1,0},{2,3},{3,2},{4,5},{5,4},{6,7},{7,6},{8,9},{9,8},{10,11... | collective-permute-start | bytes 1474568 | tf_op jit(solution)/shard_map/ppermute | solution.py:740
  162.5 22.2 %copy-start.4 = (bf16[2560,640]{1,0:T(8,128)(2,1)S(1)}, bf16[2560,640]{1,0:T(8,128)(2,1)}, u32[]{:S(2)}) copy-start(bf16[2560,640]{1,0:T(8,128)(2,1)} %get-tuple-element.120) | copy-start | bytes 9830404
  184.7 1.0 copy-start.7
  188.1 1.0 copy-start.13
  188.1 102.9 %reduce-scatter.7.cloned.1.call-start = ((), (), s32[]{:S(2)}) async-start(), calls=%async_computation.6 | async-start | bytes 1177600
  189.1 45.3 %collective-permute-start.2 = (bf16[384,384]{1,0:T(8,128)(2,1)S(1)}, bf16[384,384]{1,0:T(8,128)(2,1)S(1)}, u32[]{:S(2)}, u32[]{:S(2)}) collective-permute-start(bf16[384,384]{1,0:T(8,128)(2,1)S(1)} %copy-done.13), channel_id=1, source_target_pairs={{0,1},{1,0},{2,3},{3,2},{4,5},{5,4},{6,7},{7,6},{8,9},{9,8},{10,11... | collective-permute-start | bytes 884744 | tf_op jit(solution)/shard_map/ppermute | solution.py:740
  211.5 23.0 %collective-permute-start.3 = (bf16[384,384]{1,0:T(8,128)(2,1)}, bf16[384,384]{1,0:T(8,128)(2,1)S(1)}, u32[]{:S(2)}, u32[]{:S(2)}) collective-permute-start(bf16[384,384]{1,0:T(8,128)(2,1)} %get-tuple-element.138), channel_id=1, source_target_pairs={{0,1},{1,0},{2,3},{3,2},{4,5},{5,4},{6,7},{7,6},{8,9},{9,8},{10,11... | collective-permute-start | bytes 884744 | tf_op jit(solution)/shard_map/ppermute | solution.py:740
  211.8 22.6 %copy-start.8 = (bf16[384,384]{1,0:T(8,128)(2,1)S(1)}, bf16[384,384]{1,0:T(8,128)(2,1)}, u32[]{:S(2)}) copy-start(bf16[384,384]{1,0:T(8,128)(2,1)} %get-tuple-element.132) | copy-start | bytes 884740
  211.8 22.7 %copy-start.10 = (bf16[384,384]{1,0:T(8,128)(2,1)S(1)}, bf16[384,384]{1,0:T(8,128)(2,1)}, u32[]{:S(2)}) copy-start(bf16[384,384]{1,0:T(8,128)(2,1)} %get-tuple-element.137) | copy-start | bytes 884740
  234.1 1.9 collective-permute-start.4
  238.0 52.9 %all-to-all-start = ((bf16[16,24,1152]{2,1,0:T(8,128)(2,1)}), bf16[16,24,1152]{2,1,0:T(8,128)(2,1)S(1)}, u32[]{:S(2)}, u32[]{:S(2)}) async-start(bf16[16,24,1152]{2,1,0:T(8,128)(2,1)} %bitcast.12), calls=%async_computation.1 | async-start | bytes 1769472 | tf_op jit(solution)/shard_map/all_to_all | solution.py:737
  264.8 22.3 %copy-start.14 = (bf16[384,384]{1,0:T(8,128)(2,1)S(1)}, bf16[384,384]{1,0:T(8,128)(2,1)}, u32[]{:S(2)}) copy-start(bf16[384,384]{1,0:T(8,128)(2,1)} %get-tuple-element.156) | copy-start | bytes 884740
  264.8 25.2 %copy-start.9 = (bf16[384,384]{1,0:T(8,128)(2,1)S(1)}, bf16[384,384]{1,0:T(8,128)(2,1)}, u32[]{:S(2)}) copy-start(bf16[384,384]{1,0:T(8,128)(2,1)} %get-tuple-element.155) | copy-start | bytes 884740
  287.0 1.9 collective-permute-start.6
  287.1 2.8 collective-permute-start.5
  291.8 14.8 %collective-permute-start.9 = (bf16[24,1792]{1,0:T(8,128)(2,1)S(1)}, bf16[24,1792]{1,0:T(8,128)(2,1)S(1)}, u32[]{:S(2)}, u32[]{:S(2)}) collective-permute-start(bf16[24,1792]{1,0:T(8,128)(2,1)S(1)} %pad_maximum_fusion.5), channel_id=1, source_target_pairs={{0,2},{2,0},{4,6},{6,4},{1,3},{3,1},{5,7},{7,5},{8,10},{10,8},{12,... | collective-permute-start | bytes 258056 | tf_op jit(solution)/shard_map/ppermute | solution.py:755
  293.9 12.7 %collective-permute-start.8 = (bf16[24,1792]{1,0:T(8,128)(2,1)S(1)}, bf16[24,1792]{1,0:T(8,128)(2,1)S(1)}, u32[]{:S(2)}, u32[]{:S(2)}) collective-permute-start(bf16[24,1792]{1,0:T(8,128)(2,1)S(1)} %pad_maximum_fusion.5), channel_id=1, source_target_pairs={{0,4},{2,6},{4,0},{6,2},{1,5},{3,7},{5,1},{7,3},{8,12},{10,14},{12... | collective-permute-start | bytes 258056 | tf_op jit(solution)/shard_map/ppermute | solution.py:755
  296.3 10.3 %collective-permute-start.7 = (bf16[24,1792]{1,0:T(8,128)(2,1)S(1)}, bf16[24,1792]{1,0:T(8,128)(2,1)S(1)}, u32[]{:S(2)}, u32[]{:S(2)}) collective-permute-start(bf16[24,1792]{1,0:T(8,128)(2,1)S(1)} %pad_maximum_fusion.5), channel_id=1, source_target_pairs={{0,6},{2,4},{4,2},{6,0},{1,7},{3,5},{5,3},{7,1},{8,14},{10,12},{12... | collective-permute-start | bytes 258056 | tf_op jit(solution)/shard_map/ppermute | solution.py:755
  306.6 10.9 %copy-start.11 = (bf16[184,640]{1,0:T(8,128)(2,1)S(1)}, bf16[184,640]{1,0:T(8,128)(2,1)}, u32[]{:S(2)}) copy-start(bf16[184,640]{1,0:T(8,128)(2,1)} %reduce-scatter.7.cloned.1.call-done) | copy-start | bytes 706564
  306.7 21.1 %collective-permute-start.12 = (bf16[96,1792]{1,0:T(8,128)(2,1)S(1)}, bf16[96,1792]{1,0:T(8,128)(2,1)S(1)}, u32[]{:S(2)}, u32[]{:S(2)}) collective-permute-start(bf16[96,1792]{1,0:T(8,128)(2,1)S(1)} %pad_maximum_fusion.4), channel_id=1, source_target_pairs={{0,8},{8,0},{16,24},{24,16},{1,9},{9,1},{17,25},{25,17},{2,10},{10... | collective-permute-start | bytes 1032200 | tf_op jit(solution)/shard_map/ppermute | solution.py:755
  308.7 20.5 %collective-permute-start.11 = (bf16[96,1792]{1,0:T(8,128)(2,1)S(1)}, bf16[96,1792]{1,0:T(8,128)(2,1)S(1)}, u32[]{:S(2)}, u32[]{:S(2)}) collective-permute-start(bf16[96,1792]{1,0:T(8,128)(2,1)S(1)} %pad_maximum_fusion.4), channel_id=1, source_target_pairs={{0,16},{8,24},{16,0},{24,8},{1,17},{9,25},{17,1},{25,9},{2,18},{10... | collective-permute-start | bytes 1032200 | tf_op jit(solution)/shard_map/ppermute | solution.py:755
  310.2 20.0 %collective-permute-start.10 = (bf16[96,1792]{1,0:T(8,128)(2,1)S(1)}, bf16[96,1792]{1,0:T(8,128)(2,1)S(1)}, u32[]{:S(2)}, u32[]{:S(2)}) collective-permute-start(bf16[96,1792]{1,0:T(8,128)(2,1)S(1)} %pad_maximum_fusion.4), channel_id=1, source_target_pairs={{0,24},{8,16},{16,8},{24,0},{1,25},{9,17},{17,9},{25,1},{2,26},{10... | collective-permute-start | bytes 1032200 | tf_op jit(solution)/shard_map/ppermute | solution.py:755
  310.3 23.3 %all-to-all-start.1 = ((bf16[16,24,768]{2,1,0:T(8,128)(2,1)}), bf16[16,24,768]{2,1,0:T(8,128)(2,1)S(1)}, u32[]{:S(2)}, u32[]{:S(2)}) async-start(bf16[16,24,768]{2,1,0:T(8,128)(2,1)} %bitcast.14), calls=%async_computation.2 | async-start | bytes 1179648 | tf_op jit(solution)/shard_map/all_to_all | solution.py:737
  327.8 5.8 %copy-start.1 = (f32[48,768]{1,0:T(8,128)S(1)}, f32[48,768]{1,0:T(8,128)}, u32[]{:S(2)}) copy-start(f32[48,768]{1,0:T(8,128)} %input_back.3.tail) | copy-start | bytes 442372
  330.4 31.5 %copy-start.3 = (bf16[384,1792]{1,0:T(8,128)(2,1)}, bf16[384,1792]{1,0:T(8,128)(2,1)S(1)}, u32[]{:S(2)}) copy-start(bf16[384,1792]{1,0:T(8,128)(2,1)S(1)} %pad_maximum_fusion.1.refs_0_) | copy-start | bytes 4128772
  333.6 28.3 %collective-permute-start.13 = (bf16[384,1792]{1,0:T(8,128)(2,1)S(1)}, bf16[384,1792]{1,0:T(8,128)(2,1)S(1)}, u32[]{:S(2)}, u32[]{:S(2)}) collective-permute-start(bf16[384,1792]{1,0:T(8,128)(2,1)S(1)} %pad_maximum_fusion.1.refs_0_), channel_id=1, source_target_pairs={{0,1},{1,0},{2,3},{3,2},{4,5},{5,4},{6,7},{7,6},{8,9},{9,8},{10,11... | collective-permute-start | bytes 4128776 | tf_op jit(solution)/shard_map/ppermute | solution.py:740
  333.8 0.6 copy-start.2
  334.5 7.8 %collective-permute-start.16 = (bf16[72,768]{1,0:T(8,128)(2,1)S(1)}, bf16[72,768]{1,0:T(8,128)(2,1)S(1)}, u32[]{:S(2)}, u32[]{:S(2)}) collective-permute-start(bf16[72,768]{1,0:T(8,128)(2,1)S(1)} %get-tuple-element.177.own), channel_id=1, source_target_pairs={{0,6},{2,4},{4,2},{6,0},{1,7},{3,5},{5,3},{7,1},{8,14},{10,12},{12... | collective-permute-start | bytes 331784 | tf_op jit(solution)/shard_map/ppermute | solution.py:889
  335.7 10.7 %collective-permute-start.15 = (bf16[72,768]{1,0:T(8,128)(2,1)S(1)}, bf16[72,768]{1,0:T(8,128)(2,1)S(1)}, u32[]{:S(2)}, u32[]{:S(2)}) collective-permute-start(bf16[72,768]{1,0:T(8,128)(2,1)S(1)} %get-tuple-element.177.own), channel_id=1, source_target_pairs={{0,4},{2,6},{4,0},{6,2},{1,5},{3,7},{5,1},{7,3},{8,12},{10,14},{12... | collective-permute-start | bytes 331784 | tf_op jit(solution)/shard_map/ppermute | solution.py:889
  335.7 10.7 %collective-permute-start.14 = (bf16[72,768]{1,0:T(8,128)(2,1)S(1)}, bf16[72,768]{1,0:T(8,128)(2,1)S(1)}, u32[]{:S(2)}, u32[]{:S(2)}) collective-permute-start(bf16[72,768]{1,0:T(8,128)(2,1)S(1)} %get-tuple-element.177.own), channel_id=1, source_target_pairs={{0,2},{2,0},{4,6},{6,4},{1,3},{3,1},{5,7},{7,5},{8,10},{10,8},{12,... | collective-permute-start | bytes 331784 | tf_op jit(solution)/shard_map/ppermute | solution.py:889
  346.6 9.3 %collective-permute-start.19 = (bf16[144,768]{1,0:T(8,128)(2,1)S(1)}, bf16[144,768]{1,0:T(8,128)(2,1)S(1)}, u32[]{:S(2)}, u32[]{:S(2)}) collective-permute-start(bf16[144,768]{1,0:T(8,128)(2,1)S(1)} %stage.2.own), channel_id=1, source_target_pairs={{0,24},{8,16},{16,8},{24,0},{1,25},{9,17},{17,9},{25,1},{2,26},{10... | collective-permute-start | bytes 663560 | tf_op jit(solution)/shard_map/ppermute | solution.py:889
  347.4 11.9 %collective-permute-start.18 = (bf16[144,768]{1,0:T(8,128)(2,1)S(1)}, bf16[144,768]{1,0:T(8,128)(2,1)S(1)}, u32[]{:S(2)}, u32[]{:S(2)}) collective-permute-start(bf16[144,768]{1,0:T(8,128)(2,1)S(1)} %stage.2.own), channel_id=1, source_target_pairs={{0,16},{8,24},{16,0},{24,8},{1,17},{9,25},{17,1},{25,9},{2,18},{10... | collective-permute-start | bytes 663560 | tf_op jit(solution)/shard_map/ppermute | solution.py:889
  348.4 10.8 %collective-permute-start.17 = (bf16[144,768]{1,0:T(8,128)(2,1)S(1)}, bf16[144,768]{1,0:T(8,128)(2,1)S(1)}, u32[]{:S(2)}, u32[]{:S(2)}) collective-permute-start(bf16[144,768]{1,0:T(8,128)(2,1)S(1)} %stage.2.own), channel_id=1, source_target_pairs={{0,8},{8,0},{16,24},{24,16},{1,9},{9,1},{17,25},{25,17},{2,10},{10... | collective-permute-start | bytes 663560 | tf_op jit(solution)/shard_map/ppermute | solution.py:889
  359.5 2.4 copy-start
  359.6 2.3 collective-permute-start.20
  359.6 2.2 collective-permute-start.21
  361.9 0.6 copy-start.12
  361.9 0.9 copy-start.6
  361.9 1.3 copy-start.5
Sparse Core Ops, SparseCore 0:
  11.5 73.3 all-gather.1
  188.2 47.6 reduce-scatter.4
  238.3 38.9 reduce-scatter.6
